TPU v7x, 512 devices: a whole 4x4x16 slice. The times are simulated.
512 devices in a mesh: head: 8 (over x_hi, y), ctx: 64 (over z, x_lo, core).
Axes of the slice: x: 4 (x_hi: 2, x_lo: 2; x = x_hi * 2 + x_lo), y: 4, z: 16, core: 2. Of those that a mesh axis runs over, the one named last changes fastest.
Arguments:
- queries: bfloat16 [32768, 64, 128], P(('ctx', 'head')), may hold values from -6 to 6
- keys: bfloat16 [32768, 8, 128], P(('ctx', 'head')), may hold values from -6 to 6
- values: bfloat16 [32768, 8, 128], P(('ctx', 'head')), may hold values from -6 to 6
- out_grad: bfloat16 [32768, 64, 128], P(('ctx', 'head')), may hold values from -6 to 6
- doc_lengths: int32 [48], replicated, may hold values from 1 to 1024, 32768 in all
- stored_block_order: int32 [256], replicated, may hold values from 0 to 255, as said below
Outputs:
- attended: bfloat16 [32768, 64, 128], P(('ctx', 'head'))
- query_grad: bfloat16 [32768, 64, 128], P(('ctx', 'head'))
- key_gradient: bfloat16 [32768, 8, 128], P(('ctx', 'head'))
- value_gradient: bfloat16 [32768, 8, 128], P(('ctx', 'head'))
Inputs may be any that keep to these rules, and one draw needn't show every extreme that they name: `doc_lengths`: they sum to 32768 and the largest is exactly 1024. A permutation in which stored_block_order[b] // 4 = b // 4: the stored blocks of each aligned group of 4 are that group's sequence blocks in some order.
All inputs are finite; a program needn't handle non-finite values.
Results may differ from a plain program's by a relative error of at most 0.039.
Values may be sent and summed in bfloat16 or wider, within the bound.
No kernel may reach another device: no remote copies, remote signals or barrier semaphores. Data moves between devices by JAX's collectives and lax.ppermute only.
A program may use at most 64 MiB of HBM per device.

v0:
```python
import jax
import jax.numpy as jnp
from jax import lax
from jax.sharding import PartitionSpec as P

HEAD_SIZE = 128
BLOCK_TOKENS = 128
HOPS = 2


neg_big = -1e30


def passed_along(block, axis, distance):
    devices = range(lax.axis_size(axis))
    route = [(i - distance, i) for i in devices if i - distance in devices]
    return lax.ppermute(block, axis, route)


def segment_ids(positions, doc_lengths):
    ends = jnp.cumsum(doc_lengths)
    return jnp.sum((positions[..., None] >= ends).astype(jnp.int32), axis=-1)


def allowed_pairs(query_pos, query_doc, key_pos, key_doc, key_live):
    same_doc = query_doc[:, None] == key_doc[None, :]
    return same_doc & (key_pos[None, :] <= query_pos[:, None]) & key_live[None, :]


def raw_scores(query_four, slot_keys, score_scale):
    return (
        jnp.einsum("qhgd,khd->hgqk", query_four, slot_keys, preferred_element_type=jnp.float32)
        * score_scale
    )


def online_update(running, query_four, slot_keys, slot_values, allowed, score_scale):
    running_max, running_sum, out_acc = running
    scores = raw_scores(query_four, slot_keys, score_scale)
    new_max = jnp.maximum(running_max, jnp.max(jnp.where(allowed, scores, neg_big), axis=-1))
    weights = jnp.where(allowed, jnp.exp(scores - new_max[..., None]), 0.0)
    rescale = jnp.exp(running_max - new_max)
    new_sum = running_sum * rescale + jnp.sum(weights, axis=-1)
    added = jnp.einsum(
        "hgqk,khd->qhgd",
        weights.astype(jnp.bfloat16),
        slot_values,
        preferred_element_type=jnp.float32,
    )
    new_out = out_acc * rescale.transpose(2, 0, 1)[..., None] + added
    return (new_max, new_sum, new_out)


def grad_terms(
    query_four, grad_four, log_total, row_delta, slot_keys, slot_values, allowed, score_scale
):
    scores = raw_scores(query_four, slot_keys, score_scale)
    weights = jnp.where(allowed, jnp.exp(scores - log_total[..., None]), 0.0)
    weights_low = weights.astype(jnp.bfloat16)
    grad_weights = jnp.einsum(
        "qhgd,khd->hgqk", grad_four, slot_values, preferred_element_type=jnp.float32
    )
    grad_scores = (weights * (grad_weights - row_delta[..., None])).astype(jnp.bfloat16)
    query_part = (
        jnp.einsum("hgqk,khd->qhgd", grad_scores, slot_keys, preferred_element_type=jnp.float32)
        * score_scale
    )
    key_part = (
        jnp.einsum("hgqk,qhgd->khd", grad_scores, query_four, preferred_element_type=jnp.float32)
        * score_scale
    )
    value_part = jnp.einsum(
        "hgqk,qhgd->khd", weights_low, grad_four, preferred_element_type=jnp.float32
    )
    return (query_part, key_part, value_part)


def body(queries, keys, values, out_grad, doc_lengths, stored_block_order):
    score_scale = HEAD_SIZE ** (-0.5)
    query_loc, key_loc, value_loc, grad_loc = (
        lax.all_to_all(queries, "head", split_axis=1, concat_axis=0, tiled=True),
        lax.all_to_all(keys, "head", split_axis=1, concat_axis=0, tiled=True),
        lax.all_to_all(values, "head", split_axis=1, concat_axis=0, tiled=True),
        lax.all_to_all(out_grad, "head", split_axis=1, concat_axis=0, tiled=True),
    )
    row_count = query_loc.shape[0]
    key_heads = key_loc.shape[1]
    sharing_count = query_loc.shape[1] // key_heads
    query_four = query_loc.reshape(row_count, key_heads, sharing_count, HEAD_SIZE)
    grad_four = grad_loc.reshape(row_count, key_heads, sharing_count, HEAD_SIZE)
    devices = lax.axis_size("ctx")
    ctx_index = lax.axis_index("ctx")
    blocks = stored_block_order.shape[0]
    dev_blocks = blocks // devices
    hop_count = HOPS
    slot_count = hop_count + 1
    window_blocks = slot_count * dev_blocks
    window_rows = window_blocks * BLOCK_TOKENS
    pos_blocks = (
        stored_block_order[:, None] * BLOCK_TOKENS
        + jnp.arange(BLOCK_TOKENS, dtype=jnp.int32)[None, :]
    )
    doc_blocks = segment_ids(pos_blocks, doc_lengths)

    def device_rows(table, source):
        return lax.dynamic_slice_in_dim(table, jnp.maximum(source, 0) * dev_blocks, dev_blocks, 0)

    query_pos = device_rows(pos_blocks, ctx_index).reshape(row_count)
    query_doc = device_rows(doc_blocks, ctx_index).reshape(row_count)
    slot_pos = []
    slot_doc = []
    slot_alive = []
    for slot_index in range(slot_count):
        source = ctx_index - slot_index
        slot_pos.append(device_rows(pos_blocks, source))
        slot_doc.append(device_rows(doc_blocks, source))
        slot_alive.append(jnp.broadcast_to(source >= 0, (dev_blocks, BLOCK_TOKENS)))
    win_pos = jnp.concatenate(slot_pos, axis=0)
    win_doc = jnp.concatenate(slot_doc, axis=0)
    win_live = jnp.concatenate(slot_alive, axis=0)
    key_value = jnp.stack([key_loc, value_loc])
    arrived = [key_value]
    for hop_index in range(hop_count):
        key_value = passed_along(key_value, "ctx", 1)
        arrived.append(key_value)
    window = jnp.concatenate(arrived, axis=1)
    key_blocks = window[0].reshape(window_blocks, BLOCK_TOKENS, key_heads, HEAD_SIZE)
    value_blocks = window[1].reshape(window_blocks, BLOCK_TOKENS, key_heads, HEAD_SIZE)
    full_allowed = allowed_pairs(
        query_pos,
        query_doc,
        win_pos.reshape(window_rows),
        win_doc.reshape(window_rows),
        win_live.reshape(window_rows),
    )
    needed = jnp.any(full_allowed.reshape(row_count, window_blocks, BLOCK_TOKENS), axis=(0, 2))
    per_step = 4
    padded = -(-window_blocks // per_step) * per_step
    slot_rank = jnp.cumsum(needed.astype(jnp.int32)) - 1
    target = jnp.where(needed, slot_rank, padded)
    slot_ids = (
        jnp.zeros((padded,), jnp.int32)
        .at[target]
        .set(jnp.arange(window_blocks, dtype=jnp.int32), mode="drop")
    )
    live_count = jnp.sum(needed.astype(jnp.int32))
    step_count = (live_count + per_step - 1) // per_step

    def slot_group(turn_index):
        chosen = lax.dynamic_slice_in_dim(slot_ids, turn_index * per_step, per_step, 0)
        slot_live = turn_index * per_step + jnp.arange(per_step, dtype=jnp.int32) < live_count
        slot_keys = key_blocks[chosen].reshape(per_step * BLOCK_TOKENS, key_heads, HEAD_SIZE)
        slot_values = value_blocks[chosen].reshape(per_step * BLOCK_TOKENS, key_heads, HEAD_SIZE)
        key_pos = win_pos[chosen].reshape(per_step * BLOCK_TOKENS)
        key_doc = win_doc[chosen].reshape(per_step * BLOCK_TOKENS)
        key_live = (win_live[chosen] & slot_live[:, None]).reshape(per_step * BLOCK_TOKENS)
        allowed = allowed_pairs(query_pos, query_doc, key_pos, key_doc, key_live)
        return (chosen, slot_keys, slot_values, allowed)

    def forward_pass(turn_index, running):
        chosen, slot_keys, slot_values, allowed = slot_group(turn_index)
        return online_update(running, query_four, slot_keys, slot_values, allowed, score_scale)

    stat_shape = (key_heads, sharing_count, row_count)
    start_stats = (
        jnp.full(stat_shape, neg_big, jnp.float32),
        jnp.zeros(stat_shape, jnp.float32),
        jnp.zeros((row_count, key_heads, sharing_count, HEAD_SIZE), jnp.float32),
    )
    run_max, run_sum, out_acc = lax.fori_loop(0, step_count, forward_pass, start_stats)
    log_total = run_max + jnp.log(run_sum)
    attended_loc = (out_acc / run_sum.transpose(2, 0, 1)[..., None]).astype(jnp.bfloat16)
    row_delta = jnp.sum(
        grad_four.astype(jnp.float32) * attended_loc.astype(jnp.float32), axis=-1
    ).transpose(1, 2, 0)

    def back_pass(turn_index, running):
        query_acc, term_acc = running
        chosen, slot_keys, slot_values, allowed = slot_group(turn_index)
        query_part, key_part, value_part = grad_terms(
            query_four,
            grad_four,
            log_total,
            row_delta,
            slot_keys,
            slot_values,
            allowed,
            score_scale,
        )
        both_parts = jnp.stack(
            [
                key_part.reshape(per_step, BLOCK_TOKENS, key_heads, HEAD_SIZE),
                value_part.reshape(per_step, BLOCK_TOKENS, key_heads, HEAD_SIZE),
            ]
        )
        term_acc = term_acc.at[:, chosen].add(both_parts)
        return (query_acc + query_part, term_acc)

    start_back = (
        jnp.zeros((row_count, key_heads, sharing_count, HEAD_SIZE), jnp.float32),
        jnp.zeros((2, window_blocks, BLOCK_TOKENS, key_heads, HEAD_SIZE), jnp.float32),
    )
    query_acc, term_acc = lax.fori_loop(0, step_count, back_pass, start_back)
    slot_terms = term_acc.reshape(2, slot_count, row_count, key_heads, HEAD_SIZE)
    summed = slot_terms[:, hop_count]
    for slot_index in range(hop_count - 1, -1, -1):
        summed = (
            passed_along(summed.astype(jnp.bfloat16), "ctx", -1).astype(summed.dtype)
            + slot_terms[:, slot_index]
        )
    attended_heads = attended_loc.reshape(row_count, key_heads * sharing_count, HEAD_SIZE)
    query_heads = query_acc.reshape(row_count, key_heads * sharing_count, HEAD_SIZE).astype(
        jnp.bfloat16
    )
    key_grad_loc = summed[0].astype(jnp.bfloat16)
    value_grad_loc = summed[1].astype(jnp.bfloat16)
    attended, query_grad, key_gradient, value_gradient = (
        lax.all_to_all(attended_heads, "head", split_axis=0, concat_axis=1, tiled=True),
        lax.all_to_all(query_heads, "head", split_axis=0, concat_axis=1, tiled=True),
        lax.all_to_all(key_grad_loc, "head", split_axis=0, concat_axis=1, tiled=True),
        lax.all_to_all(value_grad_loc, "head", split_axis=0, concat_axis=1, tiled=True),
    )
    return (attended, query_grad, key_gradient, value_gradient)


def solution(mesh):
    in_specs = (
        P(("ctx", "head"), None, None),
        P(("ctx", "head"), None, None),
        P(("ctx", "head"), None, None),
        P(("ctx", "head"), None, None),
        P(),
        P(),
    )
    out_specs = (
        P(("ctx", "head"), None, None),
        P(("ctx", "head"), None, None),
        P(("ctx", "head"), None, None),
        P(("ctx", "head"), None, None),
    )
    return jax.shard_map(body, mesh=mesh, in_specs=in_specs, out_specs=out_specs, check_vma=False)
```

profile of v0, /device:TPU:102, one launch (start us, length us, event | category | flops | bytes accessed | tf_op | source)
XLA Modules:
  0.0 255.4 jit_solution(12364168022913801455)
XLA Ops:
  0.6 1.7 copy.118
  2.3 7.4 %all-to-all-start = ((bf16[64,8,128]{2,0,1:T(8,128)(2,1)}), bf16[64,8,128]{2,0,1:T(8,128)(2,1)S(1)}, u32[]{:S(2)}, u32[]{:S(2)}) async-start(bf16[64,8,128]{2,0,1:T(8,128)(2,1)} %copy.118), calls=%async_computation | async-start | bytes 262144 | tf_op jit(solution)/shard_map/all_to_all | solution.py:82
  11.3 1.6 copy.119
  13.0 1.9 all-to-all-done
  15.0 6.1 %all-to-all-start.1 = ((bf16[64,8,128]{2,0,1:T(8,128)(2,1)}), bf16[64,8,128]{2,0,1:T(8,128)(2,1)S(1)}, u32[]{:S(2)}, u32[]{:S(2)}) async-start(bf16[64,8,128]{2,0,1:T(8,128)(2,1)} %copy.119), calls=%async_computation.1 | async-start | bytes 262144 | tf_op jit(solution)/shard_map/all_to_all | solution.py:83
  22.7 2.9 %copy.120 = bf16[64,64,128]{2,0,1:T(8,128)(2,1)} copy(bf16[64,64,128]{2,1,0:T(8,128)(2,1)} %param.10) | data formatting | bytes 2097152 | tf_op args[0]
  26.4 6.5 %all-to-all-start.2 = ((bf16[64,64,128]{2,0,1:T(8,128)(2,1)}), bf16[64,64,128]{2,0,1:T(8,128)(2,1)S(1)}, u32[]{:S(2)}, u32[]{:S(2)}) async-start(bf16[64,64,128]{2,0,1:T(8,128)(2,1)} %copy.120), calls=%async_computation.2 | async-start | bytes 2097152 | tf_op jit(solution)/shard_map/all_to_all | solution.py:81
  33.0 1.9 collective-permute-start
  36.0 10.1 %collective-permute-done = bf16[2,512,1,128]{3,1,2,0:T(8,128)(2,1)} collective-permute-done((bf16[2,512,1,128]{3,1,2,0:T(8,128)(2,1)S(1)}, bf16[2,512,1,128]{3,1,2,0:T(8,128)(2,1)}, u32[]{:S(2)}, u32[]{:S(2)}) %collective-permute-start) | collective-permute-done | bytes 262176 | tf_op jit(solution)/shard_map/ppermute | solution.py:17
  46.1 1.9 collective-permute-start.1
  49.5 1.6 copy.125
  51.1 7.2 %all-to-all-start.4 = ((bf16[64,64,128]{2,0,1:T(8,128)(2,1)}), bf16[64,64,128]{2,0,1:T(8,128)(2,1)S(1)}, u32[]{:S(2)}, u32[]{:S(2)}) async-start(bf16[64,64,128]{2,0,1:T(8,128)(2,1)} %copy.125), calls=%async_computation.4 | async-start | bytes 2097152 | tf_op jit(solution)/shard_map/all_to_all | solution.py:84
  61.1 12.1 %all-to-all-done.4 = bf16[64,64,128]{2,0,1:T(8,128)(2,1)S(1)} async-done(((bf16[64,64,128]{2,0,1:T(8,128)(2,1)}), bf16[64,64,128]{2,0,1:T(8,128)(2,1)S(1)}, u32[]{:S(2)}, u32[]{:S(2)}) %all-to-all-start.4) | async-done | bytes 1048608 | tf_op jit(solution)/shard_map/all_to_all | solution.py:84
  75.6 35.1 %while.26 = (s32[]{:T(128)}, f32[1,8,512]{2,1,0:T(8,128)S(1)}, f32[1,8,512]{2,1,0:T(8,128)S(1)}, f32[512,1,8,128]{0,3,2,1:T(8,128)S(1)}, s32[]{:T(128)}, /*index...) while((s32[]{:T(128)}, f32[1,8,512]{2,1,0:T(8,128)S(1)}, ...), condition=%wide.region_9.10_spmd, body=%wide.region_6.9_spmd.sunk | while | flops 1098921472 | bytes 32529264 | solution.py:170
  78.3 1.6 gather_fusion.4
  79.8 1.6 gather_fusion.3
  83.3 1.7 fusion.78
  85.0 2.3 bitcast_add_fusion.7
  91.5 1.6 gather_fusion.3
  94.9 1.7 fusion.78
  96.6 2.3 bitcast_add_fusion.7
  103.1 1.6 gather_fusion.3
  106.5 1.7 fusion.78
  108.3 2.3 bitcast_add_fusion.7
  110.6 1.9 copy.123
  112.7 3.7 %multiply_reduce_fusion = (f32[512,8]{1,0:T(8,128)S(1)}, bf16[512,8,128]{2,1,0:T(8,128)(2,1)}) fusion(f32[512,1,8,128]{3,2,0,1:T(8,128)} %copy.123, f32[512,8]{1,0:T(8,128)S(1)} %copy.122, bf16[512,1,8,128]{3,2,0,1:T(8,128)(2,1)} %bitcast.363), kind=kLoop, calls=%fused_computation.65 | loop fusion | flops 3141632 | bytes 4227072 | tf_op jit(solution)/shard_map/reduce_sum | solution.py:173
  118.1 53.7 %while.27 = (s32[]{:T(128)}, f32[512,1,8,128]{0,3,2,1:T(8,128)S(1)}, f32[2,12,128,1,128]{4,2,1,0,3:T(8,128)}, s32[]{:T(128)}, s32[12]{0:T(128)S(1)}, /*index=5*/...) while((s32[]{:T(128)}, ...), condition=%wide.region_13.14_spmd, body=%wide.region_11.13_spmd.sunk | while | flops 2707752448 | bytes 55253928 | solution.py:203
  122.4 1.6 gather_fusion.5
  127.1 2.9 %fusion.90 = bf16[8,512,512]{1,2,0:T(8,128)(2,1)S(1)} fusion(f32[512,512,8]{1,0,2:T(8,128)S(1)} %fusion.89, f32[8,512]{1,0:T(8,128)S(1)} %bitcast.392, f32[8,512]{1,0:T(8,128)S(1)} %bitcast.391, pred[512,512]{0,1:T(8,128)(4,1)S(1)} %and_and_fusion.5, bf16[512,128,1]{1,0,2:T(8,128)(2,1)S(1)} %bitcast.369, bf16[512,1,8,128]{3,0,2,1:T(8,128)(2,1)S(1)} %copy-done.2), kind=kOutput, calls=%fused_computation.44.clone.1 | convolution fusion | flops 549453824 | bytes 14057472 | tf_op jit(solution)/shard_map/while/body/qhgd,khd->hgqk/dot_general | solution.py:60
  133.2 2.9 %scatter_fusion = f32[2,12,128,128]{3,2,1,0:T(8,128)} fusion(f32[2,12,128,128]{3,2,1,0:T(8,128)} %bitcast.353, s32[4]{0:T(128)S(1)} %compare_select_fusion.6, f32[4,2,128,128]{3,2,1,0:T(8,128)} %maximum_bitcast_fusion.2), kind=kCustom, calls=%fused_computation.10.clone.1 | custom fusion | flops 131072 | bytes 1572880 | tf_op jit(solution)/shard_map/while/body/scatter-add | solution.py:196
  140.2 1.6 gather_fusion.5
  144.9 2.9 %fusion.90 = bf16[8,512,512]{1,2,0:T(8,128)(2,1)S(1)} fusion(f32[512,512,8]{1,0,2:T(8,128)S(1)} %fusion.89, f32[8,512]{1,0:T(8,128)S(1)} %bitcast.392, f32[8,512]{1,0:T(8,128)S(1)} %bitcast.391, pred[512,512]{0,1:T(8,128)(4,1)S(1)} %and_and_fusion.5, bf16[512,128,1]{1,0,2:T(8,128)(2,1)S(1)} %bitcast.369, bf16[512,1,8,128]{3,0,2,1:T(8,128)(2,1)S(1)} %copy-done.2), kind=kOutput, calls=%fused_computation.44.clone.1 | convolution fusion | flops 549453824 | bytes 14057472 | tf_op jit(solution)/shard_map/while/body/qhgd,khd->hgqk/dot_general | solution.py:60
  151.1 2.9 %scatter_fusion = f32[2,12,128,128]{3,2,1,0:T(8,128)} fusion(f32[2,12,128,128]{3,2,1,0:T(8,128)} %bitcast.353, s32[4]{0:T(128)S(1)} %compare_select_fusion.6, f32[4,2,128,128]{3,2,1,0:T(8,128)} %maximum_bitcast_fusion.2), kind=kCustom, calls=%fused_computation.10.clone.1 | custom fusion | flops 131072 | bytes 1572880 | tf_op jit(solution)/shard_map/while/body/scatter-add | solution.py:196
  158.0 1.6 gather_fusion.5
  162.7 2.9 %fusion.90 = bf16[8,512,512]{1,2,0:T(8,128)(2,1)S(1)} fusion(f32[512,512,8]{1,0,2:T(8,128)S(1)} %fusion.89, f32[8,512]{1,0:T(8,128)S(1)} %bitcast.392, f32[8,512]{1,0:T(8,128)S(1)} %bitcast.391, pred[512,512]{0,1:T(8,128)(4,1)S(1)} %and_and_fusion.5, bf16[512,128,1]{1,0,2:T(8,128)(2,1)S(1)} %bitcast.369, bf16[512,1,8,128]{3,0,2,1:T(8,128)(2,1)S(1)} %copy-done.2), kind=kOutput, calls=%fused_computation.44.clone.1 | convolution fusion | flops 549453824 | bytes 14057472 | tf_op jit(solution)/shard_map/while/body/qhgd,khd->hgqk/dot_general | solution.py:60
  168.9 2.9 %scatter_fusion = f32[2,12,128,128]{3,2,1,0:T(8,128)} fusion(f32[2,12,128,128]{3,2,1,0:T(8,128)} %bitcast.353, s32[4]{0:T(128)S(1)} %compare_select_fusion.6, f32[4,2,128,128]{3,2,1,0:T(8,128)} %maximum_bitcast_fusion.2), kind=kCustom, calls=%fused_computation.10.clone.1 | custom fusion | flops 131072 | bytes 1572880 | tf_op jit(solution)/shard_map/while/body/scatter-add | solution.py:196
  172.8 1.9 collective-permute-start.2
  174.7 3.9 %collective-permute-done.2 = bf16[2,512,1,128]{3,1,0,2:T(8,128)(2,1)S(1)} collective-permute-done((bf16[2,512,1,128]{3,1,0,2:T(8,128)(2,1)S(1)}, bf16[2,512,1,128]{3,1,0,2:T(8,128)(2,1)S(1)}, u32[]{:S(2)}, u32[]{:S(2)}) %collective-permute-start.2) | collective-permute-done | bytes 262176 | tf_op jit(solution)/shard_map/ppermute | solution.py:17
  179.7 3.8 %collective-permute-start.3 = (bf16[2,512,1,128]{3,1,0,2:T(8,128)(2,1)S(1)}, bf16[2,512,1,128]{3,1,0,2:T(8,128)(2,1)S(1)}, u32[]{:S(2)}, u32[]{:S(2)}) collective-permute-start(bf16[2,512,1,128]{3,1,0,2:T(8,128)(2,1)S(1)} %fusion.35), channel_id=1, source_target_pairs={{1,0},{2,1},{3,2},{4,3},{5,4},{6,5},{7,6},{8,7},{9,8},{10,9},{11,1... | collective-permute-start | bytes 786440 | tf_op jit(solution)/shard_map/ppermute | solution.py:17
  183.5 3.9 %collective-permute-done.3 = bf16[2,512,1,128]{3,1,0,2:T(8,128)(2,1)S(1)} collective-permute-done((bf16[2,512,1,128]{3,1,0,2:T(8,128)(2,1)S(1)}, bf16[2,512,1,128]{3,1,0,2:T(8,128)(2,1)S(1)}, u32[]{:S(2)}, u32[]{:S(2)}) %collective-permute-start.3) | collective-permute-done | bytes 262176 | tf_op jit(solution)/shard_map/ppermute | solution.py:17
  190.4 5.7 %all-to-all-start.7 = ((bf16[8,2,4096]{2,1,0:T(2,128)(2,1)}), bf16[8,2,4096]{2,1,0:T(2,128)(2,1)S(1)}, u32[]{:S(2)}, u32[]{:S(2)}) async-start(bf16[8,2,4096]{2,1,0:T(2,128)(2,1)} %reshape.454), calls=%async_computation.7 | async-start | bytes 262144 | tf_op jit(solution)/shard_map/all_to_all | solution.py:221
  196.8 4.5 %all-to-all-done.7 = bf16[8,2,4096]{2,1,0:T(2,128)(2,1)S(1)} async-done(((bf16[8,2,4096]{2,1,0:T(2,128)(2,1)}), bf16[8,2,4096]{2,1,0:T(2,128)(2,1)S(1)}, u32[]{:S(2)}, u32[]{:S(2)}) %all-to-all-start.7) | async-done | bytes 131104 | tf_op jit(solution)/shard_map/all_to_all | solution.py:221
  201.4 10.6 %all_to_all.132 = bf16[8,2,4096]{2,1,0:T(2,128)(2,1)S(1)} all-to-all(bf16[8,2,4096]{2,1,0:T(2,128)(2,1)S(1)} %reshape.452), channel_id=1, replica_groups=mesh['head'=8,'ctx'=64] {'head'}, dimensions={0} | all-to-all | bytes 262144 | tf_op jit(solution)/shard_map/all_to_all | solution.py:220
  212.0 6.4 %all-to-all-start.3 = ((bf16[512,8,128]{2,1,0:T(8,128)(2,1)}), bf16[512,8,128]{2,1,0:T(8,128)(2,1)S(1)}, u32[]{:S(2)}, u32[]{:S(2)}) async-start(bf16[512,8,128]{2,1,0:T(8,128)(2,1)} %get-tuple-element.318), calls=%async_computation.3 | async-start | bytes 2097152 | tf_op jit(solution)/shard_map/all_to_all | solution.py:218
  218.4 1.8 copy.129
  220.1 13.5 %all-to-all-done.3 = bf16[512,8,128]{2,1,0:T(8,128)(2,1)S(1)} async-done(((bf16[512,8,128]{2,1,0:T(8,128)(2,1)}), bf16[512,8,128]{2,1,0:T(8,128)(2,1)S(1)}, u32[]{:S(2)}, u32[]{:S(2)}) %all-to-all-start.3) | async-done | bytes 1048608 | tf_op jit(solution)/shard_map/all_to_all | solution.py:218
  233.6 6.0 %all-to-all-start.5 = ((bf16[512,8,128]{2,1,0:T(8,128)(2,1)}), bf16[512,8,128]{2,1,0:T(8,128)(2,1)S(1)}, u32[]{:S(2)}, u32[]{:S(2)}) async-start(bf16[512,8,128]{2,1,0:T(8,128)(2,1)} %bitcast.230), calls=%async_computation.5 | async-start | bytes 2097152 | tf_op jit(solution)/shard_map/all_to_all | solution.py:219
  242.7 11.5 %all-to-all-done.5 = bf16[512,8,128]{2,1,0:T(8,128)(2,1)S(1)} async-done(((bf16[512,8,128]{2,1,0:T(8,128)(2,1)}), bf16[512,8,128]{2,1,0:T(8,128)(2,1)S(1)}, u32[]{:S(2)}, u32[]{:S(2)}) %all-to-all-start.5) | async-done | bytes 1048608 | tf_op jit(solution)/shard_map/all_to_all | solution.py:219
  (145 shorter events, 70.4 us)
Async XLA Ops:
  0.6 48.8 %copy-start.1 = (bf16[64,64,128]{2,1,0:T(8,128)(2,1)S(1)}, bf16[64,64,128]{2,1,0:T(8,128)(2,1)}, u32[]{:S(2)}) copy-start(bf16[64,64,128]{2,1,0:T(8,128)(2,1)} %param.13) | copy-start | bytes 3145732
  2.3 12.7 %all-to-all-start = ((bf16[64,8,128]{2,0,1:T(8,128)(2,1)}), bf16[64,8,128]{2,0,1:T(8,128)(2,1)S(1)}, u32[]{:S(2)}, u32[]{:S(2)}) async-start(bf16[64,8,128]{2,0,1:T(8,128)(2,1)} %copy.118), calls=%async_computation | async-start | bytes 262144 | tf_op jit(solution)/shard_map/all_to_all | solution.py:82
  15.0 11.4 %all-to-all-start.1 = ((bf16[64,8,128]{2,0,1:T(8,128)(2,1)}), bf16[64,8,128]{2,0,1:T(8,128)(2,1)S(1)}, u32[]{:S(2)}, u32[]{:S(2)}) async-start(bf16[64,8,128]{2,0,1:T(8,128)(2,1)} %copy.119), calls=%async_computation.1 | async-start | bytes 262144 | tf_op jit(solution)/shard_map/all_to_all | solution.py:83
  26.4 24.7 %all-to-all-start.2 = ((bf16[64,64,128]{2,0,1:T(8,128)(2,1)}), bf16[64,64,128]{2,0,1:T(8,128)(2,1)S(1)}, u32[]{:S(2)}, u32[]{:S(2)}) async-start(bf16[64,64,128]{2,0,1:T(8,128)(2,1)} %copy.120), calls=%async_computation.2 | async-start | bytes 2097152 | tf_op jit(solution)/shard_map/all_to_all | solution.py:81
  33.0 13.1 %collective-permute-start = (bf16[2,512,1,128]{3,1,2,0:T(8,128)(2,1)S(1)}, bf16[2,512,1,128]{3,1,2,0:T(8,128)(2,1)}, u32[]{:S(2)}, u32[]{:S(2)}) collective-permute-start(bf16[2,512,1,128]{3,1,2,0:T(8,128)(2,1)S(1)} %pad_maximum_fusion.1), channel_id=1, source_target_pairs={{0,1},{1,2},{2,3},{3,4},{4,5},{5,6},{6,7},{7,8},{8,9},{9,10},{10,1... | collective-permute-start | bytes 786440 | tf_op jit(solution)/shard_map/ppermute | solution.py:17
  46.1 12.9 %collective-permute-start.1 = (bf16[2,512,1,128]{3,1,2,0:T(8,128)(2,1)}, bf16[2,512,1,128]{3,1,2,0:T(8,128)(2,1)}, u32[]{:S(2)}, u32[]{:S(2)}) collective-permute-start(bf16[2,512,1,128]{3,1,2,0:T(8,128)(2,1)} %collective-permute-done), channel_id=1, source_target_pairs={{0,1},{1,2},{2,3},{3,4},{4,5},{5,6},{6,7},{7,8},{8,9},{9,10},{10,1... | collective-permute-start | bytes 786440 | tf_op jit(solution)/shard_map/ppermute | solution.py:17
  51.1 22.1 %all-to-all-start.4 = ((bf16[64,64,128]{2,0,1:T(8,128)(2,1)}), bf16[64,64,128]{2,0,1:T(8,128)(2,1)S(1)}, u32[]{:S(2)}, u32[]{:S(2)}) async-start(bf16[64,64,128]{2,0,1:T(8,128)(2,1)} %copy.125), calls=%async_computation.4 | async-start | bytes 2097152 | tf_op jit(solution)/shard_map/all_to_all | solution.py:84
  73.9 1.4 copy-start
  124.3 1.3 copy-start.2
  142.1 1.3 copy-start.2
  159.9 1.3 copy-start.2
  172.8 5.8 %collective-permute-start.2 = (bf16[2,512,1,128]{3,1,0,2:T(8,128)(2,1)S(1)}, bf16[2,512,1,128]{3,1,0,2:T(8,128)(2,1)S(1)}, u32[]{:S(2)}, u32[]{:S(2)}) collective-permute-start(bf16[2,512,1,128]{3,1,0,2:T(8,128)(2,1)S(1)} %fusion.38), channel_id=1, source_target_pairs={{1,0},{2,1},{3,2},{4,3},{5,4},{6,5},{7,6},{8,7},{9,8},{10,9},{11,1... | collective-permute-start | bytes 786440 | tf_op jit(solution)/shard_map/ppermute | solution.py:17
  179.7 7.7 %collective-permute-start.3 = (bf16[2,512,1,128]{3,1,0,2:T(8,128)(2,1)S(1)}, bf16[2,512,1,128]{3,1,0,2:T(8,128)(2,1)S(1)}, u32[]{:S(2)}, u32[]{:S(2)}) collective-permute-start(bf16[2,512,1,128]{3,1,0,2:T(8,128)(2,1)S(1)} %fusion.35), channel_id=1, source_target_pairs={{1,0},{2,1},{3,2},{4,3},{5,4},{6,5},{7,6},{8,7},{9,8},{10,9},{11,1... | collective-permute-start | bytes 786440 | tf_op jit(solution)/shard_map/ppermute | solution.py:17
  190.4 10.9 %all-to-all-start.7 = ((bf16[8,2,4096]{2,1,0:T(2,128)(2,1)}), bf16[8,2,4096]{2,1,0:T(2,128)(2,1)S(1)}, u32[]{:S(2)}, u32[]{:S(2)}) async-start(bf16[8,2,4096]{2,1,0:T(2,128)(2,1)} %reshape.454), calls=%async_computation.7 | async-start | bytes 262144 | tf_op jit(solution)/shard_map/all_to_all | solution.py:221
  212.0 21.6 %all-to-all-start.3 = ((bf16[512,8,128]{2,1,0:T(8,128)(2,1)}), bf16[512,8,128]{2,1,0:T(8,128)(2,1)S(1)}, u32[]{:S(2)}, u32[]{:S(2)}) async-start(bf16[512,8,128]{2,1,0:T(8,128)(2,1)} %get-tuple-element.318), calls=%async_computation.3 | async-start | bytes 2097152 | tf_op jit(solution)/shard_map/all_to_all | solution.py:218
  233.6 20.5 %all-to-all-start.5 = ((bf16[512,8,128]{2,1,0:T(8,128)(2,1)}), bf16[512,8,128]{2,1,0:T(8,128)(2,1)S(1)}, u32[]{:S(2)}, u32[]{:S(2)}) async-start(bf16[512,8,128]{2,1,0:T(8,128)(2,1)} %bitcast.230), calls=%async_computation.5 | async-start | bytes 2097152 | tf_op jit(solution)/shard_map/all_to_all | solution.py:219
where the time goes:
time: 257 us; the launch traced here: 255 us
  waiting for transfers between devices  62.1 us (24%)
  starting transfers between devices  54.9 us (21%)
  local copies, waits for them, and re-layouts  53.5 us (21%)
  other arithmetic  36.1 us (14%)
  matrix products  35.6 us (14%)
  blocking collectives  10.6 us (4%)
    ppermute x4, waiting for transfers between devices, passed_along(): return lax.ppermute(block, axis, route)  17.8 us
    all_to_all x1, waiting for transfers between devices, body(): lax.all_to_all(attended_heads, 'head', split_axis=0, concat_axis=1, tiled...  13.5 us
    all_to_all x1, waiting for transfers between devices, body(): lax.all_to_all(out_grad, 'head', split_axis=1, concat_axis=0, tiled=True)  12.1 us
    all_to_all x1, waiting for transfers between devices, body(): lax.all_to_all(query_heads, 'head', split_axis=0, concat_axis=1, tiled=True)  11.5 us
    all_to_all x1, blocking collectives, body(): lax.all_to_all(key_grad_loc, 'head', split_axis=0, concat_axis=1, tiled=T...  10.6 us
    unnamed x16, local copies, waits for them, and re-layouts  10.3 us
    ppermute x4, starting transfers between devices, passed_along(): return lax.ppermute(block, axis, route)  9.57 us
    gather x6, local copies, waits for them, and re-layouts, slot_group(): key_blocks[chosen].reshape(per_step * BLOCK_TOKENS, key_heads, HEAD_SIZE)  9.4 us
  transfers between devices with their start and end apart: 11, of which 9 were waited for; matrix products, arithmetic and copies ran while one was open for 8% of the time, Pallas kernels for 0%

commit v1 on v0

v1 whole, which is shorter than its diff:
```python
import functools
import math

import jax
import jax.numpy as jnp
from jax import lax
from jax.experimental import pallas as pl
from jax.experimental.pallas import tpu as pltpu
from jax.sharding import PartitionSpec as P

HEAD_SIZE = 128
BLOCK = 128
CELL_BLOCKS = 4
SLOTS = 3
WINDOW_BLOCKS = SLOTS * CELL_BLOCKS
WINDOW = WINDOW_BLOCKS * BLOCK
CHUNK = 2 * BLOCK
PADDED = WINDOW + BLOCK
REACH = 10 * BLOCK
SHARE = 8
ROWS = BLOCK * SHARE
TILE = 256

SCALE = HEAD_SIZE ** (-0.5)
EXP2_SCALE = SCALE * math.log2(math.e)
NEG_BIG = -1e30

NT = (((1,), (1,)), ((), ()))
NN = (((1,), (0,)), ((), ()))


def dot(a, b, dims=NN):
    return lax.dot_general(a, b, dims, preferred_element_type=jnp.float32)


def passed_along(block, axis, distance):
    devices = range(lax.axis_size(axis))
    route = [(i - distance, i) for i in devices if i - distance in devices]
    return lax.ppermute(block, axis, route)


def stored_rows(kv_ref, block, which):
    first = kv_ref[2 * block, pl.ds(64 * which, 64), :]
    second = kv_ref[2 * block + 1, pl.ds(64 * which, 64), :]
    return jnp.concatenate([first, second], axis=0)


def window_start(scal_ref, slot, block):
    index = (SLOTS - 1 - slot) * CELL_BLOCKS + block
    return pl.multiple_of(scal_ref[index] * BLOCK, BLOCK)


def allowed_tile(key_start, doc_start, query_pos):
    key_pos = key_start + lax.broadcasted_iota(jnp.int32, (CHUNK, TILE), 0)
    return (key_pos >= doc_start) & (key_pos <= query_pos)


def row_positions(first_block, tile):
    lane = lax.broadcasted_iota(jnp.int32, (1, TILE), 1) + tile * TILE
    return first_block * BLOCK + lax.shift_right_logical(lane, 3)


def forward_kernel(scal_ref, q_ref, doc_ref, kv0_ref, kv1_ref, kv2_ref, out_ref, out_t_ref, lse_ref, key_seq, value_t, scores, acc, top):
    step = pl.program_id(0)

    @pl.when(step == 0)
    def _():
        for slot, kv_ref in enumerate((kv0_ref, kv1_ref, kv2_ref)):
            for block in range(CELL_BLOCKS):
                start = window_start(scal_ref, slot, block)
                key_seq[pl.ds(start, BLOCK), :] = stored_rows(kv_ref, block, 0)
                value = stored_rows(kv_ref, block, 1).astype(jnp.float32)
                value_t[:, pl.ds(start, BLOCK)] = value.T.astype(jnp.bfloat16)
        key_seq[pl.ds(WINDOW, BLOCK), :] = jnp.zeros((BLOCK, HEAD_SIZE), jnp.bfloat16)
        value_t[:, pl.ds(WINDOW, BLOCK)] = jnp.zeros((HEAD_SIZE, BLOCK), jnp.bfloat16)

    first_block = scal_ref[WINDOW_BLOCKS + step]
    low_block = scal_ref[WINDOW_BLOCKS + CELL_BLOCKS + step]
    chunks = lax.shift_right_logical(first_block - low_block + 2, 1)
    top[...] = jnp.full_like(top, NEG_BIG)
    acc[...] = jnp.zeros_like(acc)

    def score_chunk(turn, _):
        key_start = pl.multiple_of((low_block + 2 * turn) * BLOCK, BLOCK)
        keys = key_seq[pl.ds(key_start, CHUNK), :]
        for tile in range(ROWS // TILE):
            cols = pl.ds(tile * TILE, TILE)
            queries = q_ref[tile // 2, pl.ds((tile % 2) * TILE, TILE), :]
            raw = dot(keys, queries, NT)
            allowed = allowed_tile(key_start, doc_ref[0, :, cols], row_positions(first_block, tile))
            raw = jnp.where(allowed, raw, NEG_BIG)
            scores[pl.ds(pl.multiple_of(turn * CHUNK, CHUNK), CHUNK), cols] = raw
            part = jnp.max(raw.reshape(CHUNK // 8, 8, TILE), axis=0)
            top[:, cols] = jnp.maximum(top[:, cols], part)
        return 0

    lax.fori_loop(0, chunks, score_chunk, 0)
    highest = jnp.max(top[...], axis=0, keepdims=True) * EXP2_SCALE
    top[...] = jnp.zeros_like(top)

    def value_chunk(turn, _):
        key_start = pl.multiple_of((low_block + 2 * turn) * BLOCK, BLOCK)
        values = value_t[:, pl.ds(key_start, CHUNK)]
        for tile in range(ROWS // TILE):
            cols = pl.ds(tile * TILE, TILE)
            raw = scores[pl.ds(pl.multiple_of(turn * CHUNK, CHUNK), CHUNK), cols]
            weights = jnp.exp2(raw * EXP2_SCALE - highest[:, tile * TILE : (tile + 1) * TILE])
            top[:, cols] += jnp.sum(weights.reshape(CHUNK // 8, 8, TILE), axis=0)
            acc[:, cols] += dot(values, weights.astype(jnp.bfloat16))
        return 0

    lax.fori_loop(0, chunks, value_chunk, 0)
    total = jnp.sum(top[...], axis=0, keepdims=True)
    lse_ref[0] = highest + jnp.log2(total)
    out_t = acc[...] * (1.0 / total)
    out_t_ref[0] = out_t.astype(jnp.bfloat16)
    out = out_t.T.astype(jnp.bfloat16)
    out_ref[0] = out[: ROWS // 2]
    out_ref[1] = out[ROWS // 2 :]


def backward_kernel(scal_ref, q_ref, grad_ref, out_t_ref, lse_ref, doc_ref, kv0_ref, kv1_ref, kv2_ref, dq_ref, dkv0_ref, dkv1_ref, dkv2_ref, key_seq, value_seq, key_t, dk_acc, dv_acc, dq_t, weights_low, grads_low, delta):
    step = pl.program_id(0)

    @pl.when(step == 0)
    def _():
        for slot, kv_ref in enumerate((kv0_ref, kv1_ref, kv2_ref)):
            for block in range(CELL_BLOCKS):
                start = window_start(scal_ref, slot, block)
                key = stored_rows(kv_ref, block, 0)
                key_seq[pl.ds(start, BLOCK), :] = key
                key_t[:, pl.ds(start, BLOCK)] = key.astype(jnp.float32).T.astype(jnp.bfloat16)
                value_seq[pl.ds(start, BLOCK), :] = stored_rows(kv_ref, block, 1)
        zeros = jnp.zeros((BLOCK, HEAD_SIZE), jnp.bfloat16)
        key_seq[pl.ds(WINDOW, BLOCK), :] = zeros
        value_seq[pl.ds(WINDOW, BLOCK), :] = zeros
        key_t[:, pl.ds(WINDOW, BLOCK)] = zeros
        dk_acc[...] = jnp.zeros_like(dk_acc)
        dv_acc[...] = jnp.zeros_like(dv_acc)

    first_block = scal_ref[WINDOW_BLOCKS + step]
    low_block = scal_ref[WINDOW_BLOCKS + CELL_BLOCKS + step]
    chunks = lax.shift_right_logical(first_block - low_block + 2, 1)
    dq_t[...] = jnp.zeros_like(dq_t)
    for half in range(2):
        cols = slice(half * ROWS // 2, (half + 1) * ROWS // 2)
        grad_t = grad_ref[half].astype(jnp.float32).T
        delta[:, cols] = jnp.sum(grad_t * out_t_ref[0, :, cols].astype(jnp.float32), axis=0, keepdims=True)

    def chunk(turn, _):
        key_start = pl.multiple_of((low_block + 2 * turn) * BLOCK, BLOCK)
        keys = key_seq[pl.ds(key_start, CHUNK), :]
        values = value_seq[pl.ds(key_start, CHUNK), :]
        for tile in range(ROWS // TILE):
            cols = pl.ds(tile * TILE, TILE)
            half, rows = tile // 2, pl.ds((tile % 2) * TILE, TILE)
            raw = dot(keys, q_ref[half, rows, :], NT)
            allowed = allowed_tile(key_start, doc_ref[0, :, cols], row_positions(first_block, tile))
            weights = jnp.exp2(jnp.where(allowed, raw * EXP2_SCALE - lse_ref[0, :, cols], NEG_BIG))
            weights_low[:, cols] = weights.astype(jnp.bfloat16)
            sent = dot(values, grad_ref[half, rows, :], NT)
            grads = (weights * (sent - delta[:, cols])).astype(jnp.bfloat16)
            grads_low[:, cols] = grads
            dq_t[:, cols] += dot(key_t[:, pl.ds(key_start, CHUNK)], grads)
        queries = jnp.concatenate([q_ref[0], q_ref[1]], axis=0)
        out_grads = jnp.concatenate([grad_ref[0], grad_ref[1]], axis=0)
        dk_acc[pl.ds(key_start, CHUNK), :] += dot(grads_low[...], queries)
        dv_acc[pl.ds(key_start, CHUNK), :] += dot(weights_low[...], out_grads)
        return 0

    lax.fori_loop(0, chunks, chunk, 0)
    query_grad = (dq_t[...] * SCALE).T.astype(jnp.bfloat16)
    dq_ref[0] = query_grad[: ROWS // 2]
    dq_ref[1] = query_grad[ROWS // 2 :]

    @pl.when(step == CELL_BLOCKS - 1)
    def _():
        for slot, dkv_ref in enumerate((dkv0_ref, dkv1_ref, dkv2_ref)):
            for block in range(CELL_BLOCKS):
                start = window_start(scal_ref, slot, block)
                dk = (dk_acc[pl.ds(start, BLOCK), :] * SCALE).astype(jnp.bfloat16)
                dv = dv_acc[pl.ds(start, BLOCK), :].astype(jnp.bfloat16)
                for half in range(2):
                    rows = slice(half * 64, (half + 1) * 64)
                    dkv_ref[2 * block + half, pl.ds(0, 64), :] = dk[rows]
                    dkv_ref[2 * block + half, pl.ds(64, 64), :] = dv[rows]


def row_spec():
    return pl.BlockSpec((2, ROWS // 2, HEAD_SIZE), lambda b, s: (b, 0, 0))


def lane_spec(rows):
    return pl.BlockSpec((1, rows, ROWS), lambda b, s: (b, 0, 0))


def kv_spec():
    return pl.BlockSpec((8, 128, HEAD_SIZE), lambda b, s: (0, 0, 0))


def params():
    return pltpu.CompilerParams(dimension_semantics=("arbitrary",), vmem_limit_bytes=40 * 1024 * 1024)


def forward(scal, q_in, doc_rows, kv):
    return pl.pallas_call(
        forward_kernel,
        grid_spec=pltpu.PrefetchScalarGridSpec(
            num_scalar_prefetch=1,
            grid=(CELL_BLOCKS,),
            in_specs=[row_spec(), lane_spec(1), kv_spec(), kv_spec(), kv_spec()],
            out_specs=[row_spec(), lane_spec(HEAD_SIZE), lane_spec(1)],
            scratch_shapes=[
                pltpu.VMEM((PADDED, HEAD_SIZE), jnp.bfloat16),
                pltpu.VMEM((HEAD_SIZE, PADDED), jnp.bfloat16),
                pltpu.VMEM((REACH, ROWS), jnp.float32),
                pltpu.VMEM((HEAD_SIZE, ROWS), jnp.float32),
                pltpu.VMEM((8, ROWS), jnp.float32),
            ],
        ),
        out_shape=[
            jax.ShapeDtypeStruct((8, ROWS // 2, HEAD_SIZE), jnp.bfloat16),
            jax.ShapeDtypeStruct((CELL_BLOCKS, HEAD_SIZE, ROWS), jnp.bfloat16),
            jax.ShapeDtypeStruct((CELL_BLOCKS, 1, ROWS), jnp.float32),
        ],
        compiler_params=params(),
        cost_estimate=pl.CostEstimate(flops=4_000_000_000, bytes_accessed=4_000_000, transcendentals=4_000_000),
        name="forward",
    )(scal, q_in, doc_rows, *kv)


def backward(scal, q_in, grad_in, out_t, lse, doc_rows, kv):
    dkv_shape = jax.ShapeDtypeStruct((8, 128, HEAD_SIZE), jnp.bfloat16)
    return pl.pallas_call(
        backward_kernel,
        grid_spec=pltpu.PrefetchScalarGridSpec(
            num_scalar_prefetch=1,
            grid=(CELL_BLOCKS,),
            in_specs=[row_spec(), row_spec(), lane_spec(HEAD_SIZE), lane_spec(1), lane_spec(1), kv_spec(), kv_spec(), kv_spec()],
            out_specs=[row_spec(), kv_spec(), kv_spec(), kv_spec()],
            scratch_shapes=[
                pltpu.VMEM((PADDED, HEAD_SIZE), jnp.bfloat16),
                pltpu.VMEM((PADDED, HEAD_SIZE), jnp.bfloat16),
                pltpu.VMEM((HEAD_SIZE, PADDED), jnp.bfloat16),
                pltpu.VMEM((PADDED, HEAD_SIZE), jnp.float32),
                pltpu.VMEM((PADDED, HEAD_SIZE), jnp.float32),
                pltpu.VMEM((HEAD_SIZE, ROWS), jnp.float32),
                pltpu.VMEM((CHUNK, ROWS), jnp.bfloat16),
                pltpu.VMEM((CHUNK, ROWS), jnp.bfloat16),
                pltpu.VMEM((1, ROWS), jnp.float32),
            ],
        ),
        out_shape=[jax.ShapeDtypeStruct((8, ROWS // 2, HEAD_SIZE), jnp.bfloat16), dkv_shape, dkv_shape, dkv_shape],
        compiler_params=params(),
        cost_estimate=pl.CostEstimate(flops=10_000_000_000, bytes_accessed=6_000_000, transcendentals=4_000_000),
        name="backward",
    )(scal, q_in, grad_in, out_t, lse, doc_rows, *kv)


def by_head(rows):
    tokens = rows.shape[0]
    split = rows.reshape(tokens, 8, -1, HEAD_SIZE).transpose(1, 0, 2, 3)
    return split.reshape(8, -1, HEAD_SIZE)


def exchanged(block):
    return lax.all_to_all(block, "head", split_axis=0, concat_axis=0, tiled=True)


def plan(doc_lengths, stored_block_order):
    cell = lax.axis_index("ctx")
    starts = jnp.cumsum(doc_lengths) - doc_lengths
    window_first = (cell - (SLOTS - 1)) * CELL_BLOCKS
    padded = jnp.pad(stored_block_order, (WINDOW_BLOCKS - CELL_BLOCKS, 0))
    window_order = lax.dynamic_slice_in_dim(padded, cell * CELL_BLOCKS, WINDOW_BLOCKS, 0)
    base = jnp.arange(WINDOW_BLOCKS, dtype=jnp.int32) // CELL_BLOCKS * CELL_BLOCKS
    place = base + window_order % CELL_BLOCKS
    own_place = place[WINDOW_BLOCKS - CELL_BLOCKS :]
    own_block = window_first + own_place
    token = lax.broadcasted_iota(jnp.int32, (CELL_BLOCKS, 1, ROWS), 2) // SHARE
    pos = own_block[:, None, None] * BLOCK + token
    begun = starts <= pos[..., None]
    doc_start = jnp.max(jnp.where(begun, starts, 0), axis=-1)
    doc_rows = doc_start - window_first * BLOCK
    low = jnp.max(jnp.where(starts <= own_block[:, None] * BLOCK, starts, 0), axis=-1)
    low_block = low // BLOCK - window_first
    scal = jnp.concatenate([place, own_place, low_block]).astype(jnp.int32)
    return scal, doc_rows.astype(jnp.int32)


def body(queries, keys, values, out_grad, doc_lengths, stored_block_order):
    scal, doc_rows = plan(doc_lengths, stored_block_order)
    first_in = exchanged(jnp.concatenate([by_head(queries), by_head(keys), by_head(values)], axis=1))
    kv0 = first_in[:, 512:, :]
    kv1 = passed_along(kv0, "ctx", 1)
    kv2 = passed_along(kv1, "ctx", 1)
    grad_in = exchanged(by_head(out_grad))
    kv = (kv0, kv1, kv2)
    attended_loc, out_t, lse = forward(scal, first_in, doc_rows, kv)
    attended_in = exchanged(attended_loc)
    query_grad_loc, dkv0, dkv1, dkv2 = backward(scal, first_in, grad_in, out_t, lse, doc_rows, kv)
    carried = passed_along(dkv2, "ctx", -1).astype(jnp.float32) + dkv1.astype(jnp.float32)
    carried = passed_along(carried.astype(jnp.bfloat16), "ctx", -1).astype(jnp.float32) + dkv0.astype(jnp.float32)
    last_in = exchanged(jnp.concatenate([query_grad_loc, carried.astype(jnp.bfloat16)], axis=1))
    tokens = queries.shape[0]

    def by_token(block, heads):
        return block.reshape(8, tokens, heads, HEAD_SIZE).transpose(1, 0, 2, 3).reshape(tokens, -1, HEAD_SIZE)

    attended = by_token(attended_in, SHARE)
    query_grad = by_token(last_in[:, :512], SHARE)
    key_gradient = by_token(last_in[:, 512:576], 1)
    value_gradient = by_token(last_in[:, 576:], 1)
    return attended, query_grad, key_gradient, value_gradient


def solution(mesh):
    spec = P(("ctx", "head"), None, None)
    return jax.shard_map(
        body,
        mesh=mesh,
        in_specs=(spec, spec, spec, spec, P(), P()),
        out_specs=(spec, spec, spec, spec),
        check_vma=False,
    )
```

time: 257 us -> 155 us (0.60)
  the two profiles are of different devices: /device:TPU:102 before, /device:TPU:418 now
where the time goes in v1:
time: 155 us
  waiting for transfers between devices  63.9 us (41%)
  Pallas kernels  38.3 us (25%)
  starting transfers between devices  32.1 us (21%)
  local copies, waits for them, and re-layouts  16.4 us (11%)
  other arithmetic  3.43 us (2%)
    ppermute x4, waiting for transfers between devices, passed_along(): return lax.ppermute(block, axis, route)  32.5 us
    all_to_all x4, waiting for transfers between devices, exchanged(): lax.all_to_all(block, 'head', split_axis=0, concat_axis=0, tiled=True)  31.4 us
    pallas_call x1, Pallas kernels, backward(): pl.pallas_call(backward_kernel, grid_spec=pltpu.PrefetchScalarGridSpec(nu...  25 us
    all_to_all x4, starting transfers between devices, exchanged(): lax.all_to_all(block, 'head', split_axis=0, concat_axis=0, tiled=True)  24.2 us
    pallas_call x1, Pallas kernels, forward(): pl.pallas_call(forward_kernel, grid_spec=pltpu.PrefetchScalarGridSpec(num...  13.3 us
    unnamed x42, local copies, waits for them, and re-layouts  12.3 us
    ppermute x4, starting transfers between devices, passed_along(): return lax.ppermute(block, axis, route)  7.92 us
  transfers between devices with their start and end apart: 8, of which 6 were waited for; matrix products, arithmetic and copies ran while one was open for 3% of the time, Pallas kernels for 9%

profile of v1, /device:TPU:418, one launch (start us, length us, event | category | flops | bytes accessed | tf_op | source)
XLA Modules:
  0.0 154.9 jit_solution(615370806060356181)
XLA Ops:
  0.6 0.0 copy-start
  0.7 1.2 copy-done
  1.9 0.2 copy_bitcast_fusion.3
  2.1 1.2 pad_maximum_fusion
  3.3 6.2 %all-to-all-start = ((bf16[8,640,128]{2,1,0:T(8,128)(2,1)}), bf16[8,640,128]{2,1,0:T(8,128)(2,1)S(1)}, u32[]{:S(2)}, u32[]{:S(2)}) async-start(bf16[8,640,128]{2,1,0:T(8,128)(2,1)} %pad_maximum_fusion), calls=%async_computation | async-start | bytes 2621440 | tf_op jit(solution)/shard_map/all_to_all | solution.py:267
  9.5 0.1 copy.28
  9.6 0.1 reduce-window.9
  9.6 0.1 reduce.1
  9.8 0.1 fusion.3
  9.9 0.1 fusion.7
  10.0 0.1 select_add_fusion
  10.0 0.2 select_reduce_fusion
  10.3 1.2 copy_bitcast_fusion.1
  11.4 16.3 %all-to-all-done.q_ref = bf16[8,640,128]{2,1,0:T(8,128)(2,1)S(1)} async-done(((bf16[8,640,128]{2,1,0:T(8,128)(2,1)}), bf16[8,640,128]{2,1,0:T(8,128)(2,1)S(1)}, u32[]{:S(2)}, u32[]{:S(2)}) %all-to-all-start) | async-done | bytes 1310752 | tf_op jit(solution)/shard_map/all_to_all | solution.py:267
  27.7 4.5 %all-to-all-start.2 = ((bf16[8,512,128]{2,1,0:T(8,128)(2,1)}), bf16[8,512,128]{2,1,0:T(8,128)(2,1)S(1)}, u32[]{:S(2)}, u32[]{:S(2)}) async-start(bf16[8,512,128]{2,1,0:T(8,128)(2,1)} %copy_bitcast_fusion.1), calls=%async_computation.2 | async-start | bytes 2097152 | tf_op jit(solution)/shard_map/all_to_all | solution.py:267
  32.2 1.9 %collective-permute-start = (bf16[8,128,128]{2,1,0:T(8,128)(2,1)S(1)}, bf16[8,128,128]{2,1,0:T(8,128)(2,1)S(1)}, u32[]{:S(2)}, u32[]{:S(2)}) collective-permute-start(bf16[8,128,128]{2,1,0:T(8,128)(2,1)S(1)} %slice.20.kv0_ref), channel_id=1, source_target_pairs={{0,1},{1,2},{2,3},{3,4},{4,5},{5,6},{6,7},{7,8},{8,9},{9,10},{10,1... | collective-permute-start | bytes 786440 | tf_op jit(solution)/shard_map/ppermute | solution.py:39
  34.2 0.2 select_reduce_fusion.1
  34.4 14.1 %collective-permute-done.kv1_ref = bf16[8,128,128]{2,1,0:T(8,128)(2,1)S(1)} collective-permute-done((bf16[8,128,128]{2,1,0:T(8,128)(2,1)S(1)}, bf16[8,128,128]{2,1,0:T(8,128)(2,1)S(1)}, u32[]{:S(2)}, u32[]{:S(2)}) %collective-permute-start) | collective-permute-done | bytes 262176 | tf_op jit(solution)/shard_map/ppermute | solution.py:39
  48.5 1.9 %collective-permute-start.1 = (bf16[8,128,128]{2,1,0:T(8,128)(2,1)S(1)}, bf16[8,128,128]{2,1,0:T(8,128)(2,1)S(1)}, u32[]{:S(2)}, u32[]{:S(2)}) collective-permute-start(bf16[8,128,128]{2,1,0:T(8,128)(2,1)S(1)} %collective-permute-done.kv1_ref), channel_id=1, source_target_pairs={{0,1},{1,2},{2,3},{3,4},{4,5},{5,6},{6,7},{7,8},{8,9},{9,10},{10,1... | collective-permute-start | bytes 786440 | tf_op jit(solution)/shard_map/ppermute | solution.py:39
  50.4 0.1 pad_add_fusion.scal_ref
  50.5 5.7 %collective-permute-done.1.kv2_ref = bf16[8,128,128]{2,1,0:T(8,128)(2,1)S(1)} collective-permute-done((bf16[8,128,128]{2,1,0:T(8,128)(2,1)S(1)}, bf16[8,128,128]{2,1,0:T(8,128)(2,1)S(1)}, u32[]{:S(2)}, u32[]{:S(2)}) %collective-permute-start.1) | collective-permute-done | bytes 262176 | tf_op jit(solution)/shard_map/ppermute | solution.py:39
  56.2 13.3 %forward.1 = (bf16[8,512,128]{2,1,0:T(8,128)(2,1)}, bf16[4,128,1024]{2,1,0:T(8,128)(2,1)S(1)}, f32[4,1,1024]{2,1,0:T(1,128)S(1)}) custom-call(s32[20]{0:T(128)S(1)} %pad_add_fusion.scal_ref, bf16[8,640,128]{2,1,0:T(8,128)(2,1)S(1)} %all-to-all-done.q_ref, s32[4,1,1024]{2,1,0:T(1,128)S(1)} %sub.41.doc_ref, bf16[8,128,128]{2,1,0:T(8,128)(2,1)S(1)} %slice.20.kv0_ref, ...), custom_call_target="tpu_custom_call" | custom-call | flops 4000000000 | bytes 4000000 | tf_op jit(solution)/shard_map/forward/pallas_call | solution.py:206
  69.4 0.7 copy-done.7
  70.2 0.7 copy-done.9
  70.9 0.7 copy-done.11
  71.6 1.0 copy-done.13
  72.6 0.9 copy-done.8
  73.6 0.9 copy-done.10
  74.5 0.9 copy-done.12
  75.5 1.2 copy-done.14
  76.7 25.0 %backward.1 = (bf16[8,512,128]{2,1,0:T(8,128)(2,1)S(1)}, bf16[8,128,128]{2,1,0:T(8,128)(2,1)S(1)}, bf16[8,128,128]{2,1,0:T(8,128)(2,1)S(1)}, bf16[8,128,128]{2,1,0:T(8,128)(2,1)}) custom-call(s32[20]{0:T(128)S(1)} %pad_add_fusion.scal_ref, bf16[8,640,128]{2,1,0:T(8,128)(2,1)S(1)} %all-to-all-done.q_ref, bf16[8,512,128]{2,1,0:T(8,128)(2,1)S(1)} %all-to-all-done.2.grad_ref, ...), custom_call_target="tpu_custom_call" | custom-call | flops 10000000000 | bytes 6000000 | tf_op jit(solution)/shard_map/backward/pallas_call | solution.py:234
  101.7 1.0 copy-done.1
  102.6 0.7 copy-done.3
  103.3 0.7 copy-done.5
  104.0 2.0 %collective-permute-start.2 = (bf16[8,128,128]{2,1,0:T(8,128)(2,1)}, bf16[8,128,128]{2,1,0:T(8,128)(2,1)S(1)}, u32[]{:S(2)}, u32[]{:S(2)}) collective-permute-start(bf16[8,128,128]{2,1,0:T(8,128)(2,1)} %get-tuple-element.15), channel_id=1, source_target_pairs={{1,0},{2,1},{3,2},{4,3},{5,4},{6,5},{7,6},{8,7},{9,8},{10,9},{11,1... | collective-permute-start | bytes 786440 | tf_op jit(solution)/shard_map/ppermute | solution.py:39
  106.1 6.5 %all-to-all-start.1 = ((bf16[8,512,128]{2,1,0:T(8,128)(2,1)}), bf16[8,512,128]{2,1,0:T(8,128)(2,1)S(1)}, u32[]{:S(2)}, u32[]{:S(2)}) async-start(bf16[8,512,128]{2,1,0:T(8,128)(2,1)} %get-tuple-element.11), calls=%async_computation.1 | async-start | bytes 2097152 | tf_op jit(solution)/shard_map/all_to_all | solution.py:267
  112.6 0.1 add_convert_fusion.1
  112.7 2.1 %collective-permute-start.3 = (bf16[8,128,128]{2,1,0:T(8,128)(2,1)S(1)}, bf16[8,128,128]{2,1,0:T(8,128)(2,1)S(1)}, u32[]{:S(2)}, u32[]{:S(2)}) collective-permute-start(bf16[8,128,128]{2,1,0:T(8,128)(2,1)S(1)} %add_convert_fusion.1), channel_id=1, source_target_pairs={{1,0},{2,1},{3,2},{4,3},{5,4},{6,5},{7,6},{8,7},{9,8},{10,9},{11,1... | collective-permute-start | bytes 786440 | tf_op jit(solution)/shard_map/ppermute | solution.py:39
  114.7 12.7 %collective-permute-done.3 = bf16[8,128,128]{2,1,0:T(8,128)(2,1)S(1)} collective-permute-done((bf16[8,128,128]{2,1,0:T(8,128)(2,1)S(1)}, bf16[8,128,128]{2,1,0:T(8,128)(2,1)S(1)}, u32[]{:S(2)}, u32[]{:S(2)}) %collective-permute-start.3) | collective-permute-done | bytes 262176 | tf_op jit(solution)/shard_map/ppermute | solution.py:39
  127.4 0.1 add_convert_fusion
  127.5 1.2 pad_maximum_fusion.1
  128.7 0.2 all-to-all-done.1
  128.8 7.0 %all-to-all-start.3 = ((bf16[8,640,128]{2,1,0:T(8,128)(2,1)}), bf16[8,640,128]{2,1,0:T(8,128)(2,1)S(1)}, u32[]{:S(2)}, u32[]{:S(2)}) async-start(bf16[8,640,128]{2,1,0:T(8,128)(2,1)} %pad_maximum_fusion.1), calls=%async_computation.3 | async-start | bytes 2621440 | tf_op jit(solution)/shard_map/all_to_all | solution.py:267
  135.9 1.3 copy_bitcast_fusion.2
  137.1 15.0 %all-to-all-done.3 = bf16[8,640,128]{2,1,0:T(8,128)(2,1)S(1)} async-done(((bf16[8,640,128]{2,1,0:T(8,128)(2,1)}), bf16[8,640,128]{2,1,0:T(8,128)(2,1)S(1)}, u32[]{:S(2)}, u32[]{:S(2)}) %all-to-all-start.3) | async-done | bytes 1310752 | tf_op jit(solution)/shard_map/all_to_all | solution.py:267
  152.1 0.7 copy.35
  152.9 0.7 copy.36
  153.6 1.3 copy_bitcast_fusion
  (38 shorter events, 0.2 us)
Async XLA Ops:
  0.6 1.2 copy-start
  0.6 1.4 copy-start.16
  0.7 1.4 copy-start.17
  3.3 6.2 %copy-start.19 = (s32[48]{0:T(128)S(1)}, s32[48]{0:T(128)}, u32[]{:S(2)}) copy-start(s32[48]{0:T(128)} %param.10) | copy-start | bytes 580
  3.3 6.5 %copy-start.18 = (s32[256]{0:T(256)S(1)}, s32[256]{0:T(256)}, u32[]{:S(2)}) copy-start(s32[256]{0:T(256)} %param.11) | copy-start | bytes 3076
  3.3 7.0 %copy-start.15 = (bf16[64,64,128]{2,1,0:T(8,128)(2,1)S(1)}, bf16[64,64,128]{2,1,0:T(8,128)(2,1)}, u32[]{:S(2)}) copy-start(bf16[64,64,128]{2,1,0:T(8,128)(2,1)} %param.9) | copy-start | bytes 3145732
  3.3 24.4 %all-to-all-start = ((bf16[8,640,128]{2,1,0:T(8,128)(2,1)}), bf16[8,640,128]{2,1,0:T(8,128)(2,1)S(1)}, u32[]{:S(2)}, u32[]{:S(2)}) async-start(bf16[8,640,128]{2,1,0:T(8,128)(2,1)} %pad_maximum_fusion), calls=%async_computation | async-start | bytes 2621440 | tf_op jit(solution)/shard_map/all_to_all | solution.py:267
  27.7 44.9 %all-to-all-start.2 = ((bf16[8,512,128]{2,1,0:T(8,128)(2,1)}), bf16[8,512,128]{2,1,0:T(8,128)(2,1)S(1)}, u32[]{:S(2)}, u32[]{:S(2)}) async-start(bf16[8,512,128]{2,1,0:T(8,128)(2,1)} %copy_bitcast_fusion.1), calls=%async_computation.2 | async-start | bytes 2097152 | tf_op jit(solution)/shard_map/all_to_all | solution.py:267
  32.2 16.2 %collective-permute-start = (bf16[8,128,128]{2,1,0:T(8,128)(2,1)S(1)}, bf16[8,128,128]{2,1,0:T(8,128)(2,1)S(1)}, u32[]{:S(2)}, u32[]{:S(2)}) collective-permute-start(bf16[8,128,128]{2,1,0:T(8,128)(2,1)S(1)} %slice.20.kv0_ref), channel_id=1, source_target_pairs={{0,1},{1,2},{2,3},{3,4},{4,5},{5,6},{6,7},{7,8},{8,9},{9,10},{10,1... | collective-permute-start | bytes 786440 | tf_op jit(solution)/shard_map/ppermute | solution.py:39
  48.5 7.7 %collective-permute-start.1 = (bf16[8,128,128]{2,1,0:T(8,128)(2,1)S(1)}, bf16[8,128,128]{2,1,0:T(8,128)(2,1)S(1)}, u32[]{:S(2)}, u32[]{:S(2)}) collective-permute-start(bf16[8,128,128]{2,1,0:T(8,128)(2,1)S(1)} %collective-permute-done.kv1_ref), channel_id=1, source_target_pairs={{0,1},{1,2},{2,3},{3,4},{4,5},{5,6},{6,7},{7,8},{8,9},{9,10},{10,1... | collective-permute-start | bytes 786440 | tf_op jit(solution)/shard_map/ppermute | solution.py:39
  69.4 0.7 copy-start.7
  70.2 0.7 copy-start.9
  70.9 0.7 copy-start.11
  71.6 1.0 copy-start.13
  72.6 1.0 copy-start.8
  73.6 0.9 copy-start.10
  74.5 0.9 copy-start.12
  75.5 1.2 copy-start.14
  101.7 1.0 copy-start.1
  102.6 0.7 copy-start.3
  103.3 0.7 copy-start.5
  104.0 8.5 %copy-start.6 = (bf16[8,128,128]{2,1,0:T(8,128)(2,1)S(1)}, bf16[8,128,128]{2,1,0:T(8,128)(2,1)}, u32[]{:S(2)}) copy-start(bf16[8,128,128]{2,1,0:T(8,128)(2,1)} %copy-done.5) | copy-start | bytes 786436
  104.0 8.5 %collective-permute-start.2 = (bf16[8,128,128]{2,1,0:T(8,128)(2,1)}, bf16[8,128,128]{2,1,0:T(8,128)(2,1)S(1)}, u32[]{:S(2)}, u32[]{:S(2)}) collective-permute-start(bf16[8,128,128]{2,1,0:T(8,128)(2,1)} %get-tuple-element.15), channel_id=1, source_target_pairs={{1,0},{2,1},{3,2},{4,3},{5,4},{6,5},{7,6},{8,7},{9,8},{10,9},{11,1... | collective-permute-start | bytes 786440 | tf_op jit(solution)/shard_map/ppermute | solution.py:39
  106.1 21.3 %copy-start.4 = (bf16[8,128,128]{2,1,0:T(8,128)(2,1)S(1)}, bf16[8,128,128]{2,1,0:T(8,128)(2,1)}, u32[]{:S(2)}) copy-start(bf16[8,128,128]{2,1,0:T(8,128)(2,1)} %copy-done.3) | copy-start | bytes 786436
  106.1 22.8 %all-to-all-start.1 = ((bf16[8,512,128]{2,1,0:T(8,128)(2,1)}), bf16[8,512,128]{2,1,0:T(8,128)(2,1)S(1)}, u32[]{:S(2)}, u32[]{:S(2)}) async-start(bf16[8,512,128]{2,1,0:T(8,128)(2,1)} %get-tuple-element.11), calls=%async_computation.1 | async-start | bytes 2097152 | tf_op jit(solution)/shard_map/all_to_all | solution.py:267
  112.6 14.9 %copy-start.2 = (bf16[8,512,128]{2,1,0:T(8,128)(2,1)S(1)}, bf16[8,512,128]{2,1,0:T(8,128)(2,1)}, u32[]{:S(2)}) copy-start(bf16[8,512,128]{2,1,0:T(8,128)(2,1)} %copy-done.1) | copy-start | bytes 3145732
  112.7 14.8 %collective-permute-start.3 = (bf16[8,128,128]{2,1,0:T(8,128)(2,1)S(1)}, bf16[8,128,128]{2,1,0:T(8,128)(2,1)S(1)}, u32[]{:S(2)}, u32[]{:S(2)}) collective-permute-start(bf16[8,128,128]{2,1,0:T(8,128)(2,1)S(1)} %add_convert_fusion.1), channel_id=1, source_target_pairs={{1,0},{2,1},{3,2},{4,3},{5,4},{6,5},{7,6},{8,7},{9,8},{10,9},{11,1... | collective-permute-start | bytes 786440 | tf_op jit(solution)/shard_map/ppermute | solution.py:39
  128.8 23.3 %all-to-all-start.3 = ((bf16[8,640,128]{2,1,0:T(8,128)(2,1)}), bf16[8,640,128]{2,1,0:T(8,128)(2,1)S(1)}, u32[]{:S(2)}, u32[]{:S(2)}) async-start(bf16[8,640,128]{2,1,0:T(8,128)(2,1)} %pad_maximum_fusion.1), calls=%async_computation.3 | async-start | bytes 2621440 | tf_op jit(solution)/shard_map/all_to_all | solution.py:267

commit v2 on v1

--- a/solution.py
+++ b/solution.py
@@ -199,7 +199,7 @@
 
 
 def params():
-    return pltpu.CompilerParams(dimension_semantics=("arbitrary",), vmem_limit_bytes=40 * 1024 * 1024)
+    return pltpu.CompilerParams(dimension_semantics=("arbitrary",), vmem_limit_bytes=60 * 1024 * 1024)
 
 
 def forward(scal, q_in, doc_rows, kv):
@@ -290,27 +290,31 @@
 
 def body(queries, keys, values, out_grad, doc_lengths, stored_block_order):
     scal, doc_rows = plan(doc_lengths, stored_block_order)
-    first_in = exchanged(jnp.concatenate([by_head(queries), by_head(keys), by_head(values)], axis=1))
-    kv0 = first_in[:, 512:, :]
+    kv0 = exchanged(jnp.concatenate([by_head(keys), by_head(values)], axis=1))
+    q_in = exchanged(by_head(queries))
     kv1 = passed_along(kv0, "ctx", 1)
     kv2 = passed_along(kv1, "ctx", 1)
-    grad_in = exchanged(by_head(out_grad))
+    grad_rows, kv2 = lax.optimization_barrier((by_head(out_grad), kv2))
+    grad_in = exchanged(grad_rows)
     kv = (kv0, kv1, kv2)
-    attended_loc, out_t, lse = forward(scal, first_in, doc_rows, kv)
+    attended_loc, out_t, lse = forward(scal, q_in, doc_rows, kv)
     attended_in = exchanged(attended_loc)
-    query_grad_loc, dkv0, dkv1, dkv2 = backward(scal, first_in, grad_in, out_t, lse, doc_rows, kv)
+    query_grad_loc, dkv0, dkv1, dkv2 = backward(scal, q_in, grad_in, out_t, lse, doc_rows, kv)
+    attended_in, dkv2, query_grad_loc = lax.optimization_barrier((attended_in, dkv2, query_grad_loc))
+    query_grad_in = exchanged(query_grad_loc)
     carried = passed_along(dkv2, "ctx", -1).astype(jnp.float32) + dkv1.astype(jnp.float32)
     carried = passed_along(carried.astype(jnp.bfloat16), "ctx", -1).astype(jnp.float32) + dkv0.astype(jnp.float32)
-    last_in = exchanged(jnp.concatenate([query_grad_loc, carried.astype(jnp.bfloat16)], axis=1))
+    carried, query_grad_in = lax.optimization_barrier((carried.astype(jnp.bfloat16), query_grad_in))
+    dkv_in = exchanged(carried)
     tokens = queries.shape[0]
 
     def by_token(block, heads):
         return block.reshape(8, tokens, heads, HEAD_SIZE).transpose(1, 0, 2, 3).reshape(tokens, -1, HEAD_SIZE)
 
     attended = by_token(attended_in, SHARE)
-    query_grad = by_token(last_in[:, :512], SHARE)
-    key_gradient = by_token(last_in[:, 512:576], 1)
-    value_gradient = by_token(last_in[:, 576:], 1)
+    query_grad = by_token(query_grad_in, SHARE)
+    key_gradient = by_token(dkv_in[:, :64], 1)
+    value_gradient = by_token(dkv_in[:, 64:], 1)
     return attended, query_grad, key_gradient, value_gradient
 
 

time: 155 us -> 146 us (0.942)
  the two profiles are of different devices: /device:TPU:418 before, /device:TPU:65 now
where the time goes in v2:
time: 146 us; the launch traced here: 145 us
  starting transfers between devices  53.8 us (37%)
  waiting for transfers between devices  50.5 us (35%)
  Pallas kernels  25.2 us (17%)
  local copies, waits for them, and re-layouts  10.5 us (7%)
  other arithmetic  4.02 us (3%)
    ppermute x4, waiting for transfers between devices, passed_along(): return lax.ppermute(block, axis, route)  35.2 us
    all_to_all x6, starting transfers between devices, exchanged(): lax.all_to_all(block, 'head', split_axis=0, concat_axis=0, tiled=True)  35 us
    ppermute x4, starting transfers between devices, passed_along(): return lax.ppermute(block, axis, route)  18.8 us
    pallas_call x1, Pallas kernels, backward(): pl.pallas_call(backward_kernel, grid_spec=pltpu.PrefetchScalarGridSpec(nu...  16 us
    all_to_all x6, waiting for transfers between devices, exchanged(): lax.all_to_all(block, 'head', split_axis=0, concat_axis=0, tiled=True)  15.4 us
    pallas_call x1, Pallas kernels, forward(): pl.pallas_call(forward_kernel, grid_spec=pltpu.PrefetchScalarGridSpec(num...  9.24 us
    unnamed x24, local copies, waits for them, and re-layouts  3.84 us
    reshape x3, local copies, waits for them, and re-layouts, by_head(): return split.reshape(8, -1, HEAD_SIZE)  3.44 us
  transfers between devices with their start and end apart: 10, of which 7 were waited for; matrix products, arithmetic and copies ran while one was open for 6% of the time, Pallas kernels for 17%

profile of v2, /device:TPU:65, one launch (start us, length us, event | category | flops | bytes accessed | tf_op | source)
XLA Modules:
  0.0 144.8 jit_solution(5243808646605311701)
XLA Ops:
  0.6 0.0 copy-start
  0.6 1.1 copy_bitcast_fusion.4
  1.8 0.7 pad_maximum_fusion
  2.5 6.7 %all-to-all-start.1 = ((bf16[8,128,128]{2,1,0:T(8,128)(2,1)}), bf16[8,128,128]{2,1,0:T(8,128)(2,1)S(1)}, u32[]{:S(2)}, u32[]{:S(2)}) async-start(bf16[8,128,128]{2,1,0:T(8,128)(2,1)} %pad_maximum_fusion), calls=%async_computation.1 | async-start | bytes 524288 | tf_op jit(solution)/shard_map/all_to_all | solution.py:267
  9.1 0.0 copy-start.8
  9.2 0.6 copy-done.8
  9.8 0.1 copy.28
  9.9 0.1 reduce-window.9
  10.0 0.1 reduce.1
  10.1 1.2 copy_bitcast_fusion.3
  11.3 5.4 %all-to-all-done.1.kv0_ref = bf16[8,128,128]{2,1,0:T(8,128)(2,1)S(1)} async-done(((bf16[8,128,128]{2,1,0:T(8,128)(2,1)}), bf16[8,128,128]{2,1,0:T(8,128)(2,1)S(1)}, u32[]{:S(2)}, u32[]{:S(2)}) %all-to-all-start.1) | async-done | bytes 262176 | tf_op jit(solution)/shard_map/all_to_all | solution.py:267
  16.7 3.6 %all-to-all-start = ((bf16[8,512,128]{2,1,0:T(8,128)(2,1)}), bf16[8,512,128]{2,1,0:T(8,128)(2,1)S(1)}, u32[]{:S(2)}, u32[]{:S(2)}) async-start(bf16[8,512,128]{2,1,0:T(8,128)(2,1)} %copy_bitcast_fusion.3), calls=%async_computation | async-start | bytes 2097152 | tf_op jit(solution)/shard_map/all_to_all | solution.py:267
  20.3 0.0 copy-done.7
  20.3 0.1 fusion.3
  20.4 0.1 fusion.7
  20.5 4.2 %collective-permute-start = (bf16[8,128,128]{2,1,0:T(8,128)(2,1)S(1)}, bf16[8,128,128]{2,1,0:T(8,128)(2,1)S(1)}, u32[]{:S(2)}, u32[]{:S(2)}) collective-permute-start(bf16[8,128,128]{2,1,0:T(8,128)(2,1)S(1)} %all-to-all-done.1.kv0_ref), channel_id=1, source_target_pairs={{0,1},{1,2},{2,3},{3,4},{4,5},{5,6},{6,7},{7,8},{8,9},{9,10},{10,1... | collective-permute-start | bytes 786440 | tf_op jit(solution)/shard_map/ppermute | solution.py:39
  24.7 0.1 select_add_fusion
  24.7 0.2 select_reduce_fusion
  25.0 10.0 %collective-permute-done.kv1_ref = bf16[8,128,128]{2,1,0:T(8,128)(2,1)S(1)} collective-permute-done((bf16[8,128,128]{2,1,0:T(8,128)(2,1)S(1)}, bf16[8,128,128]{2,1,0:T(8,128)(2,1)S(1)}, u32[]{:S(2)}, u32[]{:S(2)}) %collective-permute-start) | collective-permute-done | bytes 262176 | tf_op jit(solution)/shard_map/ppermute | solution.py:39
  35.0 4.4 %collective-permute-start.1 = (bf16[8,128,128]{2,1,0:T(8,128)(2,1)S(1)}, bf16[8,128,128]{2,1,0:T(8,128)(2,1)S(1)}, u32[]{:S(2)}, u32[]{:S(2)}) collective-permute-start(bf16[8,128,128]{2,1,0:T(8,128)(2,1)S(1)} %collective-permute-done.kv1_ref), channel_id=1, source_target_pairs={{0,1},{1,2},{2,3},{3,4},{4,5},{5,6},{6,7},{7,8},{8,9},{9,10},{10,1... | collective-permute-start | bytes 786440 | tf_op jit(solution)/shard_map/ppermute | solution.py:39
  39.4 1.2 copy_bitcast_fusion.2
  40.6 2.1 %collective-permute-done.1.kv2_ref = bf16[8,128,128]{2,1,0:T(8,128)(2,1)S(1)} collective-permute-done((bf16[8,128,128]{2,1,0:T(8,128)(2,1)S(1)}, bf16[8,128,128]{2,1,0:T(8,128)(2,1)S(1)}, u32[]{:S(2)}, u32[]{:S(2)}) %collective-permute-start.1) | collective-permute-done | bytes 262176 | tf_op jit(solution)/shard_map/ppermute | solution.py:39
  42.7 0.0 all-to-all-done.q_ref
  42.7 0.7 copy-done.10
  43.4 6.6 %all-to-all-start.3 = ((bf16[8,512,128]{2,1,0:T(8,128)(2,1)}), bf16[8,512,128]{2,1,0:T(8,128)(2,1)S(1)}, u32[]{:S(2)}, u32[]{:S(2)}) async-start(bf16[8,512,128]{2,1,0:T(8,128)(2,1)} %copy_bitcast_fusion.2), calls=%async_computation.3 | async-start | bytes 2097152 | tf_op jit(solution)/shard_map/all_to_all | solution.py:267
  50.0 0.6 sub.41.doc_ref
  50.6 0.2 select_reduce_fusion.1
  50.8 0.6 pad_add_fusion.scal_ref
  51.5 9.2 %forward.1 = (bf16[8,512,128]{2,1,0:T(8,128)(2,1)}, bf16[4,128,1024]{2,1,0:T(8,128)(2,1)}, f32[4,1,1024]{2,1,0:T(1,128)}) custom-call(s32[20]{0:T(128)} %pad_add_fusion.scal_ref, bf16[8,512,128]{2,1,0:T(8,128)(2,1)} %copy-done.2, s32[4,1,1024]{2,1,0:T(1,128)} %sub.41.doc_ref, bf16[8,128,128]{2,1,0:T(8,128)(2,1)} %copy-done.6, ...), custom_call_target="tpu_custom_call" | custom-call | flops 4000000000 | bytes 4000000 | tf_op jit(solution)/shard_map/forward/pallas_call | solution.py:206
  60.7 3.6 %all-to-all-done.3.grad_ref = bf16[8,512,128]{2,1,0:T(8,128)(2,1)S(1)} async-done(((bf16[8,512,128]{2,1,0:T(8,128)(2,1)}), bf16[8,512,128]{2,1,0:T(8,128)(2,1)S(1)}, u32[]{:S(2)}, u32[]{:S(2)}) %all-to-all-start.3) | async-done | bytes 1048608 | tf_op jit(solution)/shard_map/all_to_all | solution.py:267
  64.3 1.0 copy-done.3
  65.3 4.0 %all-to-all-start.2 = ((bf16[8,512,128]{2,1,0:T(8,128)(2,1)}), bf16[8,512,128]{2,1,0:T(8,128)(2,1)S(1)}, u32[]{:S(2)}, u32[]{:S(2)}) async-start(bf16[8,512,128]{2,1,0:T(8,128)(2,1)} %get-tuple-element.19), calls=%async_computation.2 | async-start | bytes 2097152 | tf_op jit(solution)/shard_map/all_to_all | solution.py:267
  69.3 16.0 %backward.1 = (bf16[8,512,128]{2,1,0:T(8,128)(2,1)}, bf16[8,128,128]{2,1,0:T(8,128)(2,1)}, bf16[8,128,128]{2,1,0:T(8,128)(2,1)}, bf16[8,128,128]{2,1,0:T(8,128)(2,1)}) custom-call(s32[20]{0:T(128)} %pad_add_fusion.scal_ref, bf16[8,512,128]{2,1,0:T(8,128)(2,1)} %copy-done.2, bf16[8,512,128]{2,1,0:T(8,128)(2,1)} %copy-done.3, ...), custom_call_target="tpu_custom_call" | custom-call | flops 10000000000 | bytes 6000000 | tf_op jit(solution)/shard_map/backward/pallas_call | solution.py:234
  85.3 0.0 all-to-all-done.2
  85.3 8.1 %collective-permute-start.2 = (bf16[8,128,128]{2,1,0:T(8,128)(2,1)}, bf16[8,128,128]{2,1,0:T(8,128)(2,1)}, u32[]{:S(2)}, u32[]{:S(2)}) collective-permute-start(bf16[8,128,128]{2,1,0:T(8,128)(2,1)} %get-tuple-element.26), channel_id=1, source_target_pairs={{1,0},{2,1},{3,2},{4,3},{5,4},{6,5},{7,6},{8,7},{9,8},{10,9},{11,1... | collective-permute-start | bytes 786440 | tf_op jit(solution)/shard_map/ppermute | solution.py:39
  93.4 6.9 %all-to-all-start.4 = ((bf16[8,512,128]{2,1,0:T(8,128)(2,1)}), bf16[8,512,128]{2,1,0:T(8,128)(2,1)S(1)}, u32[]{:S(2)}, u32[]{:S(2)}) async-start(bf16[8,512,128]{2,1,0:T(8,128)(2,1)} %get-tuple-element.29), calls=%async_computation.4 | async-start | bytes 2097152 | tf_op jit(solution)/shard_map/all_to_all | solution.py:267
  100.4 9.4 %collective-permute-done.2 = bf16[8,128,128]{2,1,0:T(8,128)(2,1)} collective-permute-done((bf16[8,128,128]{2,1,0:T(8,128)(2,1)}, bf16[8,128,128]{2,1,0:T(8,128)(2,1)}, u32[]{:S(2)}, u32[]{:S(2)}) %collective-permute-start.2) | collective-permute-done | bytes 262176 | tf_op jit(solution)/shard_map/ppermute | solution.py:39
  109.8 1.0 add_convert_fusion.1
  110.8 2.1 %collective-permute-start.3 = (bf16[8,128,128]{2,1,0:T(8,128)(2,1)S(1)}, bf16[8,128,128]{2,1,0:T(8,128)(2,1)S(1)}, u32[]{:S(2)}, u32[]{:S(2)}) collective-permute-start(bf16[8,128,128]{2,1,0:T(8,128)(2,1)S(1)} %add_convert_fusion.1), channel_id=1, source_target_pairs={{1,0},{2,1},{3,2},{4,3},{5,4},{6,5},{7,6},{8,7},{9,8},{10,9},{11,1... | collective-permute-start | bytes 786440 | tf_op jit(solution)/shard_map/ppermute | solution.py:39
  112.9 1.3 copy_bitcast_fusion.1
  114.1 13.6 %collective-permute-done.3 = bf16[8,128,128]{2,1,0:T(8,128)(2,1)S(1)} collective-permute-done((bf16[8,128,128]{2,1,0:T(8,128)(2,1)S(1)}, bf16[8,128,128]{2,1,0:T(8,128)(2,1)S(1)}, u32[]{:S(2)}, u32[]{:S(2)}) %collective-permute-start.3) | collective-permute-done | bytes 262176 | tf_op jit(solution)/shard_map/ppermute | solution.py:39
  127.8 0.8 add_convert_fusion
  128.5 0.0 all-to-all-done.4
  128.5 7.2 %all-to-all-start.5 = ((bf16[8,128,128]{2,1,0:T(8,128)(2,1)}), bf16[8,128,128]{2,1,0:T(8,128)(2,1)S(1)}, u32[]{:S(2)}, u32[]{:S(2)}) async-start(bf16[8,128,128]{2,1,0:T(8,128)(2,1)} %add_convert_fusion), calls=%async_computation.5 | async-start | bytes 524288 | tf_op jit(solution)/shard_map/all_to_all | solution.py:267
  135.7 1.3 copy_bitcast_fusion
  137.0 6.3 %all-to-all-done.5 = bf16[8,128,128]{2,1,0:T(8,128)(2,1)S(1)} async-done(((bf16[8,128,128]{2,1,0:T(8,128)(2,1)}), bf16[8,128,128]{2,1,0:T(8,128)(2,1)S(1)}, u32[]{:S(2)}, u32[]{:S(2)}) %all-to-all-start.5) | async-done | bytes 262176 | tf_op jit(solution)/shard_map/all_to_all | solution.py:267
  143.3 0.7 copy.35
  144.1 0.7 copy.36
  (22 shorter events, 0.1 us)
Async XLA Ops:
  0.6 9.5 %copy-start = (bf16[64,64,128]{2,1,0:T(8,128)(2,1)S(1)}, bf16[64,64,128]{2,1,0:T(8,128)(2,1)}, u32[]{:S(2)}) copy-start(bf16[64,64,128]{2,1,0:T(8,128)(2,1)} %param.6) | copy-start | bytes 3145732
  2.5 14.2 %all-to-all-start.1 = ((bf16[8,128,128]{2,1,0:T(8,128)(2,1)}), bf16[8,128,128]{2,1,0:T(8,128)(2,1)S(1)}, u32[]{:S(2)}, u32[]{:S(2)}) async-start(bf16[8,128,128]{2,1,0:T(8,128)(2,1)} %pad_maximum_fusion), calls=%async_computation.1 | async-start | bytes 524288 | tf_op jit(solution)/shard_map/all_to_all | solution.py:267
  9.1 0.7 copy-start.8
  11.3 9.0 %copy-start.7 = (s32[256]{0:T(256)S(1)}, s32[256]{0:T(256)}, u32[]{:S(2)}) copy-start(s32[256]{0:T(256)} %param.11) | copy-start | bytes 3076
  11.3 28.1 %copy-start.1 = (bf16[64,64,128]{2,1,0:T(8,128)(2,1)S(1)}, bf16[64,64,128]{2,1,0:T(8,128)(2,1)}, u32[]{:S(2)}) copy-start(bf16[64,64,128]{2,1,0:T(8,128)(2,1)} %param.9) | copy-start | bytes 3145732
  16.7 3.8 %copy-start.6 = (bf16[8,128,128]{2,1,0:T(8,128)(2,1)}, bf16[8,128,128]{2,1,0:T(8,128)(2,1)S(1)}, u32[]{:S(2)}) copy-start(bf16[8,128,128]{2,1,0:T(8,128)(2,1)S(1)} %all-to-all-done.1.kv0_ref) | copy-start | bytes 786436
  16.7 26.0 %all-to-all-start = ((bf16[8,512,128]{2,1,0:T(8,128)(2,1)}), bf16[8,512,128]{2,1,0:T(8,128)(2,1)S(1)}, u32[]{:S(2)}, u32[]{:S(2)}) async-start(bf16[8,512,128]{2,1,0:T(8,128)(2,1)} %copy_bitcast_fusion.3), calls=%async_computation | async-start | bytes 2097152 | tf_op jit(solution)/shard_map/all_to_all | solution.py:267
  20.5 14.5 %collective-permute-start = (bf16[8,128,128]{2,1,0:T(8,128)(2,1)S(1)}, bf16[8,128,128]{2,1,0:T(8,128)(2,1)S(1)}, u32[]{:S(2)}, u32[]{:S(2)}) collective-permute-start(bf16[8,128,128]{2,1,0:T(8,128)(2,1)S(1)} %all-to-all-done.1.kv0_ref), channel_id=1, source_target_pairs={{0,1},{1,2},{2,3},{3,4},{4,5},{5,6},{6,7},{7,8},{8,9},{9,10},{10,1... | collective-permute-start | bytes 786440 | tf_op jit(solution)/shard_map/ppermute | solution.py:39
  35.0 5.6 %copy-start.9 = (bf16[8,128,128]{2,1,0:T(8,128)(2,1)}, bf16[8,128,128]{2,1,0:T(8,128)(2,1)S(1)}, u32[]{:S(2)}) copy-start(bf16[8,128,128]{2,1,0:T(8,128)(2,1)S(1)} %collective-permute-done.kv1_ref) | copy-start | bytes 786436
  35.0 7.7 %collective-permute-start.1 = (bf16[8,128,128]{2,1,0:T(8,128)(2,1)S(1)}, bf16[8,128,128]{2,1,0:T(8,128)(2,1)S(1)}, u32[]{:S(2)}, u32[]{:S(2)}) collective-permute-start(bf16[8,128,128]{2,1,0:T(8,128)(2,1)S(1)} %collective-permute-done.kv1_ref), channel_id=1, source_target_pairs={{0,1},{1,2},{2,3},{3,4},{4,5},{5,6},{6,7},{7,8},{8,9},{9,10},{10,1... | collective-permute-start | bytes 786440 | tf_op jit(solution)/shard_map/ppermute | solution.py:39
  42.7 0.7 copy-start.10
  42.7 7.3 %copy-start.2 = (bf16[8,512,128]{2,1,0:T(8,128)(2,1)}, bf16[8,512,128]{2,1,0:T(8,128)(2,1)S(1)}, u32[]{:S(2)}) copy-start(bf16[8,512,128]{2,1,0:T(8,128)(2,1)S(1)} %all-to-all-done.q_ref) | copy-start | bytes 3145732
  43.4 21.0 %all-to-all-start.3 = ((bf16[8,512,128]{2,1,0:T(8,128)(2,1)}), bf16[8,512,128]{2,1,0:T(8,128)(2,1)S(1)}, u32[]{:S(2)}, u32[]{:S(2)}) async-start(bf16[8,512,128]{2,1,0:T(8,128)(2,1)} %copy_bitcast_fusion.2), calls=%async_computation.3 | async-start | bytes 2097152 | tf_op jit(solution)/shard_map/all_to_all | solution.py:267
  64.3 1.0 copy-start.3
  65.3 20.0 %all-to-all-start.2 = ((bf16[8,512,128]{2,1,0:T(8,128)(2,1)}), bf16[8,512,128]{2,1,0:T(8,128)(2,1)S(1)}, u32[]{:S(2)}, u32[]{:S(2)}) async-start(bf16[8,512,128]{2,1,0:T(8,128)(2,1)} %get-tuple-element.19), calls=%async_computation.2 | async-start | bytes 2097152 | tf_op jit(solution)/shard_map/all_to_all | solution.py:267
  85.3 24.5 %copy-start.5 = (bf16[8,128,128]{2,1,0:T(8,128)(2,1)S(1)}, bf16[8,128,128]{2,1,0:T(8,128)(2,1)}, u32[]{:S(2)}) copy-start(bf16[8,128,128]{2,1,0:T(8,128)(2,1)} %get-tuple-element.27) | copy-start | bytes 786436
  85.3 24.5 %collective-permute-start.2 = (bf16[8,128,128]{2,1,0:T(8,128)(2,1)}, bf16[8,128,128]{2,1,0:T(8,128)(2,1)}, u32[]{:S(2)}, u32[]{:S(2)}) collective-permute-start(bf16[8,128,128]{2,1,0:T(8,128)(2,1)} %get-tuple-element.26), channel_id=1, source_target_pairs={{1,0},{2,1},{3,2},{4,3},{5,4},{6,5},{7,6},{8,7},{9,8},{10,9},{11,1... | collective-permute-start | bytes 786440 | tf_op jit(solution)/shard_map/ppermute | solution.py:39
  93.4 35.1 %all-to-all-start.4 = ((bf16[8,512,128]{2,1,0:T(8,128)(2,1)}), bf16[8,512,128]{2,1,0:T(8,128)(2,1)S(1)}, u32[]{:S(2)}, u32[]{:S(2)}) async-start(bf16[8,512,128]{2,1,0:T(8,128)(2,1)} %get-tuple-element.29), calls=%async_computation.4 | async-start | bytes 2097152 | tf_op jit(solution)/shard_map/all_to_all | solution.py:267
  110.8 17.0 %copy-start.4 = (bf16[8,128,128]{2,1,0:T(8,128)(2,1)S(1)}, bf16[8,128,128]{2,1,0:T(8,128)(2,1)}, u32[]{:S(2)}) copy-start(bf16[8,128,128]{2,1,0:T(8,128)(2,1)} %get-tuple-element.28) | copy-start | bytes 786436
  110.8 17.0 %collective-permute-start.3 = (bf16[8,128,128]{2,1,0:T(8,128)(2,1)S(1)}, bf16[8,128,128]{2,1,0:T(8,128)(2,1)S(1)}, u32[]{:S(2)}, u32[]{:S(2)}) collective-permute-start(bf16[8,128,128]{2,1,0:T(8,128)(2,1)S(1)} %add_convert_fusion.1), channel_id=1, source_target_pairs={{1,0},{2,1},{3,2},{4,3},{5,4},{6,5},{7,6},{8,7},{9,8},{10,9},{11,1... | collective-permute-start | bytes 786440 | tf_op jit(solution)/shard_map/ppermute | solution.py:39
  128.5 14.8 %all-to-all-start.5 = ((bf16[8,128,128]{2,1,0:T(8,128)(2,1)}), bf16[8,128,128]{2,1,0:T(8,128)(2,1)S(1)}, u32[]{:S(2)}, u32[]{:S(2)}) async-start(bf16[8,128,128]{2,1,0:T(8,128)(2,1)} %add_convert_fusion), calls=%async_computation.5 | async-start | bytes 524288 | tf_op jit(solution)/shard_map/all_to_all | solution.py:267

commit v3 on v1

--- a/solution.py
+++ b/solution.py
@@ -19,7 +19,7 @@
 REACH = 10 * BLOCK
 SHARE = 8
 ROWS = BLOCK * SHARE
-TILE = 256
+TILE = ROWS // 2
 
 SCALE = HEAD_SIZE ** (-0.5)
 EXP2_SCALE = SCALE * math.log2(math.e)
@@ -27,6 +27,7 @@
 
 NT = (((1,), (1,)), ((), ()))
 NN = (((1,), (0,)), ((), ()))
+TN = (((0,), (0,)), ((), ()))
 
 
 def dot(a, b, dims=NN):
@@ -50,14 +51,34 @@
     return pl.multiple_of(scal_ref[index] * BLOCK, BLOCK)
 
 
-def allowed_tile(key_start, doc_start, query_pos):
-    key_pos = key_start + lax.broadcasted_iota(jnp.int32, (CHUNK, TILE), 0)
-    return (key_pos >= doc_start) & (key_pos <= query_pos)
-
-
-def row_positions(first_block, tile):
+def allowed_tile(key_start, first_block, doc_start, tile):
     lane = lax.broadcasted_iota(jnp.int32, (1, TILE), 1) + tile * TILE
-    return first_block * BLOCK + lax.shift_right_logical(lane, 3)
+    query_pos = first_block * BLOCK + lax.shift_right_logical(lane, 3)
+    key_pos = lax.broadcasted_iota(jnp.int32, (CHUNK, TILE), 0)
+    return (key_pos >= doc_start - key_start) & (key_pos <= query_pos - key_start)
+
+
+def each_chunk(scal_ref, step, work):
+    first_block = scal_ref[WINDOW_BLOCKS + step]
+    low_block = scal_ref[WINDOW_BLOCKS + CELL_BLOCKS + step]
+    last_start = scal_ref[WINDOW_BLOCKS + 2 * CELL_BLOCKS + step]
+    chunks = lax.shift_right_logical(first_block - low_block + 2, 1)
+
+    def turn_work(turn, _):
+        key_start = pl.multiple_of((low_block + 2 * turn) * BLOCK, BLOCK)
+        whole = (key_start >= last_start) & (key_start + CHUNK <= first_block * BLOCK)
+
+        @pl.when(whole)
+        def _():
+            work(turn, key_start, first_block, False)
+
+        @pl.when(jnp.logical_not(whole))
+        def _():
+            work(turn, key_start, first_block, True)
+
+        return 0
+
+    lax.fori_loop(0, chunks, turn_work, 0)
 
 
 def forward_kernel(scal_ref, q_ref, doc_ref, kv0_ref, kv1_ref, kv2_ref, out_ref, out_t_ref, lse_ref, key_seq, value_t, scores, acc, top):
@@ -74,42 +95,39 @@
         key_seq[pl.ds(WINDOW, BLOCK), :] = jnp.zeros((BLOCK, HEAD_SIZE), jnp.bfloat16)
         value_t[:, pl.ds(WINDOW, BLOCK)] = jnp.zeros((HEAD_SIZE, BLOCK), jnp.bfloat16)
 
+    top[...] = jnp.full_like(top, NEG_BIG)
+    acc[...] = jnp.zeros_like(acc)
+
+    def score_chunk(turn, key_start, first_block, masked):
+        keys = key_seq[pl.ds(key_start, CHUNK), :]
+        rows = pl.ds(pl.multiple_of(turn * CHUNK, CHUNK), CHUNK)
+        for tile in range(2):
+            cols = slice(tile * TILE, (tile + 1) * TILE)
+            raw = dot(keys, q_ref[tile], NT)
+            if masked:
+                raw = jnp.where(allowed_tile(key_start, first_block, doc_ref[0, :, cols], tile), raw, NEG_BIG)
+            scores[rows, cols] = raw
+            part = jnp.max(raw.reshape(CHUNK // 8, 8, TILE), axis=0)
+            top[:, cols] = jnp.maximum(top[:, cols], part)
+
+    each_chunk(scal_ref, step, score_chunk)
+    highest = jnp.max(top[...], axis=0, keepdims=True) * EXP2_SCALE
+    top[...] = jnp.zeros_like(top)
     first_block = scal_ref[WINDOW_BLOCKS + step]
     low_block = scal_ref[WINDOW_BLOCKS + CELL_BLOCKS + step]
-    chunks = lax.shift_right_logical(first_block - low_block + 2, 1)
-    top[...] = jnp.full_like(top, NEG_BIG)
-    acc[...] = jnp.zeros_like(acc)
-
-    def score_chunk(turn, _):
-        key_start = pl.multiple_of((low_block + 2 * turn) * BLOCK, BLOCK)
-        keys = key_seq[pl.ds(key_start, CHUNK), :]
-        for tile in range(ROWS // TILE):
-            cols = pl.ds(tile * TILE, TILE)
-            queries = q_ref[tile // 2, pl.ds((tile % 2) * TILE, TILE), :]
-            raw = dot(keys, queries, NT)
-            allowed = allowed_tile(key_start, doc_ref[0, :, cols], row_positions(first_block, tile))
-            raw = jnp.where(allowed, raw, NEG_BIG)
-            scores[pl.ds(pl.multiple_of(turn * CHUNK, CHUNK), CHUNK), cols] = raw
-            part = jnp.max(raw.reshape(CHUNK // 8, 8, TILE), axis=0)
-            top[:, cols] = jnp.maximum(top[:, cols], part)
-        return 0
-
-    lax.fori_loop(0, chunks, score_chunk, 0)
-    highest = jnp.max(top[...], axis=0, keepdims=True) * EXP2_SCALE
-    top[...] = jnp.zeros_like(top)
 
     def value_chunk(turn, _):
         key_start = pl.multiple_of((low_block + 2 * turn) * BLOCK, BLOCK)
+        rows = pl.ds(pl.multiple_of(turn * CHUNK, CHUNK), CHUNK)
         values = value_t[:, pl.ds(key_start, CHUNK)]
-        for tile in range(ROWS // TILE):
-            cols = pl.ds(tile * TILE, TILE)
-            raw = scores[pl.ds(pl.multiple_of(turn * CHUNK, CHUNK), CHUNK), cols]
-            weights = jnp.exp2(raw * EXP2_SCALE - highest[:, tile * TILE : (tile + 1) * TILE])
+        for tile in range(2):
+            cols = slice(tile * TILE, (tile + 1) * TILE)
+            weights = jnp.exp2(scores[rows, cols] * EXP2_SCALE - highest[:, cols])
             top[:, cols] += jnp.sum(weights.reshape(CHUNK // 8, 8, TILE), axis=0)
             acc[:, cols] += dot(values, weights.astype(jnp.bfloat16))
         return 0
 
-    lax.fori_loop(0, chunks, value_chunk, 0)
+    lax.fori_loop(0, lax.shift_right_logical(first_block - low_block + 2, 1), value_chunk, 0)
     total = jnp.sum(top[...], axis=0, keepdims=True)
     lse_ref[0] = highest + jnp.log2(total)
     out_t = acc[...] * (1.0 / total)
@@ -119,7 +137,7 @@
     out_ref[1] = out[ROWS // 2 :]
 
 
-def backward_kernel(scal_ref, q_ref, grad_ref, out_t_ref, lse_ref, doc_ref, kv0_ref, kv1_ref, kv2_ref, dq_ref, dkv0_ref, dkv1_ref, dkv2_ref, key_seq, value_seq, key_t, dk_acc, dv_acc, dq_t, weights_low, grads_low, delta):
+def backward_kernel(scal_ref, q_ref, grad_ref, out_t_ref, lse_ref, doc_ref, kv0_ref, kv1_ref, kv2_ref, dq_ref, dkv0_ref, dkv1_ref, dkv2_ref, key_seq, value_seq, dk_acc, dv_acc, dq_acc, weights_low, grads_low, delta):
     step = pl.program_id(0)
 
     @pl.when(step == 0)
@@ -127,51 +145,43 @@
         for slot, kv_ref in enumerate((kv0_ref, kv1_ref, kv2_ref)):
             for block in range(CELL_BLOCKS):
                 start = window_start(scal_ref, slot, block)
-                key = stored_rows(kv_ref, block, 0)
-                key_seq[pl.ds(start, BLOCK), :] = key
-                key_t[:, pl.ds(start, BLOCK)] = key.astype(jnp.float32).T.astype(jnp.bfloat16)
+                key_seq[pl.ds(start, BLOCK), :] = stored_rows(kv_ref, block, 0)
                 value_seq[pl.ds(start, BLOCK), :] = stored_rows(kv_ref, block, 1)
         zeros = jnp.zeros((BLOCK, HEAD_SIZE), jnp.bfloat16)
         key_seq[pl.ds(WINDOW, BLOCK), :] = zeros
         value_seq[pl.ds(WINDOW, BLOCK), :] = zeros
-        key_t[:, pl.ds(WINDOW, BLOCK)] = zeros
         dk_acc[...] = jnp.zeros_like(dk_acc)
         dv_acc[...] = jnp.zeros_like(dv_acc)
 
-    first_block = scal_ref[WINDOW_BLOCKS + step]
-    low_block = scal_ref[WINDOW_BLOCKS + CELL_BLOCKS + step]
-    chunks = lax.shift_right_logical(first_block - low_block + 2, 1)
-    dq_t[...] = jnp.zeros_like(dq_t)
+    dq_acc[...] = jnp.zeros_like(dq_acc)
     for half in range(2):
-        cols = slice(half * ROWS // 2, (half + 1) * ROWS // 2)
+        cols = slice(half * TILE, (half + 1) * TILE)
         grad_t = grad_ref[half].astype(jnp.float32).T
         delta[:, cols] = jnp.sum(grad_t * out_t_ref[0, :, cols].astype(jnp.float32), axis=0, keepdims=True)
 
-    def chunk(turn, _):
-        key_start = pl.multiple_of((low_block + 2 * turn) * BLOCK, BLOCK)
+    def chunk(turn, key_start, first_block, masked):
         keys = key_seq[pl.ds(key_start, CHUNK), :]
         values = value_seq[pl.ds(key_start, CHUNK), :]
-        for tile in range(ROWS // TILE):
-            cols = pl.ds(tile * TILE, TILE)
-            half, rows = tile // 2, pl.ds((tile % 2) * TILE, TILE)
-            raw = dot(keys, q_ref[half, rows, :], NT)
-            allowed = allowed_tile(key_start, doc_ref[0, :, cols], row_positions(first_block, tile))
-            weights = jnp.exp2(jnp.where(allowed, raw * EXP2_SCALE - lse_ref[0, :, cols], NEG_BIG))
+        for tile in range(2):
+            cols = slice(tile * TILE, (tile + 1) * TILE)
+            raw = dot(keys, q_ref[tile], NT)
+            scaled = raw * EXP2_SCALE - lse_ref[0, :, cols]
+            if masked:
+                scaled = jnp.where(allowed_tile(key_start, first_block, doc_ref[0, :, cols], tile), scaled, NEG_BIG)
+            weights = jnp.exp2(scaled)
             weights_low[:, cols] = weights.astype(jnp.bfloat16)
-            sent = dot(values, grad_ref[half, rows, :], NT)
-            grads = (weights * (sent - delta[:, cols])).astype(jnp.bfloat16)
-            grads_low[:, cols] = grads
-            dq_t[:, cols] += dot(key_t[:, pl.ds(key_start, CHUNK)], grads)
+            sent = dot(values, grad_ref[tile], NT)
+            grads_low[:, cols] = (weights * (sent - delta[:, cols])).astype(jnp.bfloat16)
         queries = jnp.concatenate([q_ref[0], q_ref[1]], axis=0)
         out_grads = jnp.concatenate([grad_ref[0], grad_ref[1]], axis=0)
+        dq_acc[...] += dot(grads_low[...], keys, TN)
         dk_acc[pl.ds(key_start, CHUNK), :] += dot(grads_low[...], queries)
         dv_acc[pl.ds(key_start, CHUNK), :] += dot(weights_low[...], out_grads)
-        return 0
-
-    lax.fori_loop(0, chunks, chunk, 0)
-    query_grad = (dq_t[...] * SCALE).T.astype(jnp.bfloat16)
-    dq_ref[0] = query_grad[: ROWS // 2]
-    dq_ref[1] = query_grad[ROWS // 2 :]
+
+    each_chunk(scal_ref, step, chunk)
+    query_grad = (dq_acc[...] * SCALE).astype(jnp.bfloat16)
+    dq_ref[0] = query_grad[:TILE]
+    dq_ref[1] = query_grad[TILE:]
 
     @pl.when(step == CELL_BLOCKS - 1)
     def _():
@@ -199,7 +209,7 @@
 
 
 def params():
-    return pltpu.CompilerParams(dimension_semantics=("arbitrary",), vmem_limit_bytes=40 * 1024 * 1024)
+    return pltpu.CompilerParams(dimension_semantics=("arbitrary",), vmem_limit_bytes=60 * 1024 * 1024)
 
 
 def forward(scal, q_in, doc_rows, kv):
@@ -241,16 +251,15 @@
             scratch_shapes=[
                 pltpu.VMEM((PADDED, HEAD_SIZE), jnp.bfloat16),
                 pltpu.VMEM((PADDED, HEAD_SIZE), jnp.bfloat16),
-                pltpu.VMEM((HEAD_SIZE, PADDED), jnp.bfloat16),
                 pltpu.VMEM((PADDED, HEAD_SIZE), jnp.float32),
                 pltpu.VMEM((PADDED, HEAD_SIZE), jnp.float32),
-                pltpu.VMEM((HEAD_SIZE, ROWS), jnp.float32),
+                pltpu.VMEM((ROWS, HEAD_SIZE), jnp.float32),
                 pltpu.VMEM((CHUNK, ROWS), jnp.bfloat16),
                 pltpu.VMEM((CHUNK, ROWS), jnp.bfloat16),
                 pltpu.VMEM((1, ROWS), jnp.float32),
             ],
         ),
-        out_shape=[jax.ShapeDtypeStruct((8, ROWS // 2, HEAD_SIZE), jnp.bfloat16), dkv_shape, dkv_shape, dkv_shape],
+        out_shape=[jax.ShapeDtypeStruct((8, ROWS // 2 + 128, HEAD_SIZE), jnp.bfloat16), dkv_shape, dkv_shape, dkv_shape],
         compiler_params=params(),
         cost_estimate=pl.CostEstimate(flops=10_000_000_000, bytes_accessed=6_000_000, transcendentals=4_000_000),
         name="backward",
@@ -282,9 +291,9 @@
     begun = starts <= pos[..., None]
     doc_start = jnp.max(jnp.where(begun, starts, 0), axis=-1)
     doc_rows = doc_start - window_first * BLOCK
-    low = jnp.max(jnp.where(starts <= own_block[:, None] * BLOCK, starts, 0), axis=-1)
-    low_block = low // BLOCK - window_first
-    scal = jnp.concatenate([place, own_place, low_block]).astype(jnp.int32)
+    edges = jnp.concatenate([own_block * BLOCK, own_block * BLOCK + BLOCK - 1])
+    low = jnp.max(jnp.where(starts <= edges[:, None], starts, 0), axis=-1) - window_first * BLOCK
+    scal = jnp.concatenate([place, own_place, low[:CELL_BLOCKS] // BLOCK, low[CELL_BLOCKS:]]).astype(jnp.int32)
     return scal, doc_rows.astype(jnp.int32)
 
 
@@ -292,16 +301,16 @@
     scal, doc_rows = plan(doc_lengths, stored_block_order)
     first_in = exchanged(jnp.concatenate([by_head(queries), by_head(keys), by_head(values)], axis=1))
     kv0 = first_in[:, 512:, :]
-    kv1 = passed_along(kv0, "ctx", 1)
-    kv2 = passed_along(kv1, "ctx", 1)
+    kv = (kv0, passed_along(kv0, "ctx", 1), passed_along(kv0, "ctx", 2))
     grad_in = exchanged(by_head(out_grad))
-    kv = (kv0, kv1, kv2)
     attended_loc, out_t, lse = forward(scal, first_in, doc_rows, kv)
     attended_in = exchanged(attended_loc)
-    query_grad_loc, dkv0, dkv1, dkv2 = backward(scal, first_in, grad_in, out_t, lse, doc_rows, kv)
-    carried = passed_along(dkv2, "ctx", -1).astype(jnp.float32) + dkv1.astype(jnp.float32)
-    carried = passed_along(carried.astype(jnp.bfloat16), "ctx", -1).astype(jnp.float32) + dkv0.astype(jnp.float32)
-    last_in = exchanged(jnp.concatenate([query_grad_loc, carried.astype(jnp.bfloat16)], axis=1))
+    last_loc, dkv0, dkv1, dkv2 = backward(scal, first_in, grad_in, out_t, lse, doc_rows, kv)
+    attended_in, dkv1, dkv2 = lax.optimization_barrier((attended_in, dkv1, dkv2))
+    near, far = passed_along(dkv1, "ctx", -1), passed_along(dkv2, "ctx", -2)
+    summed = dkv0.astype(jnp.float32) + near.astype(jnp.float32) + far.astype(jnp.float32)
+    last_loc = lax.dynamic_update_slice(last_loc, summed.astype(jnp.bfloat16), (0, 512, 0))
+    last_in = exchanged(last_loc)
     tokens = queries.shape[0]
 
     def by_token(block, heads):

time: 155 us -> 138 us (0.89)
  the two profiles are of different devices: /device:TPU:418 before, /device:TPU:121 now
where the time goes in v3:
time: 138 us
  starting transfers between devices  50.2 us (36%)
  waiting for transfers between devices  47.4 us (34%)
  Pallas kernels  26.7 us (19%)
  local copies, waits for them, and re-layouts  8.1 us (6%)
  other arithmetic  4.61 us (3%)
    all_to_all x4, waiting for transfers between devices, exchanged(): lax.all_to_all(block, 'head', split_axis=0, concat_axis=0, tiled=True)  30.6 us
    all_to_all x4, starting transfers between devices, exchanged(): lax.all_to_all(block, 'head', split_axis=0, concat_axis=0, tiled=True)  26.8 us
    ppermute x4, starting transfers between devices, passed_along(): return lax.ppermute(block, axis, route)  23.4 us
    ppermute x4, waiting for transfers between devices, passed_along(): return lax.ppermute(block, axis, route)  16.8 us
    pallas_call x1, Pallas kernels, backward(): pl.pallas_call(backward_kernel, grid_spec=pltpu.PrefetchScalarGridSpec(nu...  15.4 us
    pallas_call x1, Pallas kernels, forward(): pl.pallas_call(forward_kernel, grid_spec=pltpu.PrefetchScalarGridSpec(num...  11.3 us
    unnamed x24, local copies, waits for them, and re-layouts  3.43 us
  transfers between devices with their start and end apart: 8, of which 6 were waited for; matrix products, arithmetic and copies ran while one was open for 3% of the time, Pallas kernels for 19%

profile of v3, /device:TPU:121, one launch (start us, length us, event | category | flops | bytes accessed | tf_op | source)
XLA Modules:
  0.0 137.8 jit_solution(14928312296126623173)
XLA Ops:
  0.6 0.0 copy-start
  0.6 0.0 copy-start.5
  0.7 0.0 copy-start.6
  0.7 1.2 copy-done
  1.9 0.2 copy_bitcast_fusion.3
  2.1 0.0 copy-done.5
  2.1 1.2 pad_maximum_fusion
  3.3 6.7 %all-to-all-start = ((bf16[8,640,128]{2,1,0:T(8,128)(2,1)}), bf16[8,640,128]{2,1,0:T(8,128)(2,1)S(1)}, u32[]{:S(2)}, u32[]{:S(2)}) async-start(bf16[8,640,128]{2,1,0:T(8,128)(2,1)} %pad_maximum_fusion), calls=%async_computation | async-start | bytes 2621440 | tf_op jit(solution)/shard_map/all_to_all | solution.py:276
  10.0 0.1 copy.28
  10.1 0.1 reduce-window.9
  10.2 0.1 reduce.1
  10.3 0.0 copy-done.7
  10.3 0.1 fusion.4
  10.4 0.1 broadcast_add_fusion.1
  10.5 0.1 select_add_fusion
  10.6 0.2 select_reduce_fusion
  10.8 0.6 sub.51.doc_ref
  11.5 0.1 pad_add_fusion
  11.5 0.2 select_reduce_fusion.1
  11.7 1.2 copy_bitcast_fusion.2
  12.9 13.9 %all-to-all-done.q_ref = bf16[8,640,128]{2,1,0:T(8,128)(2,1)S(1)} async-done(((bf16[8,640,128]{2,1,0:T(8,128)(2,1)}), bf16[8,640,128]{2,1,0:T(8,128)(2,1)S(1)}, u32[]{:S(2)}, u32[]{:S(2)}) %all-to-all-start) | async-done | bytes 1310752 | tf_op jit(solution)/shard_map/all_to_all | solution.py:276
  26.8 6.2 %all-to-all-start.2 = ((bf16[8,512,128]{2,1,0:T(8,128)(2,1)}), bf16[8,512,128]{2,1,0:T(8,128)(2,1)S(1)}, u32[]{:S(2)}, u32[]{:S(2)}) async-start(bf16[8,512,128]{2,1,0:T(8,128)(2,1)} %copy_bitcast_fusion.2), calls=%async_computation.2 | async-start | bytes 2097152 | tf_op jit(solution)/shard_map/all_to_all | solution.py:276
  33.0 0.0 copy-done.1
  33.0 0.0 copy-start.4
  33.0 3.2 %collective-permute-start = (bf16[8,128,128]{2,1,0:T(8,128)(2,1)S(1)}, bf16[8,128,128]{2,1,0:T(8,128)(2,1)S(1)}, u32[]{:S(2)}, u32[]{:S(2)}) collective-permute-start(bf16[8,128,128]{2,1,0:T(8,128)(2,1)S(1)} %slice.28.kv0_ref), channel_id=1, source_target_pairs={{0,1},{1,2},{2,3},{3,4},{4,5},{5,6},{6,7},{7,8},{8,9},{9,10},{10,1... | collective-permute-start | bytes 786440 | tf_op jit(solution)/shard_map/ppermute | solution.py:40
  36.2 5.6 %collective-permute-start.1 = (bf16[8,128,128]{2,1,0:T(8,128)(2,1)S(1)}, bf16[8,128,128]{2,1,0:T(8,128)(2,1)S(1)}, u32[]{:S(2)}, u32[]{:S(2)}) collective-permute-start(bf16[8,128,128]{2,1,0:T(8,128)(2,1)S(1)} %slice.28.kv0_ref), channel_id=1, source_target_pairs={{0,2},{1,3},{2,4},{3,5},{4,6},{5,7},{6,8},{7,9},{8,10},{9,11},{10,... | collective-permute-start | bytes 786440 | tf_op jit(solution)/shard_map/ppermute | solution.py:40
  41.8 0.1 and_select_fusion
  41.9 0.6 pad_add_fusion.1.scal_ref
  42.5 6.7 %collective-permute-done.kv1_ref = bf16[8,128,128]{2,1,0:T(8,128)(2,1)S(1)} collective-permute-done((bf16[8,128,128]{2,1,0:T(8,128)(2,1)S(1)}, bf16[8,128,128]{2,1,0:T(8,128)(2,1)S(1)}, u32[]{:S(2)}, u32[]{:S(2)}) %collective-permute-start) | collective-permute-done | bytes 262176 | tf_op jit(solution)/shard_map/ppermute | solution.py:40
  49.3 4.1 %collective-permute-done.1.kv2_ref = bf16[8,128,128]{2,1,0:T(8,128)(2,1)S(1)} collective-permute-done((bf16[8,128,128]{2,1,0:T(8,128)(2,1)S(1)}, bf16[8,128,128]{2,1,0:T(8,128)(2,1)S(1)}, u32[]{:S(2)}, u32[]{:S(2)}) %collective-permute-start.1) | collective-permute-done | bytes 262176 | tf_op jit(solution)/shard_map/ppermute | solution.py:40
  53.3 0.0 copy-done.9
  53.4 0.7 copy-done.10
  54.1 11.3 %forward.1 = (bf16[8,512,128]{2,1,0:T(8,128)(2,1)}, bf16[4,128,1024]{2,1,0:T(8,128)(2,1)}, f32[4,1,1024]{2,1,0:T(1,128)}) custom-call(s32[24]{0:T(128)} %pad_add_fusion.1.scal_ref, bf16[8,640,128]{2,1,0:T(8,128)(2,1)} %copy-done.1, s32[4,1,1024]{2,1,0:T(1,128)} %sub.51.doc_ref, bf16[8,128,128]{2,1,0:T(8,128)(2,1)} %copy-done.4, ...), custom_call_target="tpu_custom_call" | custom-call | flops 4000000000 | bytes 4000000 | tf_op jit(solution)/shard_map/forward/pallas_call | solution.py:216
  65.4 0.0 all-to-all-done.2.grad_ref
  65.4 6.7 %all-to-all-start.1 = ((bf16[8,512,128]{2,1,0:T(8,128)(2,1)}), bf16[8,512,128]{2,1,0:T(8,128)(2,1)S(1)}, u32[]{:S(2)}, u32[]{:S(2)}) async-start(bf16[8,512,128]{2,1,0:T(8,128)(2,1)} %get-tuple-element.14), calls=%async_computation.1 | async-start | bytes 2097152 | tf_op jit(solution)/shard_map/all_to_all | solution.py:276
  72.1 15.4 %backward.1 = (bf16[8,640,128]{2,1,0:T(8,128)(2,1)}, bf16[8,128,128]{2,1,0:T(8,128)(2,1)}, bf16[8,128,128]{2,1,0:T(8,128)(2,1)}, bf16[8,128,128]{2,1,0:T(8,128)(2,1)}) custom-call(s32[24]{0:T(128)} %pad_add_fusion.1.scal_ref, bf16[8,640,128]{2,1,0:T(8,128)(2,1)} %copy-done.1, bf16[8,512,128]{2,1,0:T(8,128)(2,1)} %copy-done.3, ...), custom_call_target="tpu_custom_call" | custom-call | flops 10000000000 | bytes 6000000 | tf_op jit(solution)/shard_map/backward/pallas_call | solution.py:244
  87.5 0.0 all-to-all-done.1
  87.5 12.7 %collective-permute-start.3 = (bf16[8,128,128]{2,1,0:T(8,128)(2,1)}, bf16[8,128,128]{2,1,0:T(8,128)(2,1)S(1)}, u32[]{:S(2)}, u32[]{:S(2)}) collective-permute-start(bf16[8,128,128]{2,1,0:T(8,128)(2,1)} %get-tuple-element.23), channel_id=1, source_target_pairs={{2,0},{3,1},{4,2},{5,3},{6,4},{7,5},{8,6},{9,7},{10,8},{11,9},{12,... | collective-permute-start | bytes 786440 | tf_op jit(solution)/shard_map/ppermute | solution.py:40
  100.1 1.9 %collective-permute-start.2 = (bf16[8,128,128]{2,1,0:T(8,128)(2,1)}, bf16[8,128,128]{2,1,0:T(8,128)(2,1)S(1)}, u32[]{:S(2)}, u32[]{:S(2)}) collective-permute-start(bf16[8,128,128]{2,1,0:T(8,128)(2,1)} %get-tuple-element.22), channel_id=1, source_target_pairs={{1,0},{2,1},{3,2},{4,3},{5,4},{6,5},{7,6},{8,7},{9,8},{10,9},{11,1... | collective-permute-start | bytes 786440 | tf_op jit(solution)/shard_map/ppermute | solution.py:40
  102.1 1.9 %collective-permute-done.3 = bf16[8,128,128]{2,1,0:T(8,128)(2,1)S(1)} collective-permute-done((bf16[8,128,128]{2,1,0:T(8,128)(2,1)}, bf16[8,128,128]{2,1,0:T(8,128)(2,1)S(1)}, u32[]{:S(2)}, u32[]{:S(2)}) %collective-permute-start.3) | collective-permute-done | bytes 262176 | tf_op jit(solution)/shard_map/ppermute | solution.py:40
  104.0 4.1 %collective-permute-done.2 = bf16[8,128,128]{2,1,0:T(8,128)(2,1)S(1)} collective-permute-done((bf16[8,128,128]{2,1,0:T(8,128)(2,1)}, bf16[8,128,128]{2,1,0:T(8,128)(2,1)S(1)}, u32[]{:S(2)}, u32[]{:S(2)}) %collective-permute-start.2) | collective-permute-done | bytes 262176 | tf_op jit(solution)/shard_map/ppermute | solution.py:40
  108.0 1.8 %fusion = bf16[8,640,128]{2,1,0:T(8,128)(2,1)} fusion(bf16[8,640,128]{2,1,0:T(8,128)(2,1)} %get-tuple-element.20, bf16[8,128,128]{2,1,0:T(8,128)(2,1)S(1)} %collective-permute-done.3, bf16[8,128,128]{2,1,0:T(8,128)(2,1)S(1)} %collective-permute-done.2, bf16[8,128,128]{2,1,0:T(8,128)(2,1)} %get-tuple-element.21), kind=kLoop, calls=%fused_computation.8 | loop fusion | flops 786432 | bytes 1048576 | tf_op jit(solution)/shard_map/dynamic_update_slice | solution.py:312
  109.8 7.2 %all-to-all-start.3 = ((bf16[8,640,128]{2,1,0:T(8,128)(2,1)}), bf16[8,640,128]{2,1,0:T(8,128)(2,1)S(1)}, u32[]{:S(2)}, u32[]{:S(2)}) async-start(bf16[8,640,128]{2,1,0:T(8,128)(2,1)} %fusion), calls=%async_computation.3 | async-start | bytes 2621440 | tf_op jit(solution)/shard_map/all_to_all | solution.py:276
  117.1 1.3 copy_bitcast_fusion.1
  118.3 16.7 %all-to-all-done.3 = bf16[8,640,128]{2,1,0:T(8,128)(2,1)S(1)} async-done(((bf16[8,640,128]{2,1,0:T(8,128)(2,1)}), bf16[8,640,128]{2,1,0:T(8,128)(2,1)S(1)}, u32[]{:S(2)}, u32[]{:S(2)}) %all-to-all-start.3) | async-done | bytes 1310752 | tf_op jit(solution)/shard_map/all_to_all | solution.py:276
  135.1 0.7 copy.35
  135.8 0.7 copy.36
  136.5 1.3 copy_bitcast_fusion
  (20 shorter events, 0.1 us)
Async XLA Ops:
  0.6 1.2 copy-start
  0.6 1.4 %copy-start.5 = (bf16[64,8,128]{2,1,0:T(8,128)(2,1)S(1)}, bf16[64,8,128]{2,1,0:T(8,128)(2,1)}, u32[]{:S(2)}) copy-start(bf16[64,8,128]{2,1,0:T(8,128)(2,1)} %param.8) | copy-start | bytes 393220
  0.7 1.4 %copy-start.6 = (bf16[64,8,128]{2,1,0:T(8,128)(2,1)S(1)}, bf16[64,8,128]{2,1,0:T(8,128)(2,1)}, u32[]{:S(2)}) copy-start(bf16[64,8,128]{2,1,0:T(8,128)(2,1)} %param.7) | copy-start | bytes 393220
  3.3 6.7 %copy-start.8 = (s32[48]{0:T(128)S(1)}, s32[48]{0:T(128)}, u32[]{:S(2)}) copy-start(s32[48]{0:T(128)} %param.10) | copy-start | bytes 580
  3.3 7.0 %copy-start.7 = (s32[256]{0:T(256)S(1)}, s32[256]{0:T(256)}, u32[]{:S(2)}) copy-start(s32[256]{0:T(256)} %param.11) | copy-start | bytes 3076
  3.3 8.4 %copy-start.2 = (bf16[64,64,128]{2,1,0:T(8,128)(2,1)S(1)}, bf16[64,64,128]{2,1,0:T(8,128)(2,1)}, u32[]{:S(2)}) copy-start(bf16[64,64,128]{2,1,0:T(8,128)(2,1)} %param.9) | copy-start | bytes 3145732
  3.3 23.4 %all-to-all-start = ((bf16[8,640,128]{2,1,0:T(8,128)(2,1)}), bf16[8,640,128]{2,1,0:T(8,128)(2,1)S(1)}, u32[]{:S(2)}, u32[]{:S(2)}) async-start(bf16[8,640,128]{2,1,0:T(8,128)(2,1)} %pad_maximum_fusion), calls=%async_computation | async-start | bytes 2621440 | tf_op jit(solution)/shard_map/all_to_all | solution.py:276
  26.7 6.2 %copy-start.1 = (bf16[8,640,128]{2,1,0:T(8,128)(2,1)}, bf16[8,640,128]{2,1,0:T(8,128)(2,1)S(1)}, u32[]{:S(2)}) copy-start(bf16[8,640,128]{2,1,0:T(8,128)(2,1)S(1)} %all-to-all-done.q_ref) | copy-start | bytes 3932164
  26.8 38.7 %all-to-all-start.2 = ((bf16[8,512,128]{2,1,0:T(8,128)(2,1)}), bf16[8,512,128]{2,1,0:T(8,128)(2,1)S(1)}, u32[]{:S(2)}, u32[]{:S(2)}) async-start(bf16[8,512,128]{2,1,0:T(8,128)(2,1)} %copy_bitcast_fusion.2), calls=%async_computation.2 | async-start | bytes 2097152 | tf_op jit(solution)/shard_map/all_to_all | solution.py:276
  33.0 20.3 %copy-start.4 = (bf16[8,128,128]{2,1,0:T(8,128)(2,1)}, bf16[8,128,128]{2,1,0:T(8,128)(2,1)S(1)}, u32[]{:S(2)}) copy-start(bf16[8,128,128]{2,1,0:T(8,128)(2,1)S(1)} %slice.28.kv0_ref) | copy-start | bytes 786436
  33.0 16.3 %collective-permute-start = (bf16[8,128,128]{2,1,0:T(8,128)(2,1)S(1)}, bf16[8,128,128]{2,1,0:T(8,128)(2,1)S(1)}, u32[]{:S(2)}, u32[]{:S(2)}) collective-permute-start(bf16[8,128,128]{2,1,0:T(8,128)(2,1)S(1)} %slice.28.kv0_ref), channel_id=1, source_target_pairs={{0,1},{1,2},{2,3},{3,4},{4,5},{5,6},{6,7},{7,8},{8,9},{9,10},{10,1... | collective-permute-start | bytes 786440 | tf_op jit(solution)/shard_map/ppermute | solution.py:40
  36.2 17.2 %collective-permute-start.1 = (bf16[8,128,128]{2,1,0:T(8,128)(2,1)S(1)}, bf16[8,128,128]{2,1,0:T(8,128)(2,1)S(1)}, u32[]{:S(2)}, u32[]{:S(2)}) collective-permute-start(bf16[8,128,128]{2,1,0:T(8,128)(2,1)S(1)} %slice.28.kv0_ref), channel_id=1, source_target_pairs={{0,2},{1,3},{2,4},{3,5},{4,6},{5,7},{6,8},{7,9},{8,10},{9,11},{10,... | collective-permute-start | bytes 786440 | tf_op jit(solution)/shard_map/ppermute | solution.py:40
  49.3 4.1 %copy-start.9 = (bf16[8,128,128]{2,1,0:T(8,128)(2,1)}, bf16[8,128,128]{2,1,0:T(8,128)(2,1)S(1)}, u32[]{:S(2)}) copy-start(bf16[8,128,128]{2,1,0:T(8,128)(2,1)S(1)} %collective-permute-done.kv1_ref) | copy-start | bytes 786436
  53.4 0.7 copy-start.10
  65.4 6.7 %copy-start.3 = (bf16[8,512,128]{2,1,0:T(8,128)(2,1)}, bf16[8,512,128]{2,1,0:T(8,128)(2,1)S(1)}, u32[]{:S(2)}) copy-start(bf16[8,512,128]{2,1,0:T(8,128)(2,1)S(1)} %all-to-all-done.2.grad_ref) | copy-start | bytes 3145732
  65.4 22.0 %all-to-all-start.1 = ((bf16[8,512,128]{2,1,0:T(8,128)(2,1)}), bf16[8,512,128]{2,1,0:T(8,128)(2,1)S(1)}, u32[]{:S(2)}, u32[]{:S(2)}) async-start(bf16[8,512,128]{2,1,0:T(8,128)(2,1)} %get-tuple-element.14), calls=%async_computation.1 | async-start | bytes 2097152 | tf_op jit(solution)/shard_map/all_to_all | solution.py:276
  87.5 16.5 %collective-permute-start.3 = (bf16[8,128,128]{2,1,0:T(8,128)(2,1)}, bf16[8,128,128]{2,1,0:T(8,128)(2,1)S(1)}, u32[]{:S(2)}, u32[]{:S(2)}) collective-permute-start(bf16[8,128,128]{2,1,0:T(8,128)(2,1)} %get-tuple-element.23), channel_id=1, source_target_pairs={{2,0},{3,1},{4,2},{5,3},{6,4},{7,5},{8,6},{9,7},{10,8},{11,9},{12,... | collective-permute-start | bytes 786440 | tf_op jit(solution)/shard_map/ppermute | solution.py:40
  100.1 7.9 %collective-permute-start.2 = (bf16[8,128,128]{2,1,0:T(8,128)(2,1)}, bf16[8,128,128]{2,1,0:T(8,128)(2,1)S(1)}, u32[]{:S(2)}, u32[]{:S(2)}) collective-permute-start(bf16[8,128,128]{2,1,0:T(8,128)(2,1)} %get-tuple-element.22), channel_id=1, source_target_pairs={{1,0},{2,1},{3,2},{4,3},{5,4},{6,5},{7,6},{8,7},{9,8},{10,9},{11,1... | collective-permute-start | bytes 786440 | tf_op jit(solution)/shard_map/ppermute | solution.py:40
  109.8 25.2 %all-to-all-start.3 = ((bf16[8,640,128]{2,1,0:T(8,128)(2,1)}), bf16[8,640,128]{2,1,0:T(8,128)(2,1)S(1)}, u32[]{:S(2)}, u32[]{:S(2)}) async-start(bf16[8,640,128]{2,1,0:T(8,128)(2,1)} %fusion), calls=%async_computation.3 | async-start | bytes 2621440 | tf_op jit(solution)/shard_map/all_to_all | solution.py:276

commit v4 on v3

v4 whole, which is shorter than its diff:
```python
import functools
import math

import jax
import jax.numpy as jnp
from jax import lax
from jax.experimental import pallas as pl
from jax.experimental.pallas import tpu as pltpu
from jax.sharding import PartitionSpec as P

HEAD_SIZE = 128
BLOCK = 128
CELL_BLOCKS = 4
SLOTS = 3
WINDOW_BLOCKS = SLOTS * CELL_BLOCKS
WINDOW = WINDOW_BLOCKS * BLOCK
CHUNK = 2 * BLOCK
PADDED = WINDOW + BLOCK
REACH = 10 * BLOCK
SHARE = 8
PARTS = 2
PART_TOKENS = 64 // PARTS
PART_ROWS = PART_TOKENS * SHARE
ROWS = 2 * PART_ROWS

SCALE = HEAD_SIZE ** (-0.5)
EXP2_SCALE = SCALE * math.log2(math.e)
NEG_BIG = -1e30

NT = (((1,), (1,)), ((), ()))
NN = (((1,), (0,)), ((), ()))
TN = (((0,), (0,)), ((), ()))


def dot(a, b, dims=NN):
    return lax.dot_general(a, b, dims, preferred_element_type=jnp.float32)


def passed_along(block, axis, distance):
    devices = range(lax.axis_size(axis))
    route = [(i - distance, i) for i in devices if i - distance in devices]
    return lax.ppermute(block, axis, route)


def stored_rows(kv_ref, block, which):
    first = kv_ref[2 * block, pl.ds(64 * which, 64), :]
    second = kv_ref[2 * block + 1, pl.ds(64 * which, 64), :]
    return jnp.concatenate([first, second], axis=0)


def window_start(scal_ref, slot, block):
    index = (SLOTS - 1 - slot) * CELL_BLOCKS + block
    return pl.multiple_of(scal_ref[index] * BLOCK, BLOCK)


def allowed_tile(key_start, first_block, doc_start, part):
    lane = lax.broadcasted_iota(jnp.int32, (1, ROWS), 1)
    token = jnp.where(lane >= PART_ROWS, 64 - PART_TOKENS, 0) + lax.shift_right_logical(lane, 3)
    query_pos = first_block * BLOCK + part * PART_TOKENS + token
    key_pos = lax.broadcasted_iota(jnp.int32, (CHUNK, ROWS), 0)
    return (key_pos >= doc_start - key_start) & (key_pos <= query_pos - key_start)


def each_chunk(low_block, chunks, work):
    def turn_work(turn, _):
        key_start = pl.multiple_of((low_block + 2 * turn) * BLOCK, BLOCK)
        work(turn, key_start, pl.ds(pl.multiple_of(turn * CHUNK, CHUNK), CHUNK))
        return 0

    lax.fori_loop(0, chunks, turn_work, 0)


def attention_kernel(part, scal_ref, q_ref, grad_ref, doc_ref, kv0_ref, kv1_ref, kv2_ref, *refs):
    if part == 0:
        out_ref, dk_acc, dv_acc, *scratch = refs
    else:
        dk_in, dv_in, out_ref, dkv0_ref, dkv1_ref, dkv2_ref, dk_acc, dv_acc, *scratch = refs
    key_seq, value_seq, value_t, scores, acc, top, dq_acc = scratch
    step = pl.program_id(0)

    @pl.when(step == 0)
    def _():
        for slot, kv_ref in enumerate((kv0_ref, kv1_ref, kv2_ref)):
            for block in range(CELL_BLOCKS):
                start = window_start(scal_ref, slot, block)
                key_seq[pl.ds(start, BLOCK), :] = stored_rows(kv_ref, block, 0)
                value = stored_rows(kv_ref, block, 1)
                value_seq[pl.ds(start, BLOCK), :] = value
                value_t[:, pl.ds(start, BLOCK)] = value.astype(jnp.float32).T.astype(jnp.bfloat16)
        zeros = jnp.zeros((BLOCK, HEAD_SIZE), jnp.bfloat16)
        key_seq[pl.ds(WINDOW, BLOCK), :] = zeros
        value_seq[pl.ds(WINDOW, BLOCK), :] = zeros
        value_t[:, pl.ds(WINDOW, BLOCK)] = zeros
        if part == 0:
            dk_acc[...] = jnp.zeros_like(dk_acc)
            dv_acc[...] = jnp.zeros_like(dv_acc)
        else:
            dk_acc[...] = dk_in[...]
            dv_acc[...] = dv_in[...]

    first_block = scal_ref[WINDOW_BLOCKS + step]
    low_block = scal_ref[WINDOW_BLOCKS + CELL_BLOCKS + step]
    last_start = scal_ref[WINDOW_BLOCKS + 2 * CELL_BLOCKS + step]
    chunks = lax.shift_right_logical(first_block - low_block + 2, 1)
    queries = q_ref[...].reshape(ROWS, HEAD_SIZE)
    out_grads = grad_ref[...].reshape(ROWS, HEAD_SIZE)
    top[...] = jnp.full_like(top, NEG_BIG)
    acc[...] = jnp.zeros_like(acc)
    dq_acc[...] = jnp.zeros_like(dq_acc)

    def score_chunk(turn, key_start, rows):
        def score(masked):
            raw = dot(key_seq[pl.ds(key_start, CHUNK), :], queries, NT)
            if masked:
                raw = jnp.where(allowed_tile(key_start, first_block, doc_ref[0], part), raw, NEG_BIG)
            scores[rows, :] = raw
            top[...] = jnp.maximum(top[...], jnp.max(raw.reshape(CHUNK // 8, 8, ROWS), axis=0))

        whole = (key_start >= last_start) & (key_start + CHUNK <= first_block * BLOCK)
        pl.when(whole)(lambda: score(False))
        pl.when(jnp.logical_not(whole))(lambda: score(True))

    each_chunk(low_block, chunks, score_chunk)
    highest = jnp.max(top[...], axis=0, keepdims=True) * EXP2_SCALE
    top[...] = jnp.zeros_like(top)

    def value_chunk(turn, key_start, rows):
        weights = jnp.exp2(scores[rows, :] * EXP2_SCALE - highest)
        top[...] += jnp.sum(weights.reshape(CHUNK // 8, 8, ROWS), axis=0)
        acc[...] += dot(value_t[:, pl.ds(key_start, CHUNK)], weights.astype(jnp.bfloat16))

    each_chunk(low_block, chunks, value_chunk)
    total = jnp.sum(top[...], axis=0, keepdims=True)
    lse = highest + jnp.log2(total)
    out = (acc[...] * (1.0 / total)).T.astype(jnp.bfloat16)
    out_ref[:, :PART_ROWS, :] = out.reshape(2, PART_ROWS, HEAD_SIZE)
    delta = jnp.sum((out.astype(jnp.float32) * out_grads.astype(jnp.float32)).T, axis=0, keepdims=True)

    def grad_chunk(turn, key_start, rows):
        window = pl.ds(key_start, CHUNK)
        weights = jnp.exp2(scores[rows, :] * EXP2_SCALE - lse)
        sent = dot(value_seq[window, :], out_grads, NT)
        grads = (weights * (sent - delta)).astype(jnp.bfloat16)
        dq_acc[...] += dot(grads, key_seq[window, :], TN)
        dk_acc[window, :] += dot(grads, queries)
        dv_acc[window, :] += dot(weights.astype(jnp.bfloat16), out_grads)

    each_chunk(low_block, chunks, grad_chunk)
    query_grad = (dq_acc[...] * SCALE).astype(jnp.bfloat16)
    out_ref[:, PART_ROWS:, :] = query_grad.reshape(2, PART_ROWS, HEAD_SIZE)

    if part == 1:

        @pl.when(step == CELL_BLOCKS - 1)
        def _():
            for slot, dkv_ref in enumerate((dkv0_ref, dkv1_ref, dkv2_ref)):
                for block in range(CELL_BLOCKS):
                    start = window_start(scal_ref, slot, block)
                    dk = (dk_acc[pl.ds(start, BLOCK), :] * SCALE).astype(jnp.bfloat16)
                    dv = dv_acc[pl.ds(start, BLOCK), :].astype(jnp.bfloat16)
                    for half in range(2):
                        rows = slice(half * 64, (half + 1) * 64)
                        dkv_ref[2 * block + half, pl.ds(0, 64), :] = dk[rows]
                        dkv_ref[2 * block + half, pl.ds(64, 64), :] = dv[rows]


def attention(part, scal, rows_in, doc_rows, kv, sums=()):
    def resident(shape):
        return pl.BlockSpec(shape, lambda b, s: (0,) * len(shape))

    def row_spec(place):
        return pl.BlockSpec((2, PART_ROWS, HEAD_SIZE), lambda b, s: (b, place, 0))

    kv_spec = resident((8, 128, HEAD_SIZE))
    sum_spec = resident((PADDED, HEAD_SIZE))
    sum_shape = jax.ShapeDtypeStruct((PADDED, HEAD_SIZE), jnp.float32)
    out_rows = 2 * PART_ROWS + (128 if part else 0)
    out_specs = [pl.BlockSpec((2, 2 * PART_ROWS, HEAD_SIZE), lambda b, s: (b, 0, 0))]
    out_shape = [jax.ShapeDtypeStruct((8, out_rows, HEAD_SIZE), jnp.bfloat16)]
    scratch = [
        pltpu.VMEM((PADDED, HEAD_SIZE), jnp.bfloat16),
        pltpu.VMEM((PADDED, HEAD_SIZE), jnp.bfloat16),
        pltpu.VMEM((HEAD_SIZE, PADDED), jnp.bfloat16),
        pltpu.VMEM((REACH, ROWS), jnp.float32),
        pltpu.VMEM((HEAD_SIZE, ROWS), jnp.float32),
        pltpu.VMEM((8, ROWS), jnp.float32),
        pltpu.VMEM((ROWS, HEAD_SIZE), jnp.float32),
    ]
    if part == 0:
        out_specs += [sum_spec, sum_spec]
        out_shape += [sum_shape, sum_shape]
    else:
        out_specs += [kv_spec] * 3
        out_shape += [jax.ShapeDtypeStruct((8, 128, HEAD_SIZE), jnp.bfloat16)] * 3
        scratch = [pltpu.VMEM((PADDED, HEAD_SIZE), jnp.float32)] * 2 + scratch
    return pl.pallas_call(
        functools.partial(attention_kernel, part),
        grid_spec=pltpu.PrefetchScalarGridSpec(
            num_scalar_prefetch=1,
            grid=(CELL_BLOCKS,),
            in_specs=[row_spec(0), row_spec(1), pl.BlockSpec((1, 1, ROWS), lambda b, s: (b, 0, 0))] + [kv_spec] * 3 + [sum_spec] * len(sums),
            out_specs=out_specs,
            scratch_shapes=scratch,
        ),
        out_shape=out_shape,
        compiler_params=pltpu.CompilerParams(dimension_semantics=("arbitrary",), vmem_limit_bytes=60 * 1024 * 1024),
        cost_estimate=pl.CostEstimate(flops=10_000_000_000, bytes_accessed=6_000_000, transcendentals=4_000_000),
        name="attention_first" if part == 0 else "attention_second",
    )(scal, rows_in, rows_in, doc_rows, *kv, *sums)


def by_head(rows):
    tokens = rows.shape[0]
    split = rows.reshape(tokens, 8, -1, HEAD_SIZE).transpose(1, 0, 2, 3)
    return split.reshape(8, -1, HEAD_SIZE)


def exchanged(block):
    return lax.all_to_all(block, "head", split_axis=0, concat_axis=0, tiled=True)


def plan(doc_lengths, stored_block_order):
    cell = lax.axis_index("ctx")
    starts = jnp.cumsum(doc_lengths) - doc_lengths
    window_first = (cell - (SLOTS - 1)) * CELL_BLOCKS
    padded = jnp.pad(stored_block_order, (WINDOW_BLOCKS - CELL_BLOCKS, 0))
    window_order = lax.dynamic_slice_in_dim(padded, cell * CELL_BLOCKS, WINDOW_BLOCKS, 0)
    base = jnp.arange(WINDOW_BLOCKS, dtype=jnp.int32) // CELL_BLOCKS * CELL_BLOCKS
    place = base + window_order % CELL_BLOCKS
    own_place = place[WINDOW_BLOCKS - CELL_BLOCKS :]
    own_block = window_first + own_place
    lane = lax.broadcasted_iota(jnp.int32, (PARTS, CELL_BLOCKS, 1, ROWS), 3)
    part = lax.broadcasted_iota(jnp.int32, (PARTS, CELL_BLOCKS, 1, ROWS), 0)
    token = lane // PART_ROWS * 64 + part * PART_TOKENS + lane % PART_ROWS // SHARE
    pos = own_block[None, :, None, None] * BLOCK + token
    begun = starts <= pos[..., None]
    doc_start = jnp.max(jnp.where(begun, starts, 0), axis=-1)
    doc_rows = (doc_start - window_first * BLOCK).astype(jnp.int32)
    edges = jnp.concatenate([own_block * BLOCK, own_block * BLOCK + BLOCK - 1])
    low = jnp.max(jnp.where(starts <= edges[:, None], starts, 0), axis=-1) - window_first * BLOCK
    scal = jnp.concatenate([place, own_place, low[:CELL_BLOCKS] // BLOCK, low[CELL_BLOCKS:]]).astype(jnp.int32)
    return scal, doc_rows


def body(queries, keys, values, out_grad, doc_lengths, stored_block_order):
    scal, doc_rows = plan(doc_lengths, stored_block_order)
    half = PART_TOKENS
    first_in = exchanged(
        jnp.concatenate([by_head(queries[:half]), by_head(out_grad[:half]), by_head(keys), by_head(values)], axis=1)
    )
    kv0 = first_in[:, 2 * PART_ROWS :, :]
    kv = (kv0, passed_along(kv0, "ctx", 1), passed_along(kv0, "ctx", 2))
    second_rows = jnp.concatenate([by_head(queries[half:]), by_head(out_grad[half:])], axis=1)
    second_rows, *kv = lax.optimization_barrier((second_rows, *kv))
    second_in = exchanged(second_rows)
    first_out, *sums = attention(0, scal, first_in, doc_rows[0], kv)
    first_back = exchanged(first_out)
    second_out, dkv0, dkv1, dkv2 = attention(1, scal, second_in, doc_rows[1], kv, sums)
    first_back, dkv1, dkv2 = lax.optimization_barrier((first_back, dkv1, dkv2))
    near, far = passed_along(dkv1, "ctx", -1), passed_along(dkv2, "ctx", -2)
    summed = dkv0.astype(jnp.float32) + near.astype(jnp.float32) + far.astype(jnp.float32)
    second_out = lax.dynamic_update_slice(second_out, summed.astype(jnp.bfloat16), (0, 2 * PART_ROWS, 0))
    second_back = exchanged(second_out)

    def by_token(block, tokens, heads):
        return block.reshape(8, tokens, heads, HEAD_SIZE).transpose(1, 0, 2, 3).reshape(tokens, -1, HEAD_SIZE)

    def joined(start):
        rows = slice(start, start + PART_ROWS)
        return jnp.concatenate([by_token(back[:, rows], half, SHARE) for back in (first_back, second_back)], axis=0)

    attended, query_grad = joined(0), joined(PART_ROWS)
    key_gradient = by_token(second_back[:, 2 * PART_ROWS : 2 * PART_ROWS + 64], 64, 1)
    value_gradient = by_token(second_back[:, 2 * PART_ROWS + 64 :], 64, 1)
    return attended, query_grad, key_gradient, value_gradient


def solution(mesh):
    spec = P(("ctx", "head"), None, None)
    return jax.shard_map(
        body,
        mesh=mesh,
        in_specs=(spec, spec, spec, spec, P(), P()),
        out_specs=(spec, spec, spec, spec),
        check_vma=False,
    )
```

time: 138 us -> 149 us (1.080)
  the two profiles are of different devices: /device:TPU:121 before, /device:TPU:98 now
where the time goes in v4:
time: 149 us; the launch traced here: 148 us
  waiting for transfers between devices  59.5 us (40%)
  starting transfers between devices  43.3 us (29%)
  Pallas kernels  30.8 us (21%)
  other arithmetic  7.71 us (5%)
  local copies, waits for them, and re-layouts  5.99 us (4%)
    all_to_all x4, waiting for transfers between devices, exchanged(): lax.all_to_all(block, 'head', split_axis=0, concat_axis=0, tiled=True)  34.1 us
    pallas_call x2, Pallas kernels, attention(): pl.pallas_call(functools.partial(attention_kernel, part), grid_spec=pltpu...  30.8 us
    ppermute x4, waiting for transfers between devices, passed_along(): return lax.ppermute(block, axis, route)  25.4 us
    all_to_all x4, starting transfers between devices, exchanged(): lax.all_to_all(block, 'head', split_axis=0, concat_axis=0, tiled=True)  23.1 us
    ppermute x4, starting transfers between devices, passed_along(): return lax.ppermute(block, axis, route)  20.2 us
  transfers between devices with their start and end apart: 8, of which 6 were waited for; matrix products, arithmetic and copies ran while one was open for 3% of the time, Pallas kernels for 21%

profile of v4, /device:TPU:98, one launch (start us, length us, event | category | flops | bytes accessed | tf_op | source)
XLA Modules:
  0.0 148.1 jit_solution(497954117168997662)
XLA Ops:
  0.6 1.4 slice_bitcast_fusion.7
  2.0 0.2 copy-done.1
  2.2 0.1 slice_bitcast_fusion.6
  2.2 0.8 copy-done.4
  3.1 0.1 copy-done.5
  3.2 0.2 copy_bitcast_fusion.6
  3.4 1.2 pad_maximum_fusion
  4.6 6.2 %all-to-all-start = ((bf16[8,640,128]{2,1,0:T(8,128)(2,1)}), bf16[8,640,128]{2,1,0:T(8,128)(2,1)S(1)}, u32[]{:S(2)}, u32[]{:S(2)}) async-start(bf16[8,640,128]{2,1,0:T(8,128)(2,1)} %pad_maximum_fusion), calls=%async_computation | async-start | bytes 2621440 | tf_op jit(solution)/shard_map/all_to_all | solution.py:219
  10.8 0.1 copy.36
  10.9 0.1 reduce-window.9
  11.0 0.1 reduce.1
  11.1 0.1 fusion.12
  11.2 0.1 broadcast_add_fusion.1
  11.3 0.1 pad_add_fusion
  11.4 0.1 fusion.3
  11.5 0.2 select_reduce_fusion
  11.7 0.2 select_reduce_fusion.1
  11.9 0.2 copy_bitcast_fusion.4
  12.1 1.0 pad_maximum_fusion.1
  13.2 0.1 and_select_fusion
  13.2 15.7 %all-to-all-done.q_ref.grad_ref = bf16[8,640,128]{2,1,0:T(8,128)(2,1)S(1)} async-done(((bf16[8,640,128]{2,1,0:T(8,128)(2,1)}), bf16[8,640,128]{2,1,0:T(8,128)(2,1)S(1)}, u32[]{:S(2)}, u32[]{:S(2)}) %all-to-all-start) | async-done | bytes 1310752 | tf_op jit(solution)/shard_map/all_to_all | solution.py:219
  29.0 5.7 %collective-permute-start.1 = (bf16[8,128,128]{2,1,0:T(8,128)(2,1)S(1)}, bf16[8,128,128]{2,1,0:T(8,128)(2,1)S(1)}, u32[]{:S(2)}, u32[]{:S(2)}) collective-permute-start(bf16[8,128,128]{2,1,0:T(8,128)(2,1)S(1)} %slice.67.kv0_ref), channel_id=1, source_target_pairs={{0,2},{1,3},{2,4},{3,5},{4,6},{5,7},{6,8},{7,9},{8,10},{9,11},{10,... | collective-permute-start | bytes 786440 | tf_op jit(solution)/shard_map/ppermute | solution.py:42
  34.7 1.9 %collective-permute-start = (bf16[8,128,128]{2,1,0:T(8,128)(2,1)S(1)}, bf16[8,128,128]{2,1,0:T(8,128)(2,1)S(1)}, u32[]{:S(2)}, u32[]{:S(2)}) collective-permute-start(bf16[8,128,128]{2,1,0:T(8,128)(2,1)S(1)} %slice.67.kv0_ref), channel_id=1, source_target_pairs={{0,1},{1,2},{2,3},{3,4},{4,5},{5,6},{6,7},{7,8},{8,9},{9,10},{10,1... | collective-permute-start | bytes 786440 | tf_op jit(solution)/shard_map/ppermute | solution.py:42
  36.7 0.6 pad_add_fusion.1.scal_ref
  37.2 0.6 slice_bitcast_fusion.11
  37.9 2.1 %collective-permute-done.1.kv2_ref = bf16[8,128,128]{2,1,0:T(8,128)(2,1)S(1)} collective-permute-done((bf16[8,128,128]{2,1,0:T(8,128)(2,1)S(1)}, bf16[8,128,128]{2,1,0:T(8,128)(2,1)S(1)}, u32[]{:S(2)}, u32[]{:S(2)}) %collective-permute-start.1) | collective-permute-done | bytes 262176 | tf_op jit(solution)/shard_map/ppermute | solution.py:42
  39.9 2.5 %collective-permute-done.kv1_ref = bf16[8,128,128]{2,1,0:T(8,128)(2,1)S(1)} collective-permute-done((bf16[8,128,128]{2,1,0:T(8,128)(2,1)S(1)}, bf16[8,128,128]{2,1,0:T(8,128)(2,1)S(1)}, u32[]{:S(2)}, u32[]{:S(2)}) %collective-permute-start) | collective-permute-done | bytes 262176 | tf_op jit(solution)/shard_map/ppermute | solution.py:42
  42.4 4.2 %all-to-all-start.2 = ((bf16[8,512,128]{2,1,0:T(8,128)(2,1)}), bf16[8,512,128]{2,1,0:T(8,128)(2,1)S(1)}, u32[]{:S(2)}, u32[]{:S(2)}) async-start(bf16[8,512,128]{2,1,0:T(8,128)(2,1)} %pad_maximum_fusion.1), calls=%async_computation.2 | async-start | bytes 2097152 | tf_op jit(solution)/shard_map/all_to_all | solution.py:219
  46.6 15.2 %attention_first.1 = (bf16[8,512,128]{2,1,0:T(8,128)(2,1)}, f32[1664,128]{1,0:T(8,128)}, f32[1664,128]{1,0:T(8,128)}) custom-call(s32[24]{0:T(128)} %pad_add_fusion.1.scal_ref, bf16[8,640,128]{2,1,0:T(8,128)(2,1)} %copy-done, bf16[8,640,128]{2,1,0:T(8,128)(2,1)} %copy-done, s32[4,1,512]{2,1,0:T(1,128)} %get-tuple-element.56.doc_ref, ...), custom_call_target="tpu_custom_call" | custom-call | flops 10000000000 | bytes 6000000 | tf_op jit(solution)/shard_map/attention_first/pallas_call | solution.py:196
  61.8 1.1 all-to-all-done.2.q_ref.grad_ref
  62.9 6.2 %all-to-all-start.1 = ((bf16[8,512,128]{2,1,0:T(8,128)(2,1)}), bf16[8,512,128]{2,1,0:T(8,128)(2,1)S(1)}, u32[]{:S(2)}, u32[]{:S(2)}) async-start(bf16[8,512,128]{2,1,0:T(8,128)(2,1)} %get-tuple-element.21), calls=%async_computation.1 | async-start | bytes 2097152 | tf_op jit(solution)/shard_map/all_to_all | solution.py:219
  69.1 15.6 %attention_second.1 = (bf16[8,640,128]{2,1,0:T(8,128)(2,1)}, bf16[8,128,128]{2,1,0:T(8,128)(2,1)}, bf16[8,128,128]{2,1,0:T(8,128)(2,1)}, bf16[8,128,128]{2,1,0:T(8,128)(2,1)}) custom-call(s32[24]{0:T(128)} %pad_add_fusion.1.scal_ref, bf16[8,512,128]{2,1,0:T(8,128)(2,1)} %copy-done.2, bf16[8,512,128]{2,1,0:T(8,128)(2,1)} %copy-done.2, ...), custom_call_target="tpu_custom_call" | custom-call | flops 10000000000 | bytes 6000000 | tf_op jit(solution)/shard_map/attention_second/pallas_call | solution.py:196
  84.6 7.3 %collective-permute-start.2 = (bf16[8,128,128]{2,1,0:T(8,128)(2,1)}, bf16[8,128,128]{2,1,0:T(8,128)(2,1)S(1)}, u32[]{:S(2)}, u32[]{:S(2)}) collective-permute-start(bf16[8,128,128]{2,1,0:T(8,128)(2,1)} %get-tuple-element.30), channel_id=1, source_target_pairs={{1,0},{2,1},{3,2},{4,3},{5,4},{6,5},{7,6},{8,7},{9,8},{10,9},{11,1... | collective-permute-start | bytes 786440 | tf_op jit(solution)/shard_map/ppermute | solution.py:42
  92.0 5.3 %collective-permute-start.3 = (bf16[8,128,128]{2,1,0:T(8,128)(2,1)}, bf16[8,128,128]{2,1,0:T(8,128)(2,1)S(1)}, u32[]{:S(2)}, u32[]{:S(2)}) collective-permute-start(bf16[8,128,128]{2,1,0:T(8,128)(2,1)} %get-tuple-element.31), channel_id=1, source_target_pairs={{2,0},{3,1},{4,2},{5,3},{6,4},{7,5},{8,6},{9,7},{10,8},{11,9},{12,... | collective-permute-start | bytes 786440 | tf_op jit(solution)/shard_map/ppermute | solution.py:42
  97.3 20.8 %collective-permute-done.3 = bf16[8,128,128]{2,1,0:T(8,128)(2,1)S(1)} collective-permute-done((bf16[8,128,128]{2,1,0:T(8,128)(2,1)}, bf16[8,128,128]{2,1,0:T(8,128)(2,1)S(1)}, u32[]{:S(2)}, u32[]{:S(2)}) %collective-permute-start.3) | collective-permute-done | bytes 262176 | tf_op jit(solution)/shard_map/ppermute | solution.py:42
  118.1 1.8 %fusion = bf16[8,640,128]{2,1,0:T(8,128)(2,1)} fusion(bf16[8,640,128]{2,1,0:T(8,128)(2,1)} %get-tuple-element.28, bf16[8,128,128]{2,1,0:T(8,128)(2,1)S(1)} %collective-permute-done.3, bf16[8,128,128]{2,1,0:T(8,128)(2,1)S(1)} %collective-permute-done.2, bf16[8,128,128]{2,1,0:T(8,128)(2,1)} %get-tuple-element.29), kind=kLoop, calls=%fused_computation.22 | loop fusion | flops 786432 | bytes 1048576 | tf_op jit(solution)/shard_map/dynamic_update_slice | solution.py:262
  119.8 6.6 %all-to-all-start.3 = ((bf16[8,640,128]{2,1,0:T(8,128)(2,1)}), bf16[8,640,128]{2,1,0:T(8,128)(2,1)S(1)}, u32[]{:S(2)}, u32[]{:S(2)}) async-start(bf16[8,640,128]{2,1,0:T(8,128)(2,1)} %fusion), calls=%async_computation.3 | async-start | bytes 2621440 | tf_op jit(solution)/shard_map/all_to_all | solution.py:219
  126.4 0.1 slice_bitcast_fusion.2
  126.5 0.1 copy.62
  126.7 0.1 copy.64
  126.8 17.3 %all-to-all-done.3 = bf16[8,640,128]{2,1,0:T(8,128)(2,1)S(1)} async-done(((bf16[8,640,128]{2,1,0:T(8,128)(2,1)}), bf16[8,640,128]{2,1,0:T(8,128)(2,1)S(1)}, u32[]{:S(2)}, u32[]{:S(2)}) %all-to-all-start.3) | async-done | bytes 1310752 | tf_op jit(solution)/shard_map/all_to_all | solution.py:219
  144.1 0.1 slice_bitcast_fusion
  144.2 0.1 copy.61
  144.4 0.7 copy.49
  145.1 0.7 copy.48
  145.8 0.1 copy.63
  146.0 1.1 pad_maximum_fusion.3
  147.1 1.1 pad_maximum_fusion.2
  (29 shorter events, 0.2 us)
Async XLA Ops:
  0.6 1.5 %copy-start.1 = (bf16[64,64,128]{2,1,0:T(8,128)(2,1)S(1)}, bf16[64,64,128]{2,1,0:T(8,128)(2,1)}, u32[]{:S(2)}) copy-start(bf16[64,64,128]{2,1,0:T(8,128)(2,1)} %param.9) | copy-start | bytes 3145732
  2.2 0.9 copy-start.4
  2.2 1.0 copy-start.5
  4.6 6.2 %copy-start.7 = (s32[48]{0:T(128)S(1)}, s32[48]{0:T(128)}, u32[]{:S(2)}) copy-start(s32[48]{0:T(128)} %param.10) | copy-start | bytes 580
  4.6 6.5 %copy-start.6 = (s32[256]{0:T(256)S(1)}, s32[256]{0:T(256)}, u32[]{:S(2)}) copy-start(s32[256]{0:T(256)} %param.11) | copy-start | bytes 3076
  4.6 24.4 %all-to-all-start = ((bf16[8,640,128]{2,1,0:T(8,128)(2,1)}), bf16[8,640,128]{2,1,0:T(8,128)(2,1)S(1)}, u32[]{:S(2)}, u32[]{:S(2)}) async-start(bf16[8,640,128]{2,1,0:T(8,128)(2,1)} %pad_maximum_fusion), calls=%async_computation | async-start | bytes 2621440 | tf_op jit(solution)/shard_map/all_to_all | solution.py:219
  29.0 13.4 %copy-start = (bf16[8,640,128]{2,1,0:T(8,128)(2,1)}, bf16[8,640,128]{2,1,0:T(8,128)(2,1)S(1)}, u32[]{:S(2)}) copy-start(bf16[8,640,128]{2,1,0:T(8,128)(2,1)S(1)} %all-to-all-done.q_ref.grad_ref) | copy-start | bytes 3932164
  29.0 17.6 %copy-start.3 = (bf16[8,128,128]{2,1,0:T(8,128)(2,1)}, bf16[8,128,128]{2,1,0:T(8,128)(2,1)S(1)}, u32[]{:S(2)}) copy-start(bf16[8,128,128]{2,1,0:T(8,128)(2,1)S(1)} %slice.67.kv0_ref) | copy-start | bytes 786436
  29.0 10.9 %collective-permute-start.1 = (bf16[8,128,128]{2,1,0:T(8,128)(2,1)S(1)}, bf16[8,128,128]{2,1,0:T(8,128)(2,1)S(1)}, u32[]{:S(2)}, u32[]{:S(2)}) collective-permute-start(bf16[8,128,128]{2,1,0:T(8,128)(2,1)S(1)} %slice.67.kv0_ref), channel_id=1, source_target_pairs={{0,2},{1,3},{2,4},{3,5},{4,6},{5,7},{6,8},{7,9},{8,10},{9,11},{10,... | collective-permute-start | bytes 786440 | tf_op jit(solution)/shard_map/ppermute | solution.py:42
  34.7 7.7 %collective-permute-start = (bf16[8,128,128]{2,1,0:T(8,128)(2,1)S(1)}, bf16[8,128,128]{2,1,0:T(8,128)(2,1)S(1)}, u32[]{:S(2)}, u32[]{:S(2)}) collective-permute-start(bf16[8,128,128]{2,1,0:T(8,128)(2,1)S(1)} %slice.67.kv0_ref), channel_id=1, source_target_pairs={{0,1},{1,2},{2,3},{3,4},{4,5},{5,6},{6,7},{7,8},{8,9},{9,10},{10,1... | collective-permute-start | bytes 786440 | tf_op jit(solution)/shard_map/ppermute | solution.py:42
  39.9 6.7 %copy-start.8 = (bf16[8,128,128]{2,1,0:T(8,128)(2,1)}, bf16[8,128,128]{2,1,0:T(8,128)(2,1)S(1)}, u32[]{:S(2)}) copy-start(bf16[8,128,128]{2,1,0:T(8,128)(2,1)S(1)} %collective-permute-done.1.kv2_ref) | copy-start | bytes 786436
  42.4 4.2 %copy-start.9 = (bf16[8,128,128]{2,1,0:T(8,128)(2,1)}, bf16[8,128,128]{2,1,0:T(8,128)(2,1)S(1)}, u32[]{:S(2)}) copy-start(bf16[8,128,128]{2,1,0:T(8,128)(2,1)S(1)} %collective-permute-done.kv1_ref) | copy-start | bytes 786436
  42.4 20.5 %all-to-all-start.2 = ((bf16[8,512,128]{2,1,0:T(8,128)(2,1)}), bf16[8,512,128]{2,1,0:T(8,128)(2,1)S(1)}, u32[]{:S(2)}, u32[]{:S(2)}) async-start(bf16[8,512,128]{2,1,0:T(8,128)(2,1)} %pad_maximum_fusion.1), calls=%async_computation.2 | async-start | bytes 2097152 | tf_op jit(solution)/shard_map/all_to_all | solution.py:219
  62.9 6.2 %copy-start.2 = (bf16[8,512,128]{2,1,0:T(8,128)(2,1)}, bf16[8,512,128]{2,1,0:T(8,128)(2,1)S(1)}, u32[]{:S(2)}) copy-start(bf16[8,512,128]{2,1,0:T(8,128)(2,1)S(1)} %all-to-all-done.2.q_ref.grad_ref) | copy-start | bytes 3145732
  62.9 21.8 %all-to-all-start.1 = ((bf16[8,512,128]{2,1,0:T(8,128)(2,1)}), bf16[8,512,128]{2,1,0:T(8,128)(2,1)S(1)}, u32[]{:S(2)}, u32[]{:S(2)}) async-start(bf16[8,512,128]{2,1,0:T(8,128)(2,1)} %get-tuple-element.21), calls=%async_computation.1 | async-start | bytes 2097152 | tf_op jit(solution)/shard_map/all_to_all | solution.py:219
  84.6 12.6 %collective-permute-start.2 = (bf16[8,128,128]{2,1,0:T(8,128)(2,1)}, bf16[8,128,128]{2,1,0:T(8,128)(2,1)S(1)}, u32[]{:S(2)}, u32[]{:S(2)}) collective-permute-start(bf16[8,128,128]{2,1,0:T(8,128)(2,1)} %get-tuple-element.30), channel_id=1, source_target_pairs={{1,0},{2,1},{3,2},{4,3},{5,4},{6,5},{7,6},{8,7},{9,8},{10,9},{11,1... | collective-permute-start | bytes 786440 | tf_op jit(solution)/shard_map/ppermute | solution.py:42
  92.0 26.1 %collective-permute-start.3 = (bf16[8,128,128]{2,1,0:T(8,128)(2,1)}, bf16[8,128,128]{2,1,0:T(8,128)(2,1)S(1)}, u32[]{:S(2)}, u32[]{:S(2)}) collective-permute-start(bf16[8,128,128]{2,1,0:T(8,128)(2,1)} %get-tuple-element.31), channel_id=1, source_target_pairs={{2,0},{3,1},{4,2},{5,3},{6,4},{7,5},{8,6},{9,7},{10,8},{11,9},{12,... | collective-permute-start | bytes 786440 | tf_op jit(solution)/shard_map/ppermute | solution.py:42
  119.8 24.3 %all-to-all-start.3 = ((bf16[8,640,128]{2,1,0:T(8,128)(2,1)}), bf16[8,640,128]{2,1,0:T(8,128)(2,1)S(1)}, u32[]{:S(2)}, u32[]{:S(2)}) async-start(bf16[8,640,128]{2,1,0:T(8,128)(2,1)} %fusion), calls=%async_computation.3 | async-start | bytes 2621440 | tf_op jit(solution)/shard_map/all_to_all | solution.py:219

commit v5 on v3

--- a/solution.py
+++ b/solution.py
@@ -208,8 +208,8 @@
     return pl.BlockSpec((8, 128, HEAD_SIZE), lambda b, s: (0, 0, 0))
 
 
-def params():
-    return pltpu.CompilerParams(dimension_semantics=("arbitrary",), vmem_limit_bytes=60 * 1024 * 1024)
+def params(mebibytes):
+    return pltpu.CompilerParams(dimension_semantics=("arbitrary",), vmem_limit_bytes=mebibytes * 1024 * 1024)
 
 
 def forward(scal, q_in, doc_rows, kv):
@@ -233,7 +233,7 @@
             jax.ShapeDtypeStruct((CELL_BLOCKS, HEAD_SIZE, ROWS), jnp.bfloat16),
             jax.ShapeDtypeStruct((CELL_BLOCKS, 1, ROWS), jnp.float32),
         ],
-        compiler_params=params(),
+        compiler_params=params(60),
         cost_estimate=pl.CostEstimate(flops=4_000_000_000, bytes_accessed=4_000_000, transcendentals=4_000_000),
         name="forward",
     )(scal, q_in, doc_rows, *kv)
@@ -260,7 +260,7 @@
             ],
         ),
         out_shape=[jax.ShapeDtypeStruct((8, ROWS // 2 + 128, HEAD_SIZE), jnp.bfloat16), dkv_shape, dkv_shape, dkv_shape],
-        compiler_params=params(),
+        compiler_params=params(59),
         cost_estimate=pl.CostEstimate(flops=10_000_000_000, bytes_accessed=6_000_000, transcendentals=4_000_000),
         name="backward",
     )(scal, q_in, grad_in, out_t, lse, doc_rows, *kv)
@@ -302,7 +302,8 @@
     first_in = exchanged(jnp.concatenate([by_head(queries), by_head(keys), by_head(values)], axis=1))
     kv0 = first_in[:, 512:, :]
     kv = (kv0, passed_along(kv0, "ctx", 1), passed_along(kv0, "ctx", 2))
-    grad_in = exchanged(by_head(out_grad))
+    grad_rows, *kv = lax.optimization_barrier((by_head(out_grad), *kv))
+    grad_in = exchanged(grad_rows)
     attended_loc, out_t, lse = forward(scal, first_in, doc_rows, kv)
     attended_in = exchanged(attended_loc)
     last_loc, dkv0, dkv1, dkv2 = backward(scal, first_in, grad_in, out_t, lse, doc_rows, kv)

time: 138 us -> 130 us (0.942)
  the two profiles are of different devices: /device:TPU:121 before, /device:TPU:409 now
where the time goes in v5:
time: 130 us
  waiting for transfers between devices  48.7 us (37%)
  starting transfers between devices  42.3 us (33%)
  Pallas kernels  25.2 us (19%)
  local copies, waits for them, and re-layouts  8.09 us (6%)
  other arithmetic  4.56 us (4%)
    all_to_all x4, waiting for transfers between devices, exchanged(): lax.all_to_all(block, 'head', split_axis=0, concat_axis=0, tiled=True)  34.8 us
    all_to_all x4, starting transfers between devices, exchanged(): lax.all_to_all(block, 'head', split_axis=0, concat_axis=0, tiled=True)  24.1 us
    ppermute x4, starting transfers between devices, passed_along(): return lax.ppermute(block, axis, route)  18.2 us
    pallas_call x1, Pallas kernels, backward(): pl.pallas_call(backward_kernel, grid_spec=pltpu.PrefetchScalarGridSpec(nu...  14.5 us
    ppermute x4, waiting for transfers between devices, passed_along(): return lax.ppermute(block, axis, route)  14 us
    pallas_call x1, Pallas kernels, forward(): pl.pallas_call(forward_kernel, grid_spec=pltpu.PrefetchScalarGridSpec(num...  10.7 us
    unnamed x22, local copies, waits for them, and re-layouts  3.43 us
  transfers between devices with their start and end apart: 8, of which 5 were waited for; matrix products, arithmetic and copies ran while one was open for 4% of the time, Pallas kernels for 19%

profile of v5, /device:TPU:409, one launch (start us, length us, event | category | flops | bytes accessed | tf_op | source)
XLA Modules:
  0.0 129.6 jit_solution(3235113996233595097)
XLA Ops:
  0.6 0.0 copy-start
  0.6 0.0 copy-start.5
  0.7 0.0 copy-start.6
  0.7 1.2 copy-done
  1.9 0.2 copy_bitcast_fusion.3
  2.1 0.0 copy-done.5
  2.1 0.0 copy-done.6
  2.1 1.2 pad_maximum_fusion
  3.3 6.7 %all-to-all-start = ((bf16[8,640,128]{2,1,0:T(8,128)(2,1)}), bf16[8,640,128]{2,1,0:T(8,128)(2,1)S(1)}, u32[]{:S(2)}, u32[]{:S(2)}) async-start(bf16[8,640,128]{2,1,0:T(8,128)(2,1)} %pad_maximum_fusion), calls=%async_computation | async-start | bytes 2621440 | tf_op jit(solution)/shard_map/all_to_all | solution.py:276
  10.0 0.0 copy-done.7
  10.0 0.1 fusion.4
  10.1 0.0 copy-done.8
  10.1 0.1 copy.28
  10.2 0.1 reduce-window.9
  10.3 0.1 reduce.1
  10.4 0.1 broadcast_add_fusion.1
  10.5 0.1 select_add_fusion
  10.6 0.2 select_reduce_fusion
  10.8 0.6 sub.51.doc_ref
  11.5 0.1 pad_add_fusion
  11.5 0.2 select_reduce_fusion.1
  11.7 15.0 %all-to-all-done.q_ref = bf16[8,640,128]{2,1,0:T(8,128)(2,1)S(1)} async-done(((bf16[8,640,128]{2,1,0:T(8,128)(2,1)}), bf16[8,640,128]{2,1,0:T(8,128)(2,1)S(1)}, u32[]{:S(2)}, u32[]{:S(2)}) %all-to-all-start) | async-done | bytes 1310752 | tf_op jit(solution)/shard_map/all_to_all | solution.py:276
  26.8 4.0 %collective-permute-start = (bf16[8,128,128]{2,1,0:T(8,128)(2,1)S(1)}, bf16[8,128,128]{2,1,0:T(8,128)(2,1)S(1)}, u32[]{:S(2)}, u32[]{:S(2)}) collective-permute-start(bf16[8,128,128]{2,1,0:T(8,128)(2,1)S(1)} %slice.28.kv0_ref), channel_id=1, source_target_pairs={{0,1},{1,2},{2,3},{3,4},{4,5},{5,6},{6,7},{7,8},{8,9},{9,10},{10,1... | collective-permute-start | bytes 786440 | tf_op jit(solution)/shard_map/ppermute | solution.py:40
  30.8 3.5 %collective-permute-start.1 = (bf16[8,128,128]{2,1,0:T(8,128)(2,1)S(1)}, bf16[8,128,128]{2,1,0:T(8,128)(2,1)}, u32[]{:S(2)}, u32[]{:S(2)}) collective-permute-start(bf16[8,128,128]{2,1,0:T(8,128)(2,1)S(1)} %slice.28.kv0_ref), channel_id=1, source_target_pairs={{0,2},{1,3},{2,4},{3,5},{4,6},{5,7},{6,8},{7,9},{8,10},{9,11},{10,... | collective-permute-start | bytes 786440 | tf_op jit(solution)/shard_map/ppermute | solution.py:40
  34.3 1.2 copy_bitcast_fusion.2
  35.5 0.0 collective-permute-done.kv1_ref
  35.5 0.7 copy-done.9
  36.2 7.4 %collective-permute-done.1.kv2_ref = bf16[8,128,128]{2,1,0:T(8,128)(2,1)} collective-permute-done((bf16[8,128,128]{2,1,0:T(8,128)(2,1)S(1)}, bf16[8,128,128]{2,1,0:T(8,128)(2,1)}, u32[]{:S(2)}, u32[]{:S(2)}) %collective-permute-start.1) | collective-permute-done | bytes 262176 | tf_op jit(solution)/shard_map/ppermute | solution.py:40
  43.6 0.0 copy-done.1
  43.6 4.8 %all-to-all-start.2 = ((bf16[8,512,128]{2,1,0:T(8,128)(2,1)}), bf16[8,512,128]{2,1,0:T(8,128)(2,1)S(1)}, u32[]{:S(2)}, u32[]{:S(2)}) async-start(bf16[8,512,128]{2,1,0:T(8,128)(2,1)} %copy_bitcast_fusion.2), calls=%async_computation.2 | async-start | bytes 2097152 | tf_op jit(solution)/shard_map/all_to_all | solution.py:276
  48.4 0.1 and_select_fusion
  48.5 0.6 pad_add_fusion.1.scal_ref
  49.1 10.7 %forward.1 = (bf16[8,512,128]{2,1,0:T(8,128)(2,1)}, bf16[4,128,1024]{2,1,0:T(8,128)(2,1)}, f32[4,1,1024]{2,1,0:T(1,128)}) custom-call(s32[24]{0:T(128)} %pad_add_fusion.1.scal_ref, bf16[8,640,128]{2,1,0:T(8,128)(2,1)} %copy-done.1, s32[4,1,1024]{2,1,0:T(1,128)} %sub.51.doc_ref, bf16[8,128,128]{2,1,0:T(8,128)(2,1)} %copy-done.4, ...), custom_call_target="tpu_custom_call" | custom-call | flops 4000000000 | bytes 4000000 | tf_op jit(solution)/shard_map/forward/pallas_call | solution.py:216
  59.7 2.9 %all-to-all-done.2.grad_ref = bf16[8,512,128]{2,1,0:T(8,128)(2,1)S(1)} async-done(((bf16[8,512,128]{2,1,0:T(8,128)(2,1)}), bf16[8,512,128]{2,1,0:T(8,128)(2,1)S(1)}, u32[]{:S(2)}, u32[]{:S(2)}) %all-to-all-start.2) | async-done | bytes 1048608 | tf_op jit(solution)/shard_map/all_to_all | solution.py:276
  62.6 5.9 %all-to-all-start.1 = ((bf16[8,512,128]{2,1,0:T(8,128)(2,1)}), bf16[8,512,128]{2,1,0:T(8,128)(2,1)S(1)}, u32[]{:S(2)}, u32[]{:S(2)}) async-start(bf16[8,512,128]{2,1,0:T(8,128)(2,1)} %get-tuple-element.21), calls=%async_computation.1 | async-start | bytes 2097152 | tf_op jit(solution)/shard_map/all_to_all | solution.py:276
  68.5 14.5 %backward.1 = (bf16[8,640,128]{2,1,0:T(8,128)(2,1)}, bf16[8,128,128]{2,1,0:T(8,128)(2,1)}, bf16[8,128,128]{2,1,0:T(8,128)(2,1)}, bf16[8,128,128]{2,1,0:T(8,128)(2,1)}) custom-call(s32[24]{0:T(128)} %pad_add_fusion.1.scal_ref, bf16[8,640,128]{2,1,0:T(8,128)(2,1)} %copy-done.1, bf16[8,512,128]{2,1,0:T(8,128)(2,1)} %copy-done.3, ...), custom_call_target="tpu_custom_call" | custom-call | flops 10000000000 | bytes 6000000 | tf_op jit(solution)/shard_map/backward/pallas_call | solution.py:244
  83.0 0.0 all-to-all-done.1
  83.0 2.9 %collective-permute-start.3 = (bf16[8,128,128]{2,1,0:T(8,128)(2,1)}, bf16[8,128,128]{2,1,0:T(8,128)(2,1)S(1)}, u32[]{:S(2)}, u32[]{:S(2)}) collective-permute-start(bf16[8,128,128]{2,1,0:T(8,128)(2,1)} %get-tuple-element.31), channel_id=1, source_target_pairs={{2,0},{3,1},{4,2},{5,3},{6,4},{7,5},{8,6},{9,7},{10,8},{11,9},{12,... | collective-permute-start | bytes 786440 | tf_op jit(solution)/shard_map/ppermute | solution.py:40
  85.9 7.8 %collective-permute-start.2 = (bf16[8,128,128]{2,1,0:T(8,128)(2,1)}, bf16[8,128,128]{2,1,0:T(8,128)(2,1)S(1)}, u32[]{:S(2)}, u32[]{:S(2)}) collective-permute-start(bf16[8,128,128]{2,1,0:T(8,128)(2,1)} %get-tuple-element.30), channel_id=1, source_target_pairs={{1,0},{2,1},{3,2},{4,3},{5,4},{6,5},{7,6},{8,7},{9,8},{10,9},{11,1... | collective-permute-start | bytes 786440 | tf_op jit(solution)/shard_map/ppermute | solution.py:40
  93.7 0.0 collective-permute-done.3
  93.7 6.6 %collective-permute-done.2 = bf16[8,128,128]{2,1,0:T(8,128)(2,1)S(1)} collective-permute-done((bf16[8,128,128]{2,1,0:T(8,128)(2,1)}, bf16[8,128,128]{2,1,0:T(8,128)(2,1)S(1)}, u32[]{:S(2)}, u32[]{:S(2)}) %collective-permute-start.2) | collective-permute-done | bytes 262176 | tf_op jit(solution)/shard_map/ppermute | solution.py:40
  100.3 1.8 %fusion = bf16[8,640,128]{2,1,0:T(8,128)(2,1)} fusion(bf16[8,640,128]{2,1,0:T(8,128)(2,1)} %get-tuple-element.28, bf16[8,128,128]{2,1,0:T(8,128)(2,1)S(1)} %collective-permute-done.3, bf16[8,128,128]{2,1,0:T(8,128)(2,1)S(1)} %collective-permute-done.2, bf16[8,128,128]{2,1,0:T(8,128)(2,1)} %get-tuple-element.29), kind=kLoop, calls=%fused_computation.8 | loop fusion | flops 786432 | bytes 1048576 | tf_op jit(solution)/shard_map/dynamic_update_slice | solution.py:313
  102.1 6.6 %all-to-all-start.3 = ((bf16[8,640,128]{2,1,0:T(8,128)(2,1)}), bf16[8,640,128]{2,1,0:T(8,128)(2,1)S(1)}, u32[]{:S(2)}, u32[]{:S(2)}) async-start(bf16[8,640,128]{2,1,0:T(8,128)(2,1)} %fusion), calls=%async_computation.3 | async-start | bytes 2621440 | tf_op jit(solution)/shard_map/all_to_all | solution.py:276
  108.7 1.3 copy_bitcast_fusion.1
  110.0 16.9 %all-to-all-done.3 = bf16[8,640,128]{2,1,0:T(8,128)(2,1)S(1)} async-done(((bf16[8,640,128]{2,1,0:T(8,128)(2,1)}), bf16[8,640,128]{2,1,0:T(8,128)(2,1)S(1)}, u32[]{:S(2)}, u32[]{:S(2)}) %all-to-all-start.3) | async-done | bytes 1310752 | tf_op jit(solution)/shard_map/all_to_all | solution.py:276
  126.9 0.7 copy.35
  127.6 0.7 copy.36
  128.4 1.3 copy_bitcast_fusion
  (18 shorter events, 0.1 us)
Async XLA Ops:
  0.6 1.2 copy-start
  0.6 1.4 %copy-start.5 = (bf16[64,8,128]{2,1,0:T(8,128)(2,1)S(1)}, bf16[64,8,128]{2,1,0:T(8,128)(2,1)}, u32[]{:S(2)}) copy-start(bf16[64,8,128]{2,1,0:T(8,128)(2,1)} %param.8) | copy-start | bytes 393220
  0.7 1.4 %copy-start.6 = (bf16[64,8,128]{2,1,0:T(8,128)(2,1)S(1)}, bf16[64,8,128]{2,1,0:T(8,128)(2,1)}, u32[]{:S(2)}) copy-start(bf16[64,8,128]{2,1,0:T(8,128)(2,1)} %param.7) | copy-start | bytes 393220
  3.3 6.7 %copy-start.7 = (s32[256]{0:T(256)S(1)}, s32[256]{0:T(256)}, u32[]{:S(2)}) copy-start(s32[256]{0:T(256)} %param.11) | copy-start | bytes 3076
  3.3 6.8 %copy-start.8 = (s32[48]{0:T(128)S(1)}, s32[48]{0:T(128)}, u32[]{:S(2)}) copy-start(s32[48]{0:T(128)} %param.10) | copy-start | bytes 580
  3.3 31.0 %copy-start.2 = (bf16[64,64,128]{2,1,0:T(8,128)(2,1)S(1)}, bf16[64,64,128]{2,1,0:T(8,128)(2,1)}, u32[]{:S(2)}) copy-start(bf16[64,64,128]{2,1,0:T(8,128)(2,1)} %param.9) | copy-start | bytes 3145732
  3.3 23.4 %all-to-all-start = ((bf16[8,640,128]{2,1,0:T(8,128)(2,1)}), bf16[8,640,128]{2,1,0:T(8,128)(2,1)S(1)}, u32[]{:S(2)}, u32[]{:S(2)}) async-start(bf16[8,640,128]{2,1,0:T(8,128)(2,1)} %pad_maximum_fusion), calls=%async_computation | async-start | bytes 2621440 | tf_op jit(solution)/shard_map/all_to_all | solution.py:276
  26.7 16.8 %copy-start.1 = (bf16[8,640,128]{2,1,0:T(8,128)(2,1)}, bf16[8,640,128]{2,1,0:T(8,128)(2,1)S(1)}, u32[]{:S(2)}) copy-start(bf16[8,640,128]{2,1,0:T(8,128)(2,1)S(1)} %all-to-all-done.q_ref) | copy-start | bytes 3932164
  26.8 8.7 %copy-start.4 = (bf16[8,128,128]{2,1,0:T(8,128)(2,1)}, bf16[8,128,128]{2,1,0:T(8,128)(2,1)S(1)}, u32[]{:S(2)}) copy-start(bf16[8,128,128]{2,1,0:T(8,128)(2,1)S(1)} %slice.28.kv0_ref) | copy-start | bytes 786436
  26.8 8.7 %collective-permute-start = (bf16[8,128,128]{2,1,0:T(8,128)(2,1)S(1)}, bf16[8,128,128]{2,1,0:T(8,128)(2,1)S(1)}, u32[]{:S(2)}, u32[]{:S(2)}) collective-permute-start(bf16[8,128,128]{2,1,0:T(8,128)(2,1)S(1)} %slice.28.kv0_ref), channel_id=1, source_target_pairs={{0,1},{1,2},{2,3},{3,4},{4,5},{5,6},{6,7},{7,8},{8,9},{9,10},{10,1... | collective-permute-start | bytes 786440 | tf_op jit(solution)/shard_map/ppermute | solution.py:40
  30.8 12.8 %collective-permute-start.1 = (bf16[8,128,128]{2,1,0:T(8,128)(2,1)S(1)}, bf16[8,128,128]{2,1,0:T(8,128)(2,1)}, u32[]{:S(2)}, u32[]{:S(2)}) collective-permute-start(bf16[8,128,128]{2,1,0:T(8,128)(2,1)S(1)} %slice.28.kv0_ref), channel_id=1, source_target_pairs={{0,2},{1,3},{2,4},{3,5},{4,6},{5,7},{6,8},{7,9},{8,10},{9,11},{10,... | collective-permute-start | bytes 786440 | tf_op jit(solution)/shard_map/ppermute | solution.py:40
  35.5 0.7 copy-start.9
  43.6 19.0 %all-to-all-start.2 = ((bf16[8,512,128]{2,1,0:T(8,128)(2,1)}), bf16[8,512,128]{2,1,0:T(8,128)(2,1)S(1)}, u32[]{:S(2)}, u32[]{:S(2)}) async-start(bf16[8,512,128]{2,1,0:T(8,128)(2,1)} %copy_bitcast_fusion.2), calls=%async_computation.2 | async-start | bytes 2097152 | tf_op jit(solution)/shard_map/all_to_all | solution.py:276
  62.6 5.9 %copy-start.3 = (bf16[8,512,128]{2,1,0:T(8,128)(2,1)}, bf16[8,512,128]{2,1,0:T(8,128)(2,1)S(1)}, u32[]{:S(2)}) copy-start(bf16[8,512,128]{2,1,0:T(8,128)(2,1)S(1)} %all-to-all-done.2.grad_ref) | copy-start | bytes 3145732
  62.6 20.4 %all-to-all-start.1 = ((bf16[8,512,128]{2,1,0:T(8,128)(2,1)}), bf16[8,512,128]{2,1,0:T(8,128)(2,1)S(1)}, u32[]{:S(2)}, u32[]{:S(2)}) async-start(bf16[8,512,128]{2,1,0:T(8,128)(2,1)} %get-tuple-element.21), calls=%async_computation.1 | async-start | bytes 2097152 | tf_op jit(solution)/shard_map/all_to_all | solution.py:276
  83.0 10.7 %collective-permute-start.3 = (bf16[8,128,128]{2,1,0:T(8,128)(2,1)}, bf16[8,128,128]{2,1,0:T(8,128)(2,1)S(1)}, u32[]{:S(2)}, u32[]{:S(2)}) collective-permute-start(bf16[8,128,128]{2,1,0:T(8,128)(2,1)} %get-tuple-element.31), channel_id=1, source_target_pairs={{2,0},{3,1},{4,2},{5,3},{6,4},{7,5},{8,6},{9,7},{10,8},{11,9},{12,... | collective-permute-start | bytes 786440 | tf_op jit(solution)/shard_map/ppermute | solution.py:40
  85.9 14.4 %collective-permute-start.2 = (bf16[8,128,128]{2,1,0:T(8,128)(2,1)}, bf16[8,128,128]{2,1,0:T(8,128)(2,1)S(1)}, u32[]{:S(2)}, u32[]{:S(2)}) collective-permute-start(bf16[8,128,128]{2,1,0:T(8,128)(2,1)} %get-tuple-element.30), channel_id=1, source_target_pairs={{1,0},{2,1},{3,2},{4,3},{5,4},{6,5},{7,6},{8,7},{9,8},{10,9},{11,1... | collective-permute-start | bytes 786440 | tf_op jit(solution)/shard_map/ppermute | solution.py:40
  102.1 24.8 %all-to-all-start.3 = ((bf16[8,640,128]{2,1,0:T(8,128)(2,1)}), bf16[8,640,128]{2,1,0:T(8,128)(2,1)S(1)}, u32[]{:S(2)}, u32[]{:S(2)}) async-start(bf16[8,640,128]{2,1,0:T(8,128)(2,1)} %fusion), calls=%async_computation.3 | async-start | bytes 2621440 | tf_op jit(solution)/shard_map/all_to_all | solution.py:276

commit v6 on v4

v6 whole, which is shorter than its diff:
```python
import functools
import math

import jax
import jax.numpy as jnp
from jax import lax
from jax.experimental import pallas as pl
from jax.experimental.pallas import tpu as pltpu
from jax.sharding import PartitionSpec as P

HEAD_SIZE = 128
BLOCK = 128
CELL_BLOCKS = 4
SLOTS = 3
WINDOW_BLOCKS = SLOTS * CELL_BLOCKS
WINDOW = WINDOW_BLOCKS * BLOCK
CHUNK = 2 * BLOCK
PADDED = WINDOW + BLOCK
REACH = 10 * BLOCK
SHARE = 8
HALF = 64 * SHARE
ROWS = 2 * HALF

SCALE = HEAD_SIZE ** (-0.5)
EXP2_SCALE = SCALE * math.log2(math.e)
NEG_BIG = -1e30

NT = (((1,), (1,)), ((), ()))
NN = (((1,), (0,)), ((), ()))
TN = (((0,), (0,)), ((), ()))


def dot(a, b, dims=NN):
    return lax.dot_general(a, b, dims, preferred_element_type=jnp.float32)


def passed_along(block, axis, distance):
    devices = range(lax.axis_size(axis))
    route = [(i - distance, i) for i in devices if i - distance in devices]
    return lax.ppermute(block, axis, route)


def stored_rows(kv_ref, block, which):
    first = kv_ref[2 * block, pl.ds(64 * which, 64), :]
    second = kv_ref[2 * block + 1, pl.ds(64 * which, 64), :]
    return jnp.concatenate([first, second], axis=0)


def window_start(scal_ref, slot, block):
    index = (SLOTS - 1 - slot) * CELL_BLOCKS + block
    return pl.multiple_of(scal_ref[index] * BLOCK, BLOCK)


def allowed_tile(key_start, count, first_block, doc_start, tile):
    lane = lax.broadcasted_iota(jnp.int32, (1, HALF), 1) + tile * HALF
    query_pos = first_block * BLOCK + lax.shift_right_logical(lane, 3)
    key_pos = lax.broadcasted_iota(jnp.int32, (count, HALF), 0)
    return (key_pos >= doc_start - key_start) & (key_pos <= query_pos - key_start)


def attention_kernel(scal_ref, q_ref, grad_ref, doc_ref, kv0_ref, kv1_ref, kv2_ref, out_ref, dkv0_ref, dkv1_ref, dkv2_ref, key_seq, value_seq, value_t, scores, acc, top, dq_acc, dk_acc, dv_acc, weights_low, grads_low):
    step = pl.program_id(0)

    @pl.when(step == 0)
    def _():
        for slot, kv_ref in enumerate((kv0_ref, kv1_ref, kv2_ref)):
            for block in range(CELL_BLOCKS):
                start = window_start(scal_ref, slot, block)
                key_seq[pl.ds(start, BLOCK), :] = stored_rows(kv_ref, block, 0)
                value = stored_rows(kv_ref, block, 1)
                value_seq[pl.ds(start, BLOCK), :] = value
                value_t[:, pl.ds(start, BLOCK)] = value.astype(jnp.float32).T.astype(jnp.bfloat16)
        zeros = jnp.zeros((BLOCK, HEAD_SIZE), jnp.bfloat16)
        key_seq[pl.ds(WINDOW, BLOCK), :] = zeros
        value_seq[pl.ds(WINDOW, BLOCK), :] = zeros
        value_t[:, pl.ds(WINDOW, BLOCK)] = zeros
        dk_acc[...] = jnp.zeros_like(dk_acc)
        dv_acc[...] = jnp.zeros_like(dv_acc)

    first_block = scal_ref[WINDOW_BLOCKS + step]
    low_block = scal_ref[WINDOW_BLOCKS + CELL_BLOCKS + step]
    last_start = scal_ref[WINDOW_BLOCKS + 2 * CELL_BLOCKS + step]
    chunks = lax.shift_right_logical(first_block - low_block + 2, 1)
    pairs = lax.shift_right_logical(chunks, 1)
    top[...] = jnp.full_like(top, NEG_BIG)
    acc[...] = jnp.zeros_like(acc)
    dq_acc[...] = jnp.zeros_like(dq_acc)

    def span(turn, count):
        key_start = pl.multiple_of((low_block + 4 * turn) * BLOCK, BLOCK)
        return key_start, pl.ds(key_start, count), pl.ds(pl.multiple_of(turn * 2 * CHUNK, CHUNK), count)

    def score(turn, count, masked):
        key_start, window, rows = span(turn, count)
        for tile in range(2):
            cols = slice(tile * HALF, (tile + 1) * HALF)
            raw = dot(key_seq[window, :], q_ref[tile], NT)
            if masked:
                allowed = allowed_tile(key_start, count, first_block, doc_ref[0, :, cols], tile)
                raw = jnp.where(allowed, raw, NEG_BIG)
            scores[rows, cols] = raw
            top[:, cols] = jnp.maximum(top[:, cols], jnp.max(raw.reshape(count // 8, 8, HALF), axis=0))

    def score_pair(turn, _):
        key_start = (low_block + 4 * turn) * BLOCK
        whole = (key_start >= last_start) & (key_start + 2 * CHUNK <= first_block * BLOCK)
        pl.when(whole)(lambda: score(turn, 2 * CHUNK, False))
        pl.when(jnp.logical_not(whole))(lambda: score(turn, 2 * CHUNK, True))
        return 0

    lax.fori_loop(0, pairs, score_pair, 0)
    pl.when(chunks > 2 * pairs)(lambda: score(pairs, CHUNK, True))
    highest = jnp.max(top[...], axis=0, keepdims=True) * EXP2_SCALE
    top[...] = jnp.zeros_like(top)

    def weigh(turn, count):
        _, window, rows = span(turn, count)
        for tile in range(2):
            cols = slice(tile * HALF, (tile + 1) * HALF)
            weights = jnp.exp2(scores[rows, cols] * EXP2_SCALE - highest[:, cols])
            top[:, cols] += jnp.sum(weights.reshape(count // 8, 8, HALF), axis=0)
            acc[:, cols] += dot(value_t[:, window], weights.astype(jnp.bfloat16))

    def weigh_pair(turn, _):
        weigh(turn, 2 * CHUNK)
        return 0

    lax.fori_loop(0, pairs, weigh_pair, 0)
    pl.when(chunks > 2 * pairs)(lambda: weigh(pairs, CHUNK))
    total = jnp.sum(top[...], axis=0, keepdims=True)
    lse = highest + jnp.log2(total)
    out = (acc[...] * (1.0 / total)).T.astype(jnp.bfloat16)
    out_ref[:, :HALF, :] = out.reshape(2, HALF, HEAD_SIZE)
    delta = jnp.sum((out.astype(jnp.float32) * grad_ref[...].reshape(ROWS, HEAD_SIZE).astype(jnp.float32)).T, axis=0, keepdims=True)

    def grad_chunk(turn, _):
        window = pl.ds(pl.multiple_of((low_block + 2 * turn) * BLOCK, BLOCK), CHUNK)
        rows = pl.ds(pl.multiple_of(turn * CHUNK, CHUNK), CHUNK)
        keys = key_seq[window, :]
        for tile in range(2):
            cols = slice(tile * HALF, (tile + 1) * HALF)
            weights = jnp.exp2(scores[rows, cols] * EXP2_SCALE - lse[:, cols])
            weights_low[:, cols] = weights.astype(jnp.bfloat16)
            sent = dot(value_seq[window, :], grad_ref[tile], NT)
            grads_low[:, cols] = (weights * (sent - delta[:, cols])).astype(jnp.bfloat16)
        dq_acc[...] += dot(grads_low[...], keys, TN)
        dk_acc[window, :] += dot(grads_low[...], q_ref[...].reshape(ROWS, HEAD_SIZE))
        dv_acc[window, :] += dot(weights_low[...], grad_ref[...].reshape(ROWS, HEAD_SIZE))
        return 0

    lax.fori_loop(0, chunks, grad_chunk, 0)
    query_grad = (dq_acc[...] * SCALE).astype(jnp.bfloat16)
    out_ref[:, HALF:, :] = query_grad.reshape(2, HALF, HEAD_SIZE)

    @pl.when(step == CELL_BLOCKS - 1)
    def _():
        for slot, dkv_ref in enumerate((dkv0_ref, dkv1_ref, dkv2_ref)):
            for block in range(CELL_BLOCKS):
                start = window_start(scal_ref, slot, block)
                dk = (dk_acc[pl.ds(start, BLOCK), :] * SCALE).astype(jnp.bfloat16)
                dv = dv_acc[pl.ds(start, BLOCK), :].astype(jnp.bfloat16)
                for half in range(2):
                    rows = slice(half * 64, (half + 1) * 64)
                    dkv_ref[2 * block + half, pl.ds(0, 64), :] = dk[rows]
                    dkv_ref[2 * block + half, pl.ds(64, 64), :] = dv[rows]


def attention(scal, rows_in, doc_rows, kv):
    def row_spec(place):
        return pl.BlockSpec((2, HALF, HEAD_SIZE), lambda b, s: (b, place, 0))

    kv_spec = pl.BlockSpec((8, 128, HEAD_SIZE), lambda b, s: (0, 0, 0))
    return pl.pallas_call(
        attention_kernel,
        grid_spec=pltpu.PrefetchScalarGridSpec(
            num_scalar_prefetch=1,
            grid=(CELL_BLOCKS,),
            in_specs=[row_spec(0), row_spec(1), pl.BlockSpec((1, 1, ROWS), lambda b, s: (b, 0, 0))] + [kv_spec] * 3,
            out_specs=[pl.BlockSpec((2, 2 * HALF, HEAD_SIZE), lambda b, s: (b, 0, 0))] + [kv_spec] * 3,
            scratch_shapes=[
                pltpu.VMEM((PADDED, HEAD_SIZE), jnp.bfloat16),
                pltpu.VMEM((PADDED, HEAD_SIZE), jnp.bfloat16),
                pltpu.VMEM((HEAD_SIZE, PADDED), jnp.bfloat16),
                pltpu.VMEM((REACH, ROWS), jnp.float32),
                pltpu.VMEM((HEAD_SIZE, ROWS), jnp.float32),
                pltpu.VMEM((8, ROWS), jnp.float32),
                pltpu.VMEM((ROWS, HEAD_SIZE), jnp.float32),
                pltpu.VMEM((PADDED, HEAD_SIZE), jnp.float32),
                pltpu.VMEM((PADDED, HEAD_SIZE), jnp.float32),
                pltpu.VMEM((CHUNK, ROWS), jnp.bfloat16),
                pltpu.VMEM((CHUNK, ROWS), jnp.bfloat16),
            ],
        ),
        out_shape=[jax.ShapeDtypeStruct((8, 2 * HALF + 128, HEAD_SIZE), jnp.bfloat16)] + [jax.ShapeDtypeStruct((8, 128, HEAD_SIZE), jnp.bfloat16)] * 3,
        compiler_params=pltpu.CompilerParams(dimension_semantics=("arbitrary",), vmem_limit_bytes=60 * 1024 * 1024),
        cost_estimate=pl.CostEstimate(flops=10_000_000_000, bytes_accessed=6_000_000, transcendentals=4_000_000),
        name="attention",
    )(scal, rows_in, rows_in, doc_rows, *kv)


def by_head(rows):
    tokens = rows.shape[0]
    split = rows.reshape(tokens, 8, -1, HEAD_SIZE).transpose(1, 0, 2, 3)
    return split.reshape(8, -1, HEAD_SIZE)


def exchanged(block):
    return lax.all_to_all(block, "head", split_axis=0, concat_axis=0, tiled=True)


def plan(doc_lengths, stored_block_order):
    cell = lax.axis_index("ctx")
    starts = jnp.cumsum(doc_lengths) - doc_lengths
    window_first = (cell - (SLOTS - 1)) * CELL_BLOCKS
    padded = jnp.pad(stored_block_order, (WINDOW_BLOCKS - CELL_BLOCKS, 0))
    window_order = lax.dynamic_slice_in_dim(padded, cell * CELL_BLOCKS, WINDOW_BLOCKS, 0)
    base = jnp.arange(WINDOW_BLOCKS, dtype=jnp.int32) // CELL_BLOCKS * CELL_BLOCKS
    place = base + window_order % CELL_BLOCKS
    own_place = place[WINDOW_BLOCKS - CELL_BLOCKS :]
    own_block = window_first + own_place
    token = lax.broadcasted_iota(jnp.int32, (CELL_BLOCKS, 1, ROWS), 2) // SHARE
    pos = own_block[:, None, None] * BLOCK + token
    begun = starts <= pos[..., None]
    doc_start = jnp.max(jnp.where(begun, starts, 0), axis=-1)
    doc_rows = (doc_start - window_first * BLOCK).astype(jnp.int32)
    edges = jnp.concatenate([own_block * BLOCK, own_block * BLOCK + BLOCK - 1])
    low = jnp.max(jnp.where(starts <= edges[:, None], starts, 0), axis=-1) - window_first * BLOCK
    scal = jnp.concatenate([place, own_place, low[:CELL_BLOCKS] // BLOCK, low[CELL_BLOCKS:]]).astype(jnp.int32)
    return scal, doc_rows


def body(queries, keys, values, out_grad, doc_lengths, stored_block_order):
    scal, doc_rows = plan(doc_lengths, stored_block_order)
    first_in = exchanged(jnp.concatenate([by_head(queries), by_head(out_grad), by_head(keys), by_head(values)], axis=1))
    kv0 = first_in[:, 2 * HALF :, :]
    kv = (kv0, passed_along(kv0, "ctx", 1), passed_along(kv0, "ctx", 2))
    rows_out, dkv0, dkv1, dkv2 = attention(scal, first_in, doc_rows, kv)
    near, far = passed_along(dkv1, "ctx", -1), passed_along(dkv2, "ctx", -2)
    summed = dkv0.astype(jnp.float32) + near.astype(jnp.float32) + far.astype(jnp.float32)
    rows_out = lax.dynamic_update_slice(rows_out, summed.astype(jnp.bfloat16), (0, 2 * HALF, 0))
    back = exchanged(rows_out)
    tokens = queries.shape[0]

    def by_token(block, heads):
        return block.reshape(8, tokens, heads, HEAD_SIZE).transpose(1, 0, 2, 3).reshape(tokens, -1, HEAD_SIZE)

    attended, query_grad = by_token(back[:, :HALF], SHARE), by_token(back[:, HALF : 2 * HALF], SHARE)
    key_gradient = by_token(back[:, 2 * HALF : 2 * HALF + 64], 1)
    value_gradient = by_token(back[:, 2 * HALF + 64 :], 1)
    return attended, query_grad, key_gradient, value_gradient


def solution(mesh):
    spec = P(("ctx", "head"), None, None)
    return jax.shard_map(
        body,
        mesh=mesh,
        in_specs=(spec, spec, spec, spec, P(), P()),
        out_specs=(spec, spec, spec, spec),
        check_vma=False,
    )
```

time: 149 us -> 141 us (0.946)
  the two profiles are of different devices: /device:TPU:98 before, /device:TPU:226 now
where the time goes in v6:
time: 141 us
  waiting for transfers between devices  48.4 us (34%)
  blocking collectives  35.3 us (25%)
  starting transfers between devices  23.5 us (17%)
  Pallas kernels  20 us (14%)
  local copies, waits for them, and re-layouts  8.05 us (6%)
  other arithmetic  4.94 us (4%)
    all_to_all x1, blocking collectives, exchanged(): lax.all_to_all(block, 'head', split_axis=0, concat_axis=0, tiled=True)  35.3 us
    all_to_all x1, waiting for transfers between devices, exchanged(): lax.all_to_all(block, 'head', split_axis=0, concat_axis=0, tiled=True)  27.5 us
    ppermute x4, waiting for transfers between devices, passed_along(): return lax.ppermute(block, axis, route)  20.9 us
    pallas_call x1, Pallas kernels, attention(): pl.pallas_call(attention_kernel, grid_spec=pltpu.PrefetchScalarGridSpec(n...  20 us
    ppermute x4, starting transfers between devices, passed_along(): return lax.ppermute(block, axis, route)  17.4 us
    all_to_all x1, starting transfers between devices, exchanged(): lax.all_to_all(block, 'head', split_axis=0, concat_axis=0, tiled=True)  6.16 us
    reshape x2, local copies, waits for them, and re-layouts, by_head(): return split.reshape(8, -1, HEAD_SIZE)  2.83 us
  transfers between devices with their start and end apart: 5, of which 5 were waited for; matrix products, arithmetic and copies ran while one was open for 2% of the time, Pallas kernels for 0%

profile of v6, /device:TPU:226, one launch (start us, length us, event | category | flops | bytes accessed | tf_op | source)
XLA Modules:
  0.0 141.0 jit_solution(2304544783707007480)
XLA Ops:
  0.6 0.0 copy-start
  0.6 1.1 copy_bitcast_fusion.4
  1.8 0.2 copy-done
  2.0 1.7 %copy_bitcast_fusion.2 = (bf16[8,512,128]{2,1,0:T(8,128)(2,1)S(1)}, bf16[8,512,128]{2,1,0:T(8,128)(2,1)S(1)}) fusion(bf16[64,64,128]{2,1,0:T(8,128)(2,1)S(1)} %copy-done, bf16[64,64,128]{2,1,0:T(8,128)(2,1)} %param.9), kind=kLoop, calls=%fused_computation.5 | loop fusion | bytes 4194304 | tf_op jit(solution)/shard_map/reshape | solution.py:204
  3.7 1.5 %pad_maximum_fusion = bf16[8,1152,128]{2,1,0:T(8,128)(2,1)} fusion(bf16[8,64,128]{2,1,0:T(8,128)(2,1)S(1)} %get-tuple-element.35, bf16[8,64,128]{2,1,0:T(8,128)(2,1)S(1)} %get-tuple-element.36, bf16[8,512,128]{2,1,0:T(8,128)(2,1)S(1)} %get-tuple-element.33, bf16[8,512,128]{2,1,0:T(8,128)(2,1)S(1)} %get-tuple-element.34), kind=kLoop, calls=%fused_computation | loop fusion | flops 9437184 | bytes 4718592 | tf_op jit(solution)/shard_map/concatenate | solution.py:234
  5.2 0.0 copy-start.4
  5.2 0.0 copy-start.3
  5.2 6.2 %all-to-all-start = ((bf16[8,1152,128]{2,1,0:T(8,128)(2,1)}), bf16[8,1152,128]{2,1,0:T(8,128)(2,1)S(1)}, u32[]{:S(2)}, u32[]{:S(2)}) async-start(bf16[8,1152,128]{2,1,0:T(8,128)(2,1)} %pad_maximum_fusion), calls=%async_computation | async-start | bytes 4718592 | tf_op jit(solution)/shard_map/all_to_all | solution.py:208
  11.4 0.0 copy-done.4
  11.4 0.1 copy.28
  11.5 0.1 reduce-window.9
  11.6 0.1 reduce.1
  11.7 0.0 copy-done.3
  11.7 0.1 fusion.4
  11.8 0.1 broadcast_add_fusion.1
  11.9 0.1 select_add_fusion
  12.0 0.2 select_reduce_fusion
  12.2 0.6 sub.51.doc_ref
  12.8 0.1 pad_add_fusion
  12.9 0.2 select_reduce_fusion.1
  13.1 27.5 %all-to-all-done.q_ref.grad_ref = bf16[8,1152,128]{2,1,0:T(8,128)(2,1)S(1)} async-done(((bf16[8,1152,128]{2,1,0:T(8,128)(2,1)}), bf16[8,1152,128]{2,1,0:T(8,128)(2,1)S(1)}, u32[]{:S(2)}, u32[]{:S(2)}) %all-to-all-start) | async-done | bytes 2359328 | tf_op jit(solution)/shard_map/all_to_all | solution.py:208
  40.6 0.0 copy-start.1
  40.7 0.0 copy-start.2
  40.7 5.9 %collective-permute-start.1 = (bf16[8,128,128]{2,1,0:T(8,128)(2,1)S(1)}, bf16[8,128,128]{2,1,0:T(8,128)(2,1)S(1)}, u32[]{:S(2)}, u32[]{:S(2)}) collective-permute-start(bf16[8,128,128]{2,1,0:T(8,128)(2,1)S(1)} %slice.32.kv0_ref), channel_id=1, source_target_pairs={{0,2},{1,3},{2,4},{3,5},{4,6},{5,7},{6,8},{7,9},{8,10},{9,11},{10,... | collective-permute-start | bytes 786440 | tf_op jit(solution)/shard_map/ppermute | solution.py:40
  46.6 1.9 %collective-permute-start = (bf16[8,128,128]{2,1,0:T(8,128)(2,1)S(1)}, bf16[8,128,128]{2,1,0:T(8,128)(2,1)}, u32[]{:S(2)}, u32[]{:S(2)}) collective-permute-start(bf16[8,128,128]{2,1,0:T(8,128)(2,1)S(1)} %slice.32.kv0_ref), channel_id=1, source_target_pairs={{0,1},{1,2},{2,3},{3,4},{4,5},{5,6},{6,7},{7,8},{8,9},{9,10},{10,1... | collective-permute-start | bytes 786440 | tf_op jit(solution)/shard_map/ppermute | solution.py:40
  48.5 0.1 and_select_fusion
  48.6 0.6 pad_add_fusion.1.scal_ref
  49.2 4.1 %collective-permute-done.1.kv2_ref = bf16[8,128,128]{2,1,0:T(8,128)(2,1)S(1)} collective-permute-done((bf16[8,128,128]{2,1,0:T(8,128)(2,1)S(1)}, bf16[8,128,128]{2,1,0:T(8,128)(2,1)S(1)}, u32[]{:S(2)}, u32[]{:S(2)}) %collective-permute-start.1) | collective-permute-done | bytes 262176 | tf_op jit(solution)/shard_map/ppermute | solution.py:40
  53.3 0.0 copy-start.5
  53.3 1.1 collective-permute-done.kv1_ref
  54.4 0.0 copy-done.1
  54.4 0.0 copy-done.2
  54.4 0.0 copy-done.5
  54.4 20.0 %attention.1 = (bf16[8,1152,128]{2,1,0:T(8,128)(2,1)}, bf16[8,128,128]{2,1,0:T(8,128)(2,1)}, bf16[8,128,128]{2,1,0:T(8,128)(2,1)}, bf16[8,128,128]{2,1,0:T(8,128)(2,1)}) custom-call(s32[24]{0:T(128)} %pad_add_fusion.1.scal_ref, bf16[8,1152,128]{2,1,0:T(8,128)(2,1)} %copy-done.1, bf16[8,1152,128]{2,1,0:T(8,128)(2,1)} %copy-done.1, ...), custom_call_target="tpu_custom_call" | custom-call | flops 10000000000 | bytes 6000000 | tf_op jit(solution)/shard_map/attention/pallas_call | solution.py:173
  74.4 6.7 %collective-permute-start.2 = (bf16[8,128,128]{2,1,0:T(8,128)(2,1)}, bf16[8,128,128]{2,1,0:T(8,128)(2,1)S(1)}, u32[]{:S(2)}, u32[]{:S(2)}) collective-permute-start(bf16[8,128,128]{2,1,0:T(8,128)(2,1)} %get-tuple-element.10), channel_id=1, source_target_pairs={{1,0},{2,1},{3,2},{4,3},{5,4},{6,5},{7,6},{8,7},{9,8},{10,9},{11,1... | collective-permute-start | bytes 786440 | tf_op jit(solution)/shard_map/ppermute | solution.py:40
  81.1 2.8 %collective-permute-start.3 = (bf16[8,128,128]{2,1,0:T(8,128)(2,1)}, bf16[8,128,128]{2,1,0:T(8,128)(2,1)S(1)}, u32[]{:S(2)}, u32[]{:S(2)}) collective-permute-start(bf16[8,128,128]{2,1,0:T(8,128)(2,1)} %get-tuple-element.11), channel_id=1, source_target_pairs={{2,0},{3,1},{4,2},{5,3},{6,4},{7,5},{8,6},{9,7},{10,8},{11,9},{12,... | collective-permute-start | bytes 786440 | tf_op jit(solution)/shard_map/ppermute | solution.py:40
  83.9 2.7 %collective-permute-done.2 = bf16[8,128,128]{2,1,0:T(8,128)(2,1)S(1)} collective-permute-done((bf16[8,128,128]{2,1,0:T(8,128)(2,1)}, bf16[8,128,128]{2,1,0:T(8,128)(2,1)S(1)}, u32[]{:S(2)}, u32[]{:S(2)}) %collective-permute-start.2) | collective-permute-done | bytes 262176 | tf_op jit(solution)/shard_map/ppermute | solution.py:40
  86.7 12.9 %collective-permute-done.3 = bf16[8,128,128]{2,1,0:T(8,128)(2,1)S(1)} collective-permute-done((bf16[8,128,128]{2,1,0:T(8,128)(2,1)}, bf16[8,128,128]{2,1,0:T(8,128)(2,1)S(1)}, u32[]{:S(2)}, u32[]{:S(2)}) %collective-permute-start.3) | collective-permute-done | bytes 262176 | tf_op jit(solution)/shard_map/ppermute | solution.py:40
  99.6 1.8 %fusion = bf16[8,1152,128]{2,1,0:T(8,128)(2,1)} fusion(bf16[8,1152,128]{2,1,0:T(8,128)(2,1)} %get-tuple-element.8, bf16[8,128,128]{2,1,0:T(8,128)(2,1)S(1)} %collective-permute-done.3, bf16[8,128,128]{2,1,0:T(8,128)(2,1)S(1)} %collective-permute-done.2, bf16[8,128,128]{2,1,0:T(8,128)(2,1)} %get-tuple-element.9), kind=kLoop, calls=%fused_computation.9 | loop fusion | flops 786432 | bytes 1048576 | tf_op jit(solution)/shard_map/dynamic_update_slice | solution.py:240
  101.5 35.3 %all_to_all.10 = bf16[8,1152,128]{2,1,0:T(8,128)(2,1)S(1)} all-to-all(bf16[8,1152,128]{2,1,0:T(8,128)(2,1)} %fusion), channel_id=1, replica_groups=mesh['head'=8,'ctx'=64] {'head'}, dimensions={0} | all-to-all | bytes 4718592 | tf_op jit(solution)/shard_map/all_to_all | solution.py:208
  136.8 0.2 slice_bitcast_fusion
  137.0 1.3 copy.43
  138.2 0.7 copy.36
  139.0 0.7 copy.35
  139.7 1.3 copy.44
  (7 shorter events, 0.1 us)
Async XLA Ops:
  0.6 1.4 copy-start
  5.2 6.2 %copy-start.4 = (s32[48]{0:T(128)S(1)}, s32[48]{0:T(128)}, u32[]{:S(2)}) copy-start(s32[48]{0:T(128)} %param.10) | copy-start | bytes 580
  5.2 6.5 %copy-start.3 = (s32[256]{0:T(256)S(1)}, s32[256]{0:T(256)}, u32[]{:S(2)}) copy-start(s32[256]{0:T(256)} %param.11) | copy-start | bytes 3076
  5.2 35.4 %all-to-all-start = ((bf16[8,1152,128]{2,1,0:T(8,128)(2,1)}), bf16[8,1152,128]{2,1,0:T(8,128)(2,1)S(1)}, u32[]{:S(2)}, u32[]{:S(2)}) async-start(bf16[8,1152,128]{2,1,0:T(8,128)(2,1)} %pad_maximum_fusion), calls=%async_computation | async-start | bytes 4718592 | tf_op jit(solution)/shard_map/all_to_all | solution.py:208
  40.6 13.7 %copy-start.1 = (bf16[8,1152,128]{2,1,0:T(8,128)(2,1)}, bf16[8,1152,128]{2,1,0:T(8,128)(2,1)S(1)}, u32[]{:S(2)}) copy-start(bf16[8,1152,128]{2,1,0:T(8,128)(2,1)S(1)} %all-to-all-done.q_ref.grad_ref) | copy-start | bytes 7077892
  40.7 13.7 %copy-start.2 = (bf16[8,128,128]{2,1,0:T(8,128)(2,1)}, bf16[8,128,128]{2,1,0:T(8,128)(2,1)S(1)}, u32[]{:S(2)}) copy-start(bf16[8,128,128]{2,1,0:T(8,128)(2,1)S(1)} %slice.32.kv0_ref) | copy-start | bytes 786436
  40.7 12.7 %collective-permute-start.1 = (bf16[8,128,128]{2,1,0:T(8,128)(2,1)S(1)}, bf16[8,128,128]{2,1,0:T(8,128)(2,1)S(1)}, u32[]{:S(2)}, u32[]{:S(2)}) collective-permute-start(bf16[8,128,128]{2,1,0:T(8,128)(2,1)S(1)} %slice.32.kv0_ref), channel_id=1, source_target_pairs={{0,2},{1,3},{2,4},{3,5},{4,6},{5,7},{6,8},{7,9},{8,10},{9,11},{10,... | collective-permute-start | bytes 786440 | tf_op jit(solution)/shard_map/ppermute | solution.py:40
  46.6 7.8 %collective-permute-start = (bf16[8,128,128]{2,1,0:T(8,128)(2,1)S(1)}, bf16[8,128,128]{2,1,0:T(8,128)(2,1)}, u32[]{:S(2)}, u32[]{:S(2)}) collective-permute-start(bf16[8,128,128]{2,1,0:T(8,128)(2,1)S(1)} %slice.32.kv0_ref), channel_id=1, source_target_pairs={{0,1},{1,2},{2,3},{3,4},{4,5},{5,6},{6,7},{7,8},{8,9},{9,10},{10,1... | collective-permute-start | bytes 786440 | tf_op jit(solution)/shard_map/ppermute | solution.py:40
  53.3 1.1 copy-start.5
  74.4 12.3 %collective-permute-start.2 = (bf16[8,128,128]{2,1,0:T(8,128)(2,1)}, bf16[8,128,128]{2,1,0:T(8,128)(2,1)S(1)}, u32[]{:S(2)}, u32[]{:S(2)}) collective-permute-start(bf16[8,128,128]{2,1,0:T(8,128)(2,1)} %get-tuple-element.10), channel_id=1, source_target_pairs={{1,0},{2,1},{3,2},{4,3},{5,4},{6,5},{7,6},{8,7},{9,8},{10,9},{11,1... | collective-permute-start | bytes 786440 | tf_op jit(solution)/shard_map/ppermute | solution.py:40
  81.1 18.5 %collective-permute-start.3 = (bf16[8,128,128]{2,1,0:T(8,128)(2,1)}, bf16[8,128,128]{2,1,0:T(8,128)(2,1)S(1)}, u32[]{:S(2)}, u32[]{:S(2)}) collective-permute-start(bf16[8,128,128]{2,1,0:T(8,128)(2,1)} %get-tuple-element.11), channel_id=1, source_target_pairs={{2,0},{3,1},{4,2},{5,3},{6,4},{7,5},{8,6},{9,7},{10,8},{11,9},{12,... | collective-permute-start | bytes 786440 | tf_op jit(solution)/shard_map/ppermute | solution.py:40

commit v7 on v6

--- a/solution.py
+++ b/solution.py
@@ -165,17 +165,15 @@
                     dkv_ref[2 * block + half, pl.ds(64, 64), :] = dv[rows]
 
 
-def attention(scal, rows_in, doc_rows, kv):
-    def row_spec(place):
-        return pl.BlockSpec((2, HALF, HEAD_SIZE), lambda b, s: (b, place, 0))
-
+def attention(scal, q_in, grad_in, doc_rows, kv):
+    row_spec = pl.BlockSpec((2, HALF, HEAD_SIZE), lambda b, s: (b, 0, 0))
     kv_spec = pl.BlockSpec((8, 128, HEAD_SIZE), lambda b, s: (0, 0, 0))
     return pl.pallas_call(
         attention_kernel,
         grid_spec=pltpu.PrefetchScalarGridSpec(
             num_scalar_prefetch=1,
             grid=(CELL_BLOCKS,),
-            in_specs=[row_spec(0), row_spec(1), pl.BlockSpec((1, 1, ROWS), lambda b, s: (b, 0, 0))] + [kv_spec] * 3,
+            in_specs=[row_spec, row_spec, pl.BlockSpec((1, 1, ROWS), lambda b, s: (b, 0, 0))] + [kv_spec] * 3,
             out_specs=[pl.BlockSpec((2, 2 * HALF, HEAD_SIZE), lambda b, s: (b, 0, 0))] + [kv_spec] * 3,
             scratch_shapes=[
                 pltpu.VMEM((PADDED, HEAD_SIZE), jnp.bfloat16),
@@ -191,11 +189,11 @@
                 pltpu.VMEM((CHUNK, ROWS), jnp.bfloat16),
             ],
         ),
-        out_shape=[jax.ShapeDtypeStruct((8, 2 * HALF + 128, HEAD_SIZE), jnp.bfloat16)] + [jax.ShapeDtypeStruct((8, 128, HEAD_SIZE), jnp.bfloat16)] * 3,
+        out_shape=[jax.ShapeDtypeStruct((8, 2 * HALF, HEAD_SIZE), jnp.bfloat16)] + [jax.ShapeDtypeStruct((8, 128, HEAD_SIZE), jnp.bfloat16)] * 3,
         compiler_params=pltpu.CompilerParams(dimension_semantics=("arbitrary",), vmem_limit_bytes=60 * 1024 * 1024),
         cost_estimate=pl.CostEstimate(flops=10_000_000_000, bytes_accessed=6_000_000, transcendentals=4_000_000),
         name="attention",
-    )(scal, rows_in, rows_in, doc_rows, *kv)
+    )(scal, q_in, grad_in, doc_rows, *kv)
 
 
 def by_head(rows):
@@ -231,22 +229,23 @@
 
 def body(queries, keys, values, out_grad, doc_lengths, stored_block_order):
     scal, doc_rows = plan(doc_lengths, stored_block_order)
-    first_in = exchanged(jnp.concatenate([by_head(queries), by_head(out_grad), by_head(keys), by_head(values)], axis=1))
-    kv0 = first_in[:, 2 * HALF :, :]
+    first_in = exchanged(jnp.concatenate([by_head(queries), by_head(keys), by_head(values)], axis=1))
+    kv0 = first_in[:, HALF:, :]
     kv = (kv0, passed_along(kv0, "ctx", 1), passed_along(kv0, "ctx", 2))
-    rows_out, dkv0, dkv1, dkv2 = attention(scal, first_in, doc_rows, kv)
+    grad_in = exchanged(by_head(out_grad))
+    rows_out, dkv0, dkv1, dkv2 = attention(scal, first_in, grad_in, doc_rows, kv)
     near, far = passed_along(dkv1, "ctx", -1), passed_along(dkv2, "ctx", -2)
+    rows_in = exchanged(rows_out)
     summed = dkv0.astype(jnp.float32) + near.astype(jnp.float32) + far.astype(jnp.float32)
-    rows_out = lax.dynamic_update_slice(rows_out, summed.astype(jnp.bfloat16), (0, 2 * HALF, 0))
-    back = exchanged(rows_out)
+    summed, rows_in = lax.optimization_barrier((summed.astype(jnp.bfloat16), rows_in))
+    sums_in = exchanged(summed)
     tokens = queries.shape[0]
 
     def by_token(block, heads):
         return block.reshape(8, tokens, heads, HEAD_SIZE).transpose(1, 0, 2, 3).reshape(tokens, -1, HEAD_SIZE)
 
-    attended, query_grad = by_token(back[:, :HALF], SHARE), by_token(back[:, HALF : 2 * HALF], SHARE)
-    key_gradient = by_token(back[:, 2 * HALF : 2 * HALF + 64], 1)
-    value_gradient = by_token(back[:, 2 * HALF + 64 :], 1)
+    attended, query_grad = by_token(rows_in[:, :HALF], SHARE), by_token(rows_in[:, HALF:], SHARE)
+    key_gradient, value_gradient = by_token(sums_in[:, :64], 1), by_token(sums_in[:, 64:], 1)
     return attended, query_grad, key_gradient, value_gradient
 
 

time: 141 us -> 135 us (0.957)
  the two profiles are of different devices: /device:TPU:226 before, /device:TPU:416 now
where the time goes in v7:
time: 135 us
  waiting for transfers between devices  58.4 us (43%)
  starting transfers between devices  43.9 us (33%)
  Pallas kernels  19.9 us (15%)
  local copies, waits for them, and re-layouts  8.25 us (6%)
  other arithmetic  3.58 us (3%)
    all_to_all x4, waiting for transfers between devices, exchanged(): lax.all_to_all(block, 'head', split_axis=0, concat_axis=0, tiled=True)  31.9 us
    all_to_all x4, starting transfers between devices, exchanged(): lax.all_to_all(block, 'head', split_axis=0, concat_axis=0, tiled=True)  26.6 us
    ppermute x4, waiting for transfers between devices, passed_along(): return lax.ppermute(block, axis, route)  26.5 us
    pallas_call x1, Pallas kernels, attention(): pl.pallas_call(attention_kernel, grid_spec=pltpu.PrefetchScalarGridSpec(n...  19.9 us
    ppermute x4, starting transfers between devices, passed_along(): return lax.ppermute(block, axis, route)  17.3 us
    unnamed x20, local copies, waits for them, and re-layouts  2.73 us
  transfers between devices with their start and end apart: 8, of which 6 were waited for; matrix products, arithmetic and copies ran while one was open for 6% of the time, Pallas kernels for 0%

profile of v7, /device:TPU:416, one launch (start us, length us, event | category | flops | bytes accessed | tf_op | source)
XLA Modules:
  0.0 134.8 jit_solution(1930099885821081922)
XLA Ops:
  0.6 0.0 copy-start
  0.6 0.0 copy-start.5
  0.7 0.0 copy-start.6
  0.7 1.2 copy-done
  1.9 0.2 copy_bitcast_fusion.3
  2.1 0.0 copy-done.5
  2.1 0.0 copy-done.6
  2.1 0.0 copy-start.8
  2.1 0.0 copy-start.7
  2.2 0.0 copy-start.2
  2.2 1.2 pad_maximum_fusion
  3.3 6.9 %all-to-all-start = ((bf16[8,640,128]{2,1,0:T(8,128)(2,1)}), bf16[8,640,128]{2,1,0:T(8,128)(2,1)S(1)}, u32[]{:S(2)}, u32[]{:S(2)}) async-start(bf16[8,640,128]{2,1,0:T(8,128)(2,1)} %pad_maximum_fusion), calls=%async_computation | async-start | bytes 2621440 | tf_op jit(solution)/shard_map/all_to_all | solution.py:206
  10.3 0.1 copy.28
  10.3 0.1 reduce-window.9
  10.4 0.1 reduce.1
  10.6 0.1 fusion.3
  10.7 0.1 broadcast_add_fusion.1
  10.7 0.1 select_add_fusion
  10.8 0.2 select_reduce_fusion
  11.0 1.2 copy_bitcast_fusion.2
  12.2 16.0 %all-to-all-done.q_ref = bf16[8,640,128]{2,1,0:T(8,128)(2,1)S(1)} async-done(((bf16[8,640,128]{2,1,0:T(8,128)(2,1)}), bf16[8,640,128]{2,1,0:T(8,128)(2,1)S(1)}, u32[]{:S(2)}, u32[]{:S(2)}) %all-to-all-start) | async-done | bytes 1310752 | tf_op jit(solution)/shard_map/all_to_all | solution.py:206
  28.3 4.7 %all-to-all-start.1 = ((bf16[8,512,128]{2,1,0:T(8,128)(2,1)}), bf16[8,512,128]{2,1,0:T(8,128)(2,1)S(1)}, u32[]{:S(2)}, u32[]{:S(2)}) async-start(bf16[8,512,128]{2,1,0:T(8,128)(2,1)} %copy_bitcast_fusion.2), calls=%async_computation.1 | async-start | bytes 2097152 | tf_op jit(solution)/shard_map/all_to_all | solution.py:206
  33.0 0.6 sub.51.doc_ref
  33.6 0.1 pad_add_fusion
  33.7 0.2 select_reduce_fusion.1
  33.9 0.7 slice.32.kv0_ref
  34.6 2.5 %collective-permute-start.1 = (bf16[8,128,128]{2,1,0:T(8,128)(2,1)}, bf16[8,128,128]{2,1,0:T(8,128)(2,1)}, u32[]{:S(2)}, u32[]{:S(2)}) collective-permute-start(bf16[8,128,128]{2,1,0:T(8,128)(2,1)} %slice.32.kv0_ref), channel_id=1, source_target_pairs={{0,2},{1,3},{2,4},{3,5},{4,6},{5,7},{6,8},{7,9},{8,10},{9,11},{10,... | collective-permute-start | bytes 786440 | tf_op jit(solution)/shard_map/ppermute | solution.py:40
  37.1 1.9 %collective-permute-start = (bf16[8,128,128]{2,1,0:T(8,128)(2,1)}, bf16[8,128,128]{2,1,0:T(8,128)(2,1)}, u32[]{:S(2)}, u32[]{:S(2)}) collective-permute-start(bf16[8,128,128]{2,1,0:T(8,128)(2,1)} %slice.32.kv0_ref), channel_id=1, source_target_pairs={{0,1},{1,2},{2,3},{3,4},{4,5},{5,6},{6,7},{7,8},{8,9},{9,10},{10,1... | collective-permute-start | bytes 786440 | tf_op jit(solution)/shard_map/ppermute | solution.py:40
  39.0 0.1 and_select_fusion
  39.1 0.6 pad_add_fusion.1.scal_ref
  39.7 9.8 %all-to-all-done.1.grad_ref = bf16[8,512,128]{2,1,0:T(8,128)(2,1)S(1)} async-done(((bf16[8,512,128]{2,1,0:T(8,128)(2,1)}), bf16[8,512,128]{2,1,0:T(8,128)(2,1)S(1)}, u32[]{:S(2)}, u32[]{:S(2)}) %all-to-all-start.1) | async-done | bytes 1048608 | tf_op jit(solution)/shard_map/all_to_all | solution.py:206
  49.5 1.7 %collective-permute-done.1.kv2_ref = bf16[8,128,128]{2,1,0:T(8,128)(2,1)} collective-permute-done((bf16[8,128,128]{2,1,0:T(8,128)(2,1)}, bf16[8,128,128]{2,1,0:T(8,128)(2,1)}, u32[]{:S(2)}, u32[]{:S(2)}) %collective-permute-start.1) | collective-permute-done | bytes 262176 | tf_op jit(solution)/shard_map/ppermute | solution.py:40
  51.2 0.0 collective-permute-done.kv1_ref
  51.2 19.9 %attention.1 = (bf16[8,1024,128]{2,1,0:T(8,128)(2,1)}, bf16[8,128,128]{2,1,0:T(8,128)(2,1)}, bf16[8,128,128]{2,1,0:T(8,128)(2,1)}, bf16[8,128,128]{2,1,0:T(8,128)(2,1)}) custom-call(s32[24]{0:T(128)} %pad_add_fusion.1.scal_ref, bf16[8,640,128]{2,1,0:T(8,128)(2,1)} %copy-done.1, bf16[8,512,128]{2,1,0:T(8,128)(2,1)} %copy-done.3, s32[4,1,1024]{2,1,0:T(1,128)} %sub.51.doc_ref, ...), custom_call_target="tpu_custom_call" | custom-call | flops 10000000000 | bytes 6000000 | tf_op jit(solution)/shard_map/attention/pallas_call | solution.py:171
  71.2 7.4 %all-to-all-start.2 = ((bf16[8,1024,128]{2,1,0:T(8,128)(2,1)}), bf16[8,1024,128]{2,1,0:T(8,128)(2,1)S(1)}, u32[]{:S(2)}, u32[]{:S(2)}) async-start(bf16[8,1024,128]{2,1,0:T(8,128)(2,1)} %get-tuple-element.13), calls=%async_computation.2 | async-start | bytes 4194304 | tf_op jit(solution)/shard_map/all_to_all | solution.py:206
  78.5 10.5 %collective-permute-start.2 = (bf16[8,128,128]{2,1,0:T(8,128)(2,1)}, bf16[8,128,128]{2,1,0:T(8,128)(2,1)S(1)}, u32[]{:S(2)}, u32[]{:S(2)}) collective-permute-start(bf16[8,128,128]{2,1,0:T(8,128)(2,1)} %get-tuple-element.11), channel_id=1, source_target_pairs={{1,0},{2,1},{3,2},{4,3},{5,4},{6,5},{7,6},{8,7},{9,8},{10,9},{11,1... | collective-permute-start | bytes 786440 | tf_op jit(solution)/shard_map/ppermute | solution.py:40
  89.0 2.5 %collective-permute-start.3 = (bf16[8,128,128]{2,1,0:T(8,128)(2,1)}, bf16[8,128,128]{2,1,0:T(8,128)(2,1)S(1)}, u32[]{:S(2)}, u32[]{:S(2)}) collective-permute-start(bf16[8,128,128]{2,1,0:T(8,128)(2,1)} %get-tuple-element.12), channel_id=1, source_target_pairs={{2,0},{3,1},{4,2},{5,3},{6,4},{7,5},{8,6},{9,7},{10,8},{11,9},{12,... | collective-permute-start | bytes 786440 | tf_op jit(solution)/shard_map/ppermute | solution.py:40
  91.5 3.2 %collective-permute-done.2 = bf16[8,128,128]{2,1,0:T(8,128)(2,1)S(1)} collective-permute-done((bf16[8,128,128]{2,1,0:T(8,128)(2,1)}, bf16[8,128,128]{2,1,0:T(8,128)(2,1)S(1)}, u32[]{:S(2)}, u32[]{:S(2)}) %collective-permute-start.2) | collective-permute-done | bytes 262176 | tf_op jit(solution)/shard_map/ppermute | solution.py:40
  94.7 21.5 %collective-permute-done.3 = bf16[8,128,128]{2,1,0:T(8,128)(2,1)S(1)} collective-permute-done((bf16[8,128,128]{2,1,0:T(8,128)(2,1)}, bf16[8,128,128]{2,1,0:T(8,128)(2,1)S(1)}, u32[]{:S(2)}, u32[]{:S(2)}) %collective-permute-start.3) | collective-permute-done | bytes 262176 | tf_op jit(solution)/shard_map/ppermute | solution.py:40
  116.2 0.8 add_convert_fusion
  117.1 0.0 all-to-all-done.2
  117.1 7.5 %all-to-all-start.3 = ((bf16[8,128,128]{2,1,0:T(8,128)(2,1)}), bf16[8,128,128]{2,1,0:T(8,128)(2,1)S(1)}, u32[]{:S(2)}, u32[]{:S(2)}) async-start(bf16[8,128,128]{2,1,0:T(8,128)(2,1)} %add_convert_fusion), calls=%async_computation.3 | async-start | bytes 524288 | tf_op jit(solution)/shard_map/all_to_all | solution.py:206
  124.6 0.1 slice_bitcast_fusion
  124.8 1.3 copy.43
  126.0 1.3 copy.44
  127.3 6.0 %all-to-all-done.3 = bf16[8,128,128]{2,1,0:T(8,128)(2,1)S(1)} async-done(((bf16[8,128,128]{2,1,0:T(8,128)(2,1)}), bf16[8,128,128]{2,1,0:T(8,128)(2,1)S(1)}, u32[]{:S(2)}, u32[]{:S(2)}) %all-to-all-start.3) | async-done | bytes 262176 | tf_op jit(solution)/shard_map/all_to_all | solution.py:206
  133.4 0.7 copy.36
  134.1 0.7 copy.35
  (16 shorter events, 0.1 us)
Async XLA Ops:
  0.6 1.2 copy-start
  0.6 1.4 %copy-start.5 = (bf16[64,8,128]{2,1,0:T(8,128)(2,1)S(1)}, bf16[64,8,128]{2,1,0:T(8,128)(2,1)}, u32[]{:S(2)}) copy-start(bf16[64,8,128]{2,1,0:T(8,128)(2,1)} %param.8) | copy-start | bytes 393220
  0.7 1.4 %copy-start.6 = (bf16[64,8,128]{2,1,0:T(8,128)(2,1)S(1)}, bf16[64,8,128]{2,1,0:T(8,128)(2,1)}, u32[]{:S(2)}) copy-start(bf16[64,8,128]{2,1,0:T(8,128)(2,1)} %param.7) | copy-start | bytes 393220
  2.1 8.1 %copy-start.8 = (s32[48]{0:T(128)S(1)}, s32[48]{0:T(128)}, u32[]{:S(2)}) copy-start(s32[48]{0:T(128)} %param.10) | copy-start | bytes 580
  2.1 8.4 %copy-start.7 = (s32[256]{0:T(256)S(1)}, s32[256]{0:T(256)}, u32[]{:S(2)}) copy-start(s32[256]{0:T(256)} %param.11) | copy-start | bytes 3076
  2.2 8.9 %copy-start.2 = (bf16[64,64,128]{2,1,0:T(8,128)(2,1)S(1)}, bf16[64,64,128]{2,1,0:T(8,128)(2,1)}, u32[]{:S(2)}) copy-start(bf16[64,64,128]{2,1,0:T(8,128)(2,1)} %param.9) | copy-start | bytes 3145732
  3.3 24.9 %all-to-all-start = ((bf16[8,640,128]{2,1,0:T(8,128)(2,1)}), bf16[8,640,128]{2,1,0:T(8,128)(2,1)S(1)}, u32[]{:S(2)}, u32[]{:S(2)}) async-start(bf16[8,640,128]{2,1,0:T(8,128)(2,1)} %pad_maximum_fusion), calls=%async_computation | async-start | bytes 2621440 | tf_op jit(solution)/shard_map/all_to_all | solution.py:206
  28.3 23.0 %copy-start.1 = (bf16[8,640,128]{2,1,0:T(8,128)(2,1)}, bf16[8,640,128]{2,1,0:T(8,128)(2,1)S(1)}, u32[]{:S(2)}) copy-start(bf16[8,640,128]{2,1,0:T(8,128)(2,1)S(1)} %all-to-all-done.q_ref) | copy-start | bytes 3932164
  28.3 21.3 %all-to-all-start.1 = ((bf16[8,512,128]{2,1,0:T(8,128)(2,1)}), bf16[8,512,128]{2,1,0:T(8,128)(2,1)S(1)}, u32[]{:S(2)}, u32[]{:S(2)}) async-start(bf16[8,512,128]{2,1,0:T(8,128)(2,1)} %copy_bitcast_fusion.2), calls=%async_computation.1 | async-start | bytes 2097152 | tf_op jit(solution)/shard_map/all_to_all | solution.py:206
  34.6 16.6 %collective-permute-start.1 = (bf16[8,128,128]{2,1,0:T(8,128)(2,1)}, bf16[8,128,128]{2,1,0:T(8,128)(2,1)}, u32[]{:S(2)}, u32[]{:S(2)}) collective-permute-start(bf16[8,128,128]{2,1,0:T(8,128)(2,1)} %slice.32.kv0_ref), channel_id=1, source_target_pairs={{0,2},{1,3},{2,4},{3,5},{4,6},{5,7},{6,8},{7,9},{8,10},{9,11},{10,... | collective-permute-start | bytes 786440 | tf_op jit(solution)/shard_map/ppermute | solution.py:40
  37.1 14.1 %collective-permute-start = (bf16[8,128,128]{2,1,0:T(8,128)(2,1)}, bf16[8,128,128]{2,1,0:T(8,128)(2,1)}, u32[]{:S(2)}, u32[]{:S(2)}) collective-permute-start(bf16[8,128,128]{2,1,0:T(8,128)(2,1)} %slice.32.kv0_ref), channel_id=1, source_target_pairs={{0,1},{1,2},{2,3},{3,4},{4,5},{5,6},{6,7},{7,8},{8,9},{9,10},{10,1... | collective-permute-start | bytes 786440 | tf_op jit(solution)/shard_map/ppermute | solution.py:40
  49.5 1.7 %copy-start.3 = (bf16[8,512,128]{2,1,0:T(8,128)(2,1)}, bf16[8,512,128]{2,1,0:T(8,128)(2,1)S(1)}, u32[]{:S(2)}) copy-start(bf16[8,512,128]{2,1,0:T(8,128)(2,1)S(1)} %all-to-all-done.1.grad_ref) | copy-start | bytes 3145732
  71.1 45.1 %copy-start.4 = (bf16[8,128,128]{2,1,0:T(8,128)(2,1)S(1)}, bf16[8,128,128]{2,1,0:T(8,128)(2,1)}, u32[]{:S(2)}) copy-start(bf16[8,128,128]{2,1,0:T(8,128)(2,1)} %get-tuple-element.10) | copy-start | bytes 786436
  71.2 45.9 %all-to-all-start.2 = ((bf16[8,1024,128]{2,1,0:T(8,128)(2,1)}), bf16[8,1024,128]{2,1,0:T(8,128)(2,1)S(1)}, u32[]{:S(2)}, u32[]{:S(2)}) async-start(bf16[8,1024,128]{2,1,0:T(8,128)(2,1)} %get-tuple-element.13), calls=%async_computation.2 | async-start | bytes 4194304 | tf_op jit(solution)/shard_map/all_to_all | solution.py:206
  78.5 16.1 %collective-permute-start.2 = (bf16[8,128,128]{2,1,0:T(8,128)(2,1)}, bf16[8,128,128]{2,1,0:T(8,128)(2,1)S(1)}, u32[]{:S(2)}, u32[]{:S(2)}) collective-permute-start(bf16[8,128,128]{2,1,0:T(8,128)(2,1)} %get-tuple-element.11), channel_id=1, source_target_pairs={{1,0},{2,1},{3,2},{4,3},{5,4},{6,5},{7,6},{8,7},{9,8},{10,9},{11,1... | collective-permute-start | bytes 786440 | tf_op jit(solution)/shard_map/ppermute | solution.py:40
  89.0 27.2 %collective-permute-start.3 = (bf16[8,128,128]{2,1,0:T(8,128)(2,1)}, bf16[8,128,128]{2,1,0:T(8,128)(2,1)S(1)}, u32[]{:S(2)}, u32[]{:S(2)}) collective-permute-start(bf16[8,128,128]{2,1,0:T(8,128)(2,1)} %get-tuple-element.12), channel_id=1, source_target_pairs={{2,0},{3,1},{4,2},{5,3},{6,4},{7,5},{8,6},{9,7},{10,8},{11,9},{12,... | collective-permute-start | bytes 786440 | tf_op jit(solution)/shard_map/ppermute | solution.py:40
  117.1 16.3 %all-to-all-start.3 = ((bf16[8,128,128]{2,1,0:T(8,128)(2,1)}), bf16[8,128,128]{2,1,0:T(8,128)(2,1)S(1)}, u32[]{:S(2)}, u32[]{:S(2)}) async-start(bf16[8,128,128]{2,1,0:T(8,128)(2,1)} %add_convert_fusion), calls=%async_computation.3 | async-start | bytes 524288 | tf_op jit(solution)/shard_map/all_to_all | solution.py:206

commit v8 on v7

--- a/solution.py
+++ b/solution.py
@@ -58,7 +58,7 @@
     return (key_pos >= doc_start - key_start) & (key_pos <= query_pos - key_start)
 
 
-def attention_kernel(scal_ref, q_ref, grad_ref, doc_ref, kv0_ref, kv1_ref, kv2_ref, out_ref, dkv0_ref, dkv1_ref, dkv2_ref, key_seq, value_seq, value_t, scores, acc, top, dq_acc, dk_acc, dv_acc, weights_low, grads_low):
+def attention_kernel(scal_ref, q_ref, grad_ref, doc_ref, kv0_ref, kv1_ref, kv2_ref, att_ref, dq_ref, dkv0_ref, dkv1_ref, dkv2_ref, key_seq, value_seq, value_t, scores, acc, top, dq_acc, dk_acc, dv_acc, weights_low, grads_low):
     step = pl.program_id(0)
 
     @pl.when(step == 0)
@@ -130,7 +130,7 @@
     total = jnp.sum(top[...], axis=0, keepdims=True)
     lse = highest + jnp.log2(total)
     out = (acc[...] * (1.0 / total)).T.astype(jnp.bfloat16)
-    out_ref[:, :HALF, :] = out.reshape(2, HALF, HEAD_SIZE)
+    att_ref[...] = out.reshape(2, HALF, HEAD_SIZE)
     delta = jnp.sum((out.astype(jnp.float32) * grad_ref[...].reshape(ROWS, HEAD_SIZE).astype(jnp.float32)).T, axis=0, keepdims=True)
 
     def grad_chunk(turn, _):
@@ -150,7 +150,7 @@
 
     lax.fori_loop(0, chunks, grad_chunk, 0)
     query_grad = (dq_acc[...] * SCALE).astype(jnp.bfloat16)
-    out_ref[:, HALF:, :] = query_grad.reshape(2, HALF, HEAD_SIZE)
+    dq_ref[...] = query_grad.reshape(2, HALF, HEAD_SIZE)
 
     @pl.when(step == CELL_BLOCKS - 1)
     def _():
@@ -174,7 +174,7 @@
             num_scalar_prefetch=1,
             grid=(CELL_BLOCKS,),
             in_specs=[row_spec, row_spec, pl.BlockSpec((1, 1, ROWS), lambda b, s: (b, 0, 0))] + [kv_spec] * 3,
-            out_specs=[pl.BlockSpec((2, 2 * HALF, HEAD_SIZE), lambda b, s: (b, 0, 0))] + [kv_spec] * 3,
+            out_specs=[row_spec, row_spec] + [kv_spec] * 3,
             scratch_shapes=[
                 pltpu.VMEM((PADDED, HEAD_SIZE), jnp.bfloat16),
                 pltpu.VMEM((PADDED, HEAD_SIZE), jnp.bfloat16),
@@ -189,7 +189,7 @@
                 pltpu.VMEM((CHUNK, ROWS), jnp.bfloat16),
             ],
         ),
-        out_shape=[jax.ShapeDtypeStruct((8, 2 * HALF, HEAD_SIZE), jnp.bfloat16)] + [jax.ShapeDtypeStruct((8, 128, HEAD_SIZE), jnp.bfloat16)] * 3,
+        out_shape=[jax.ShapeDtypeStruct((8, rows, HEAD_SIZE), jnp.bfloat16) for rows in (HALF, HALF + 128)] + [jax.ShapeDtypeStruct((8, 128, HEAD_SIZE), jnp.bfloat16)] * 3,
         compiler_params=pltpu.CompilerParams(dimension_semantics=("arbitrary",), vmem_limit_bytes=60 * 1024 * 1024),
         cost_estimate=pl.CostEstimate(flops=10_000_000_000, bytes_accessed=6_000_000, transcendentals=4_000_000),
         name="attention",
@@ -233,19 +233,21 @@
     kv0 = first_in[:, HALF:, :]
     kv = (kv0, passed_along(kv0, "ctx", 1), passed_along(kv0, "ctx", 2))
     grad_in = exchanged(by_head(out_grad))
-    rows_out, dkv0, dkv1, dkv2 = attention(scal, first_in, grad_in, doc_rows, kv)
+    attended_loc, last_loc, dkv0, dkv1, dkv2 = attention(scal, first_in, grad_in, doc_rows, kv)
     near, far = passed_along(dkv1, "ctx", -1), passed_along(dkv2, "ctx", -2)
-    rows_in = exchanged(rows_out)
+    attended_in = exchanged(attended_loc)
     summed = dkv0.astype(jnp.float32) + near.astype(jnp.float32) + far.astype(jnp.float32)
-    summed, rows_in = lax.optimization_barrier((summed.astype(jnp.bfloat16), rows_in))
-    sums_in = exchanged(summed)
+    last_loc = lax.dynamic_update_slice(last_loc, summed.astype(jnp.bfloat16), (0, HALF, 0))
+    last_loc, attended_in = lax.optimization_barrier((last_loc, attended_in))
+    last_in = exchanged(last_loc)
     tokens = queries.shape[0]
 
     def by_token(block, heads):
         return block.reshape(8, tokens, heads, HEAD_SIZE).transpose(1, 0, 2, 3).reshape(tokens, -1, HEAD_SIZE)
 
-    attended, query_grad = by_token(rows_in[:, :HALF], SHARE), by_token(rows_in[:, HALF:], SHARE)
-    key_gradient, value_gradient = by_token(sums_in[:, :64], 1), by_token(sums_in[:, 64:], 1)
+    attended, query_grad = by_token(attended_in, SHARE), by_token(last_in[:, :HALF], SHARE)
+    key_gradient = by_token(last_in[:, HALF : HALF + 64], 1)
+    value_gradient = by_token(last_in[:, HALF + 64 :], 1)
     return attended, query_grad, key_gradient, value_gradient
 
 

time: 135 us -> 135 us (level)
    ppermute x4, waiting for transfers between devices: 26.5 us -> 14.2 us  [passed_along(): return lax.ppermute(block, axis, route)]
    all_to_all x4, waiting for transfers between devices: 31.9 us -> 42.9 us  [exchanged(): lax.all_to_all(block, 'head', split_axis=0, concat_axis=0, tiled=True)]
    transpose x3 -> x0, local copies, waits for them, and re-layouts: 2.68 us -> none  [by_token(): block.reshape(8, tokens, heads, HEAD_SIZE).transpose(1, 0, 2, 3)]
    reshape x1 -> x3, local copies, waits for them, and re-layouts: 0.02 us -> 2.55 us  [by_token(): block.reshape(8, tokens, heads, HEAD_SIZE).transpose(1, 0, 2, 3)]
    all_to_all x4, starting transfers between devices: 26.6 us -> 28.1 us  [exchanged(): lax.all_to_all(block, 'head', split_axis=0, concat_axis=0, tiled=True)]
    unnamed x20 -> x26, local copies, waits for them, and re-layouts: 2.73 us -> 3.43 us
  transfers between devices with their start and end apart: 8 -> 8, of which waited for: 6 -> 6; matrix products, arithmetic and copies ran while one was open for 6% -> 5% of each run, Pallas kernels for 0% -> 0%
where the time goes in v8:
time: 135 us
  waiting for transfers between devices  57.1 us (42%)
  starting transfers between devices  44.9 us (33%)
  Pallas kernels  19.9 us (15%)
  local copies, waits for them, and re-layouts  8.82 us (7%)
  other arithmetic  3.59 us (3%)
    all_to_all x4, waiting for transfers between devices, exchanged(): lax.all_to_all(block, 'head', split_axis=0, concat_axis=0, tiled=True)  42.9 us
    all_to_all x4, starting transfers between devices, exchanged(): lax.all_to_all(block, 'head', split_axis=0, concat_axis=0, tiled=True)  28.1 us
    pallas_call x1, Pallas kernels, attention(): pl.pallas_call(attention_kernel, grid_spec=pltpu.PrefetchScalarGridSpec(n...  19.9 us
    ppermute x4, starting transfers between devices, passed_along(): return lax.ppermute(block, axis, route)  16.8 us
    ppermute x4, waiting for transfers between devices, passed_along(): return lax.ppermute(block, axis, route)  14.2 us
    unnamed x26, local copies, waits for them, and re-layouts  3.43 us
  transfers between devices with their start and end apart: 8, of which 6 were waited for; matrix products, arithmetic and copies ran while one was open for 5% of the time, Pallas kernels for 0%

profile of v8, /device:TPU:416, one launch (start us, length us, event | category | flops | bytes accessed | tf_op | source)
XLA Modules:
  0.0 135.0 jit_solution(5418667448933889316)
XLA Ops:
  0.6 0.0 copy-start
  0.6 0.0 copy-start.5
  0.7 0.0 copy-start.6
  0.7 1.2 copy-done
  1.9 0.2 copy_bitcast_fusion.3
  2.1 0.0 copy-done.5
  2.1 0.0 copy-done.6
  2.1 1.2 pad_maximum_fusion
  3.3 7.1 %all-to-all-start = ((bf16[8,640,128]{2,1,0:T(8,128)(2,1)}), bf16[8,640,128]{2,1,0:T(8,128)(2,1)S(1)}, u32[]{:S(2)}, u32[]{:S(2)}) async-start(bf16[8,640,128]{2,1,0:T(8,128)(2,1)} %pad_maximum_fusion), calls=%async_computation | async-start | bytes 2621440 | tf_op jit(solution)/shard_map/all_to_all | solution.py:206
  10.4 0.0 copy-done.8
  10.4 0.1 copy.28
  10.5 0.1 reduce-window.9
  10.6 0.1 reduce.1
  10.7 0.0 copy-done.7
  10.7 0.1 fusion.4
  10.8 0.1 broadcast_add_fusion.1
  10.9 0.1 select_add_fusion
  10.9 0.2 select_reduce_fusion
  11.2 1.2 copy_bitcast_fusion.2
  12.3 16.0 %all-to-all-done.q_ref = bf16[8,640,128]{2,1,0:T(8,128)(2,1)S(1)} async-done(((bf16[8,640,128]{2,1,0:T(8,128)(2,1)}), bf16[8,640,128]{2,1,0:T(8,128)(2,1)S(1)}, u32[]{:S(2)}, u32[]{:S(2)}) %all-to-all-start) | async-done | bytes 1310752 | tf_op jit(solution)/shard_map/all_to_all | solution.py:206
  28.4 4.7 %all-to-all-start.1 = ((bf16[8,512,128]{2,1,0:T(8,128)(2,1)}), bf16[8,512,128]{2,1,0:T(8,128)(2,1)S(1)}, u32[]{:S(2)}, u32[]{:S(2)}) async-start(bf16[8,512,128]{2,1,0:T(8,128)(2,1)} %copy_bitcast_fusion.2), calls=%async_computation.1 | async-start | bytes 2097152 | tf_op jit(solution)/shard_map/all_to_all | solution.py:206
  33.1 0.6 sub.51.doc_ref
  33.8 0.1 pad_add_fusion
  33.8 0.2 select_reduce_fusion.1
  34.0 0.7 slice.28.kv0_ref
  34.8 2.5 %collective-permute-start.1 = (bf16[8,128,128]{2,1,0:T(8,128)(2,1)}, bf16[8,128,128]{2,1,0:T(8,128)(2,1)}, u32[]{:S(2)}, u32[]{:S(2)}) collective-permute-start(bf16[8,128,128]{2,1,0:T(8,128)(2,1)} %slice.28.kv0_ref), channel_id=1, source_target_pairs={{0,2},{1,3},{2,4},{3,5},{4,6},{5,7},{6,8},{7,9},{8,10},{9,11},{10,... | collective-permute-start | bytes 786440 | tf_op jit(solution)/shard_map/ppermute | solution.py:40
  37.3 1.9 %collective-permute-start = (bf16[8,128,128]{2,1,0:T(8,128)(2,1)}, bf16[8,128,128]{2,1,0:T(8,128)(2,1)S(1)}, u32[]{:S(2)}, u32[]{:S(2)}) collective-permute-start(bf16[8,128,128]{2,1,0:T(8,128)(2,1)} %slice.28.kv0_ref), channel_id=1, source_target_pairs={{0,1},{1,2},{2,3},{3,4},{4,5},{5,6},{6,7},{7,8},{8,9},{9,10},{10,1... | collective-permute-start | bytes 786440 | tf_op jit(solution)/shard_map/ppermute | solution.py:40
  39.2 0.1 and_select_fusion
  39.3 0.6 pad_add_fusion.1.scal_ref
  39.9 9.8 %all-to-all-done.1.grad_ref = bf16[8,512,128]{2,1,0:T(8,128)(2,1)S(1)} async-done(((bf16[8,512,128]{2,1,0:T(8,128)(2,1)}), bf16[8,512,128]{2,1,0:T(8,128)(2,1)S(1)}, u32[]{:S(2)}, u32[]{:S(2)}) %all-to-all-start.1) | async-done | bytes 1048608 | tf_op jit(solution)/shard_map/all_to_all | solution.py:206
  49.7 1.7 %collective-permute-done.1.kv2_ref = bf16[8,128,128]{2,1,0:T(8,128)(2,1)} collective-permute-done((bf16[8,128,128]{2,1,0:T(8,128)(2,1)}, bf16[8,128,128]{2,1,0:T(8,128)(2,1)}, u32[]{:S(2)}, u32[]{:S(2)}) %collective-permute-start.1) | collective-permute-done | bytes 262176 | tf_op jit(solution)/shard_map/ppermute | solution.py:40
  51.4 0.0 collective-permute-done.kv1_ref
  51.4 0.7 copy-done.9
  52.1 19.9 %attention.1 = (bf16[8,512,128]{2,1,0:T(8,128)(2,1)}, bf16[8,640,128]{2,1,0:T(8,128)(2,1)}, bf16[8,128,128]{2,1,0:T(8,128)(2,1)}, bf16[8,128,128]{2,1,0:T(8,128)(2,1)}, bf16[8,128,128]{2,1,0:T(8,128)(2,1)}) custom-call(s32[24]{0:T(128)} %pad_add_fusion.1.scal_ref, bf16[8,640,128]{2,1,0:T(8,128)(2,1)} %copy-done.1, bf16[8,512,128]{2,1,0:T(8,128)(2,1)} %copy-done.3, ...), custom_call_target="tpu_custom_call" | custom-call | flops 10000000000 | bytes 6000000 | tf_op jit(solution)/shard_map/attention/pallas_call | solution.py:171
  72.0 7.4 %all-to-all-start.2 = ((bf16[8,512,128]{2,1,0:T(8,128)(2,1)}), bf16[8,512,128]{2,1,0:T(8,128)(2,1)S(1)}, u32[]{:S(2)}, u32[]{:S(2)}) async-start(bf16[8,512,128]{2,1,0:T(8,128)(2,1)} %get-tuple-element.15), calls=%async_computation.2 | async-start | bytes 2097152 | tf_op jit(solution)/shard_map/all_to_all | solution.py:206
  79.4 0.0 copy-done.11
  79.4 10.5 %collective-permute-start.2 = (bf16[8,128,128]{2,1,0:T(8,128)(2,1)S(1)}, bf16[8,128,128]{2,1,0:T(8,128)(2,1)S(1)}, u32[]{:S(2)}, u32[]{:S(2)}) collective-permute-start(bf16[8,128,128]{2,1,0:T(8,128)(2,1)S(1)} %copy-done.11), channel_id=1, source_target_pairs={{1,0},{2,1},{3,2},{4,3},{5,4},{6,5},{7,6},{8,7},{9,8},{10,9},{11,1... | collective-permute-start | bytes 786440 | tf_op jit(solution)/shard_map/ppermute | solution.py:40
  89.8 1.9 %collective-permute-start.3 = (bf16[8,128,128]{2,1,0:T(8,128)(2,1)S(1)}, bf16[8,128,128]{2,1,0:T(8,128)(2,1)S(1)}, u32[]{:S(2)}, u32[]{:S(2)}) collective-permute-start(bf16[8,128,128]{2,1,0:T(8,128)(2,1)S(1)} %copy-done.10), channel_id=1, source_target_pairs={{2,0},{3,1},{4,2},{5,3},{6,4},{7,5},{8,6},{9,7},{10,8},{11,9},{12,... | collective-permute-start | bytes 786440 | tf_op jit(solution)/shard_map/ppermute | solution.py:40
  91.8 3.4 %collective-permute-done.2 = bf16[8,128,128]{2,1,0:T(8,128)(2,1)S(1)} collective-permute-done((bf16[8,128,128]{2,1,0:T(8,128)(2,1)S(1)}, bf16[8,128,128]{2,1,0:T(8,128)(2,1)S(1)}, u32[]{:S(2)}, u32[]{:S(2)}) %collective-permute-start.2) | collective-permute-done | bytes 262176 | tf_op jit(solution)/shard_map/ppermute | solution.py:40
  95.2 9.1 %collective-permute-done.3 = bf16[8,128,128]{2,1,0:T(8,128)(2,1)S(1)} collective-permute-done((bf16[8,128,128]{2,1,0:T(8,128)(2,1)S(1)}, bf16[8,128,128]{2,1,0:T(8,128)(2,1)S(1)}, u32[]{:S(2)}, u32[]{:S(2)}) %collective-permute-start.3) | collective-permute-done | bytes 262176 | tf_op jit(solution)/shard_map/ppermute | solution.py:40
  104.3 0.8 fusion
  105.1 0.0 all-to-all-done.2
  105.1 8.9 %all-to-all-start.3 = ((bf16[8,640,128]{2,1,0:T(8,128)(2,1)}), bf16[8,640,128]{2,1,0:T(8,128)(2,1)S(1)}, u32[]{:S(2)}, u32[]{:S(2)}) async-start(bf16[8,640,128]{2,1,0:T(8,128)(2,1)} %fusion), calls=%async_computation.3 | async-start | bytes 2621440 | tf_op jit(solution)/shard_map/all_to_all | solution.py:206
  114.0 1.3 copy_bitcast_fusion.1
  115.2 17.0 %all-to-all-done.3 = bf16[8,640,128]{2,1,0:T(8,128)(2,1)S(1)} async-done(((bf16[8,640,128]{2,1,0:T(8,128)(2,1)}), bf16[8,640,128]{2,1,0:T(8,128)(2,1)S(1)}, u32[]{:S(2)}, u32[]{:S(2)}) %all-to-all-start.3) | async-done | bytes 1310752 | tf_op jit(solution)/shard_map/all_to_all | solution.py:206
  132.3 0.7 copy.36
  133.0 0.7 copy.35
  133.7 1.3 copy_bitcast_fusion
  (21 shorter events, 0.1 us)
Async XLA Ops:
  0.6 1.2 copy-start
  0.6 1.4 %copy-start.5 = (bf16[64,8,128]{2,1,0:T(8,128)(2,1)S(1)}, bf16[64,8,128]{2,1,0:T(8,128)(2,1)}, u32[]{:S(2)}) copy-start(bf16[64,8,128]{2,1,0:T(8,128)(2,1)} %param.8) | copy-start | bytes 393220
  0.7 1.4 %copy-start.6 = (bf16[64,8,128]{2,1,0:T(8,128)(2,1)S(1)}, bf16[64,8,128]{2,1,0:T(8,128)(2,1)}, u32[]{:S(2)}) copy-start(bf16[64,8,128]{2,1,0:T(8,128)(2,1)} %param.7) | copy-start | bytes 393220
  3.3 7.1 %copy-start.8 = (s32[48]{0:T(128)S(1)}, s32[48]{0:T(128)}, u32[]{:S(2)}) copy-start(s32[48]{0:T(128)} %param.10) | copy-start | bytes 580
  3.3 7.4 %copy-start.7 = (s32[256]{0:T(256)S(1)}, s32[256]{0:T(256)}, u32[]{:S(2)}) copy-start(s32[256]{0:T(256)} %param.11) | copy-start | bytes 3076
  3.3 7.9 %copy-start.2 = (bf16[64,64,128]{2,1,0:T(8,128)(2,1)S(1)}, bf16[64,64,128]{2,1,0:T(8,128)(2,1)}, u32[]{:S(2)}) copy-start(bf16[64,64,128]{2,1,0:T(8,128)(2,1)} %param.9) | copy-start | bytes 3145732
  3.3 25.1 %all-to-all-start = ((bf16[8,640,128]{2,1,0:T(8,128)(2,1)}), bf16[8,640,128]{2,1,0:T(8,128)(2,1)S(1)}, u32[]{:S(2)}, u32[]{:S(2)}) async-start(bf16[8,640,128]{2,1,0:T(8,128)(2,1)} %pad_maximum_fusion), calls=%async_computation | async-start | bytes 2621440 | tf_op jit(solution)/shard_map/all_to_all | solution.py:206
  28.4 6.4 %copy-start.1 = (bf16[8,640,128]{2,1,0:T(8,128)(2,1)}, bf16[8,640,128]{2,1,0:T(8,128)(2,1)S(1)}, u32[]{:S(2)}) copy-start(bf16[8,640,128]{2,1,0:T(8,128)(2,1)S(1)} %all-to-all-done.q_ref) | copy-start | bytes 3932164
  28.4 21.3 %all-to-all-start.1 = ((bf16[8,512,128]{2,1,0:T(8,128)(2,1)}), bf16[8,512,128]{2,1,0:T(8,128)(2,1)S(1)}, u32[]{:S(2)}, u32[]{:S(2)}) async-start(bf16[8,512,128]{2,1,0:T(8,128)(2,1)} %copy_bitcast_fusion.2), calls=%async_computation.1 | async-start | bytes 2097152 | tf_op jit(solution)/shard_map/all_to_all | solution.py:206
  34.8 16.6 %collective-permute-start.1 = (bf16[8,128,128]{2,1,0:T(8,128)(2,1)}, bf16[8,128,128]{2,1,0:T(8,128)(2,1)}, u32[]{:S(2)}, u32[]{:S(2)}) collective-permute-start(bf16[8,128,128]{2,1,0:T(8,128)(2,1)} %slice.28.kv0_ref), channel_id=1, source_target_pairs={{0,2},{1,3},{2,4},{3,5},{4,6},{5,7},{6,8},{7,9},{8,10},{9,11},{10,... | collective-permute-start | bytes 786440 | tf_op jit(solution)/shard_map/ppermute | solution.py:40
  37.3 14.1 %collective-permute-start = (bf16[8,128,128]{2,1,0:T(8,128)(2,1)}, bf16[8,128,128]{2,1,0:T(8,128)(2,1)S(1)}, u32[]{:S(2)}, u32[]{:S(2)}) collective-permute-start(bf16[8,128,128]{2,1,0:T(8,128)(2,1)} %slice.28.kv0_ref), channel_id=1, source_target_pairs={{0,1},{1,2},{2,3},{3,4},{4,5},{5,6},{6,7},{7,8},{8,9},{9,10},{10,1... | collective-permute-start | bytes 786440 | tf_op jit(solution)/shard_map/ppermute | solution.py:40
  49.7 1.7 %copy-start.3 = (bf16[8,512,128]{2,1,0:T(8,128)(2,1)}, bf16[8,512,128]{2,1,0:T(8,128)(2,1)S(1)}, u32[]{:S(2)}) copy-start(bf16[8,512,128]{2,1,0:T(8,128)(2,1)S(1)} %all-to-all-done.1.grad_ref) | copy-start | bytes 3145732
  51.4 0.7 copy-start.9
  71.9 7.4 %copy-start.11 = (bf16[8,128,128]{2,1,0:T(8,128)(2,1)S(1)}, bf16[8,128,128]{2,1,0:T(8,128)(2,1)}, u32[]{:S(2)}) copy-start(bf16[8,128,128]{2,1,0:T(8,128)(2,1)} %get-tuple-element.13) | copy-start | bytes 786436
  71.9 17.9 %copy-start.10 = (bf16[8,128,128]{2,1,0:T(8,128)(2,1)S(1)}, bf16[8,128,128]{2,1,0:T(8,128)(2,1)}, u32[]{:S(2)}) copy-start(bf16[8,128,128]{2,1,0:T(8,128)(2,1)} %get-tuple-element.14) | copy-start | bytes 786436
  72.0 32.3 %copy-start.4 = (bf16[8,128,128]{2,1,0:T(8,128)(2,1)S(1)}, bf16[8,128,128]{2,1,0:T(8,128)(2,1)}, u32[]{:S(2)}) copy-start(bf16[8,128,128]{2,1,0:T(8,128)(2,1)} %get-tuple-element.12) | copy-start | bytes 786436
  72.0 33.1 %all-to-all-start.2 = ((bf16[8,512,128]{2,1,0:T(8,128)(2,1)}), bf16[8,512,128]{2,1,0:T(8,128)(2,1)S(1)}, u32[]{:S(2)}, u32[]{:S(2)}) async-start(bf16[8,512,128]{2,1,0:T(8,128)(2,1)} %get-tuple-element.15), calls=%async_computation.2 | async-start | bytes 2097152 | tf_op jit(solution)/shard_map/all_to_all | solution.py:206
  79.4 15.8 %collective-permute-start.2 = (bf16[8,128,128]{2,1,0:T(8,128)(2,1)S(1)}, bf16[8,128,128]{2,1,0:T(8,128)(2,1)S(1)}, u32[]{:S(2)}, u32[]{:S(2)}) collective-permute-start(bf16[8,128,128]{2,1,0:T(8,128)(2,1)S(1)} %copy-done.11), channel_id=1, source_target_pairs={{1,0},{2,1},{3,2},{4,3},{5,4},{6,5},{7,6},{8,7},{9,8},{10,9},{11,1... | collective-permute-start | bytes 786440 | tf_op jit(solution)/shard_map/ppermute | solution.py:40
  89.8 14.4 %collective-permute-start.3 = (bf16[8,128,128]{2,1,0:T(8,128)(2,1)S(1)}, bf16[8,128,128]{2,1,0:T(8,128)(2,1)S(1)}, u32[]{:S(2)}, u32[]{:S(2)}) collective-permute-start(bf16[8,128,128]{2,1,0:T(8,128)(2,1)S(1)} %copy-done.10), channel_id=1, source_target_pairs={{2,0},{3,1},{4,2},{5,3},{6,4},{7,5},{8,6},{9,7},{10,8},{11,9},{12,... | collective-permute-start | bytes 786440 | tf_op jit(solution)/shard_map/ppermute | solution.py:40
  105.1 27.1 %all-to-all-start.3 = ((bf16[8,640,128]{2,1,0:T(8,128)(2,1)}), bf16[8,640,128]{2,1,0:T(8,128)(2,1)S(1)}, u32[]{:S(2)}, u32[]{:S(2)}) async-start(bf16[8,640,128]{2,1,0:T(8,128)(2,1)} %fusion), calls=%async_computation.3 | async-start | bytes 2621440 | tf_op jit(solution)/shard_map/all_to_all | solution.py:206

commit v9 on v5

--- a/solution.py
+++ b/solution.py
@@ -51,10 +51,10 @@
     return pl.multiple_of(scal_ref[index] * BLOCK, BLOCK)
 
 
-def allowed_tile(key_start, first_block, doc_start, tile):
+def allowed_tile(key_start, first_block, doc_start, tile, count=CHUNK):
     lane = lax.broadcasted_iota(jnp.int32, (1, TILE), 1) + tile * TILE
     query_pos = first_block * BLOCK + lax.shift_right_logical(lane, 3)
-    key_pos = lax.broadcasted_iota(jnp.int32, (CHUNK, TILE), 0)
+    key_pos = lax.broadcasted_iota(jnp.int32, (count, TILE), 0)
     return (key_pos >= doc_start - key_start) & (key_pos <= query_pos - key_start)
 
 
@@ -98,36 +98,54 @@
     top[...] = jnp.full_like(top, NEG_BIG)
     acc[...] = jnp.zeros_like(acc)
 
-    def score_chunk(turn, key_start, first_block, masked):
-        keys = key_seq[pl.ds(key_start, CHUNK), :]
-        rows = pl.ds(pl.multiple_of(turn * CHUNK, CHUNK), CHUNK)
+    first_block = scal_ref[WINDOW_BLOCKS + step]
+    low_block = scal_ref[WINDOW_BLOCKS + CELL_BLOCKS + step]
+    last_start = scal_ref[WINDOW_BLOCKS + 2 * CELL_BLOCKS + step]
+    chunks = lax.shift_right_logical(first_block - low_block + 2, 1)
+    pairs = lax.shift_right_logical(chunks, 1)
+
+    def score(turn, count, masked):
+        key_start = pl.multiple_of((low_block + 4 * turn) * BLOCK, BLOCK)
+        keys = key_seq[pl.ds(key_start, count), :]
+        rows = pl.ds(pl.multiple_of(turn * 2 * CHUNK, CHUNK), count)
         for tile in range(2):
             cols = slice(tile * TILE, (tile + 1) * TILE)
             raw = dot(keys, q_ref[tile], NT)
             if masked:
-                raw = jnp.where(allowed_tile(key_start, first_block, doc_ref[0, :, cols], tile), raw, NEG_BIG)
+                allowed = allowed_tile(key_start, first_block, doc_ref[0, :, cols], tile, count)
+                raw = jnp.where(allowed, raw, NEG_BIG)
             scores[rows, cols] = raw
-            part = jnp.max(raw.reshape(CHUNK // 8, 8, TILE), axis=0)
+            part = jnp.max(raw.reshape(count // 8, 8, TILE), axis=0)
             top[:, cols] = jnp.maximum(top[:, cols], part)
 
-    each_chunk(scal_ref, step, score_chunk)
+    def score_pair(turn, _):
+        key_start = (low_block + 4 * turn) * BLOCK
+        whole = (key_start >= last_start) & (key_start + 2 * CHUNK <= first_block * BLOCK)
+        pl.when(whole)(lambda: score(turn, 2 * CHUNK, False))
+        pl.when(jnp.logical_not(whole))(lambda: score(turn, 2 * CHUNK, True))
+        return 0
+
+    lax.fori_loop(0, pairs, score_pair, 0)
+    pl.when(chunks > 2 * pairs)(lambda: score(pairs, CHUNK, True))
     highest = jnp.max(top[...], axis=0, keepdims=True) * EXP2_SCALE
     top[...] = jnp.zeros_like(top)
-    first_block = scal_ref[WINDOW_BLOCKS + step]
-    low_block = scal_ref[WINDOW_BLOCKS + CELL_BLOCKS + step]
-
-    def value_chunk(turn, _):
-        key_start = pl.multiple_of((low_block + 2 * turn) * BLOCK, BLOCK)
-        rows = pl.ds(pl.multiple_of(turn * CHUNK, CHUNK), CHUNK)
-        values = value_t[:, pl.ds(key_start, CHUNK)]
+
+    def weigh(turn, count):
+        key_start = pl.multiple_of((low_block + 4 * turn) * BLOCK, BLOCK)
+        rows = pl.ds(pl.multiple_of(turn * 2 * CHUNK, CHUNK), count)
+        values = value_t[:, pl.ds(key_start, count)]
         for tile in range(2):
             cols = slice(tile * TILE, (tile + 1) * TILE)
             weights = jnp.exp2(scores[rows, cols] * EXP2_SCALE - highest[:, cols])
-            top[:, cols] += jnp.sum(weights.reshape(CHUNK // 8, 8, TILE), axis=0)
+            top[:, cols] += jnp.sum(weights.reshape(count // 8, 8, TILE), axis=0)
             acc[:, cols] += dot(values, weights.astype(jnp.bfloat16))
+
+    def weigh_pair(turn, _):
+        weigh(turn, 2 * CHUNK)
         return 0
 
-    lax.fori_loop(0, lax.shift_right_logical(first_block - low_block + 2, 1), value_chunk, 0)
+    lax.fori_loop(0, pairs, weigh_pair, 0)
+    pl.when(chunks > 2 * pairs)(lambda: weigh(pairs, CHUNK))
     total = jnp.sum(top[...], axis=0, keepdims=True)
     lse_ref[0] = highest + jnp.log2(total)
     out_t = acc[...] * (1.0 / total)

time: 130 us -> 132 us (1.015)
  the two profiles are of different devices: /device:TPU:409 before, /device:TPU:103 now
where the time goes in v9:
time: 132 us; the launch traced here: 131 us
  waiting for transfers between devices  54.1 us (41%)
  starting transfers between devices  46.3 us (35%)
  Pallas kernels  17.4 us (13%)
  local copies, waits for them, and re-layouts  8.09 us (6%)
  other arithmetic  4.56 us (3%)
    all_to_all x4, waiting for transfers between devices, exchanged(): lax.all_to_all(block, 'head', split_axis=0, concat_axis=0, tiled=True)  41.9 us
    all_to_all x4, starting transfers between devices, exchanged(): lax.all_to_all(block, 'head', split_axis=0, concat_axis=0, tiled=True)  24.3 us
    ppermute x4, starting transfers between devices, passed_along(): return lax.ppermute(block, axis, route)  22.1 us
    ppermute x4, waiting for transfers between devices, passed_along(): return lax.ppermute(block, axis, route)  12.2 us
    pallas_call x1, Pallas kernels, backward(): pl.pallas_call(backward_kernel, grid_spec=pltpu.PrefetchScalarGridSpec(nu...  10 us
    pallas_call x1, Pallas kernels, forward(): pl.pallas_call(forward_kernel, grid_spec=pltpu.PrefetchScalarGridSpec(num...  7.35 us
    unnamed x22, local copies, waits for them, and re-layouts  3.43 us
  transfers between devices with their start and end apart: 8, of which 6 were waited for; matrix products, arithmetic and copies ran while one was open for 4% of the time, Pallas kernels for 13%

profile of v9, /device:TPU:103, one launch (start us, length us, event | category | flops | bytes accessed | tf_op | source)
XLA Modules:
  0.0 131.3 jit_solution(790233461291719805)
XLA Ops:
  0.6 0.0 copy-start
  0.6 0.0 copy-start.5
  0.7 0.0 copy-start.6
  0.7 1.2 copy-done
  1.9 0.2 copy_bitcast_fusion.3
  2.1 0.0 copy-done.5
  2.1 0.0 copy-done.6
  2.1 1.2 pad_maximum_fusion
  3.3 7.0 %all-to-all-start = ((bf16[8,640,128]{2,1,0:T(8,128)(2,1)}), bf16[8,640,128]{2,1,0:T(8,128)(2,1)S(1)}, u32[]{:S(2)}, u32[]{:S(2)}) async-start(bf16[8,640,128]{2,1,0:T(8,128)(2,1)} %pad_maximum_fusion), calls=%async_computation | async-start | bytes 2621440 | tf_op jit(solution)/shard_map/all_to_all | solution.py:294
  10.3 0.0 copy-done.7
  10.3 0.1 fusion.4
  10.4 0.0 copy-done.8
  10.4 0.1 copy.28
  10.5 0.1 reduce-window.9
  10.6 0.1 reduce.1
  10.7 0.1 broadcast_add_fusion.1
  10.8 0.1 select_add_fusion
  10.9 0.2 select_reduce_fusion
  11.1 0.6 sub.51.doc_ref
  11.7 0.1 pad_add_fusion
  11.8 0.2 select_reduce_fusion.1
  12.0 15.7 %all-to-all-done.q_ref = bf16[8,640,128]{2,1,0:T(8,128)(2,1)S(1)} async-done(((bf16[8,640,128]{2,1,0:T(8,128)(2,1)}), bf16[8,640,128]{2,1,0:T(8,128)(2,1)S(1)}, u32[]{:S(2)}, u32[]{:S(2)}) %all-to-all-start) | async-done | bytes 1310752 | tf_op jit(solution)/shard_map/all_to_all | solution.py:294
  27.8 0.0 copy-start.4
  27.8 5.8 %collective-permute-start = (bf16[8,128,128]{2,1,0:T(8,128)(2,1)S(1)}, bf16[8,128,128]{2,1,0:T(8,128)(2,1)S(1)}, u32[]{:S(2)}, u32[]{:S(2)}) collective-permute-start(bf16[8,128,128]{2,1,0:T(8,128)(2,1)S(1)} %slice.28.kv0_ref), channel_id=1, source_target_pairs={{0,1},{1,2},{2,3},{3,4},{4,5},{5,6},{6,7},{7,8},{8,9},{9,10},{10,1... | collective-permute-start | bytes 786440 | tf_op jit(solution)/shard_map/ppermute | solution.py:40
  33.5 2.8 %collective-permute-start.1 = (bf16[8,128,128]{2,1,0:T(8,128)(2,1)S(1)}, bf16[8,128,128]{2,1,0:T(8,128)(2,1)}, u32[]{:S(2)}, u32[]{:S(2)}) collective-permute-start(bf16[8,128,128]{2,1,0:T(8,128)(2,1)S(1)} %slice.28.kv0_ref), channel_id=1, source_target_pairs={{0,2},{1,3},{2,4},{3,5},{4,6},{5,7},{6,8},{7,9},{8,10},{9,11},{10,... | collective-permute-start | bytes 786440 | tf_op jit(solution)/shard_map/ppermute | solution.py:40
  36.4 1.2 copy_bitcast_fusion.2
  37.6 0.0 collective-permute-done.kv1_ref
  37.6 0.7 copy-done.9
  38.3 4.2 %collective-permute-done.1.kv2_ref = bf16[8,128,128]{2,1,0:T(8,128)(2,1)} collective-permute-done((bf16[8,128,128]{2,1,0:T(8,128)(2,1)S(1)}, bf16[8,128,128]{2,1,0:T(8,128)(2,1)}, u32[]{:S(2)}, u32[]{:S(2)}) %collective-permute-start.1) | collective-permute-done | bytes 262176 | tf_op jit(solution)/shard_map/ppermute | solution.py:40
  42.5 5.2 %all-to-all-start.2 = ((bf16[8,512,128]{2,1,0:T(8,128)(2,1)}), bf16[8,512,128]{2,1,0:T(8,128)(2,1)S(1)}, u32[]{:S(2)}, u32[]{:S(2)}) async-start(bf16[8,512,128]{2,1,0:T(8,128)(2,1)} %copy_bitcast_fusion.2), calls=%async_computation.2 | async-start | bytes 2097152 | tf_op jit(solution)/shard_map/all_to_all | solution.py:294
  47.6 0.1 and_select_fusion
  47.7 0.6 pad_add_fusion.1.scal_ref
  48.3 7.3 %forward.1 = (bf16[8,512,128]{2,1,0:T(8,128)(2,1)}, bf16[4,128,1024]{2,1,0:T(8,128)(2,1)}, f32[4,1,1024]{2,1,0:T(1,128)}) custom-call(s32[24]{0:T(128)} %pad_add_fusion.1.scal_ref, bf16[8,640,128]{2,1,0:T(8,128)(2,1)} %copy-done.1, s32[4,1,1024]{2,1,0:T(1,128)} %sub.51.doc_ref, bf16[8,128,128]{2,1,0:T(8,128)(2,1)} %copy-done.4, ...), custom_call_target="tpu_custom_call" | custom-call | flops 4000000000 | bytes 4000000 | tf_op jit(solution)/shard_map/forward/pallas_call | solution.py:234
  55.7 6.7 %all-to-all-done.2.grad_ref = bf16[8,512,128]{2,1,0:T(8,128)(2,1)S(1)} async-done(((bf16[8,512,128]{2,1,0:T(8,128)(2,1)}), bf16[8,512,128]{2,1,0:T(8,128)(2,1)S(1)}, u32[]{:S(2)}, u32[]{:S(2)}) %all-to-all-start.2) | async-done | bytes 1048608 | tf_op jit(solution)/shard_map/all_to_all | solution.py:294
  62.3 5.4 %all-to-all-start.1 = ((bf16[8,512,128]{2,1,0:T(8,128)(2,1)}), bf16[8,512,128]{2,1,0:T(8,128)(2,1)S(1)}, u32[]{:S(2)}, u32[]{:S(2)}) async-start(bf16[8,512,128]{2,1,0:T(8,128)(2,1)} %get-tuple-element.21), calls=%async_computation.1 | async-start | bytes 2097152 | tf_op jit(solution)/shard_map/all_to_all | solution.py:294
  67.8 10.0 %backward.1 = (bf16[8,640,128]{2,1,0:T(8,128)(2,1)}, bf16[8,128,128]{2,1,0:T(8,128)(2,1)}, bf16[8,128,128]{2,1,0:T(8,128)(2,1)}, bf16[8,128,128]{2,1,0:T(8,128)(2,1)}) custom-call(s32[24]{0:T(128)} %pad_add_fusion.1.scal_ref, bf16[8,640,128]{2,1,0:T(8,128)(2,1)} %copy-done.1, bf16[8,512,128]{2,1,0:T(8,128)(2,1)} %copy-done.3, ...), custom_call_target="tpu_custom_call" | custom-call | flops 10000000000 | bytes 6000000 | tf_op jit(solution)/shard_map/backward/pallas_call | solution.py:262
  77.8 4.5 %all-to-all-done.1 = bf16[8,512,128]{2,1,0:T(8,128)(2,1)S(1)} async-done(((bf16[8,512,128]{2,1,0:T(8,128)(2,1)}), bf16[8,512,128]{2,1,0:T(8,128)(2,1)S(1)}, u32[]{:S(2)}, u32[]{:S(2)}) %all-to-all-start.1) | async-done | bytes 1048608 | tf_op jit(solution)/shard_map/all_to_all | solution.py:294
  82.4 2.2 %collective-permute-start.3 = (bf16[8,128,128]{2,1,0:T(8,128)(2,1)}, bf16[8,128,128]{2,1,0:T(8,128)(2,1)S(1)}, u32[]{:S(2)}, u32[]{:S(2)}) collective-permute-start(bf16[8,128,128]{2,1,0:T(8,128)(2,1)} %get-tuple-element.31), channel_id=1, source_target_pairs={{2,0},{3,1},{4,2},{5,3},{6,4},{7,5},{8,6},{9,7},{10,8},{11,9},{12,... | collective-permute-start | bytes 786440 | tf_op jit(solution)/shard_map/ppermute | solution.py:40
  84.6 11.2 %collective-permute-start.2 = (bf16[8,128,128]{2,1,0:T(8,128)(2,1)}, bf16[8,128,128]{2,1,0:T(8,128)(2,1)S(1)}, u32[]{:S(2)}, u32[]{:S(2)}) collective-permute-start(bf16[8,128,128]{2,1,0:T(8,128)(2,1)} %get-tuple-element.30), channel_id=1, source_target_pairs={{1,0},{2,1},{3,2},{4,3},{5,4},{6,5},{7,6},{8,7},{9,8},{10,9},{11,1... | collective-permute-start | bytes 786440 | tf_op jit(solution)/shard_map/ppermute | solution.py:40
  95.9 0.0 collective-permute-done.3
  95.9 8.0 %collective-permute-done.2 = bf16[8,128,128]{2,1,0:T(8,128)(2,1)S(1)} collective-permute-done((bf16[8,128,128]{2,1,0:T(8,128)(2,1)}, bf16[8,128,128]{2,1,0:T(8,128)(2,1)S(1)}, u32[]{:S(2)}, u32[]{:S(2)}) %collective-permute-start.2) | collective-permute-done | bytes 262176 | tf_op jit(solution)/shard_map/ppermute | solution.py:40
  103.9 1.8 %fusion = bf16[8,640,128]{2,1,0:T(8,128)(2,1)} fusion(bf16[8,640,128]{2,1,0:T(8,128)(2,1)} %get-tuple-element.28, bf16[8,128,128]{2,1,0:T(8,128)(2,1)S(1)} %collective-permute-done.3, bf16[8,128,128]{2,1,0:T(8,128)(2,1)S(1)} %collective-permute-done.2, bf16[8,128,128]{2,1,0:T(8,128)(2,1)} %get-tuple-element.29), kind=kLoop, calls=%fused_computation.8 | loop fusion | flops 786432 | bytes 1048576 | tf_op jit(solution)/shard_map/dynamic_update_slice | solution.py:331
  105.6 6.6 %all-to-all-start.3 = ((bf16[8,640,128]{2,1,0:T(8,128)(2,1)}), bf16[8,640,128]{2,1,0:T(8,128)(2,1)S(1)}, u32[]{:S(2)}, u32[]{:S(2)}) async-start(bf16[8,640,128]{2,1,0:T(8,128)(2,1)} %fusion), calls=%async_computation.3 | async-start | bytes 2621440 | tf_op jit(solution)/shard_map/all_to_all | solution.py:294
  112.3 1.3 copy_bitcast_fusion.1
  113.6 15.0 %all-to-all-done.3 = bf16[8,640,128]{2,1,0:T(8,128)(2,1)S(1)} async-done(((bf16[8,640,128]{2,1,0:T(8,128)(2,1)}), bf16[8,640,128]{2,1,0:T(8,128)(2,1)S(1)}, u32[]{:S(2)}, u32[]{:S(2)}) %all-to-all-start.3) | async-done | bytes 1310752 | tf_op jit(solution)/shard_map/all_to_all | solution.py:294
  128.5 0.7 copy.35
  129.3 0.7 copy.36
  130.0 1.3 copy_bitcast_fusion
  (18 shorter events, 0.1 us)
Async XLA Ops:
  0.6 1.2 copy-start
  0.6 1.4 %copy-start.5 = (bf16[64,8,128]{2,1,0:T(8,128)(2,1)S(1)}, bf16[64,8,128]{2,1,0:T(8,128)(2,1)}, u32[]{:S(2)}) copy-start(bf16[64,8,128]{2,1,0:T(8,128)(2,1)} %param.8) | copy-start | bytes 393220
  0.7 1.4 %copy-start.6 = (bf16[64,8,128]{2,1,0:T(8,128)(2,1)S(1)}, bf16[64,8,128]{2,1,0:T(8,128)(2,1)}, u32[]{:S(2)}) copy-start(bf16[64,8,128]{2,1,0:T(8,128)(2,1)} %param.7) | copy-start | bytes 393220
  3.3 7.0 %copy-start.7 = (s32[256]{0:T(256)S(1)}, s32[256]{0:T(256)}, u32[]{:S(2)}) copy-start(s32[256]{0:T(256)} %param.11) | copy-start | bytes 3076
  3.3 7.1 %copy-start.8 = (s32[48]{0:T(128)S(1)}, s32[48]{0:T(128)}, u32[]{:S(2)}) copy-start(s32[48]{0:T(128)} %param.10) | copy-start | bytes 580
  3.3 33.1 %copy-start.2 = (bf16[64,64,128]{2,1,0:T(8,128)(2,1)S(1)}, bf16[64,64,128]{2,1,0:T(8,128)(2,1)}, u32[]{:S(2)}) copy-start(bf16[64,64,128]{2,1,0:T(8,128)(2,1)} %param.9) | copy-start | bytes 3145732
  3.3 24.4 %all-to-all-start = ((bf16[8,640,128]{2,1,0:T(8,128)(2,1)}), bf16[8,640,128]{2,1,0:T(8,128)(2,1)S(1)}, u32[]{:S(2)}, u32[]{:S(2)}) async-start(bf16[8,640,128]{2,1,0:T(8,128)(2,1)} %pad_maximum_fusion), calls=%async_computation | async-start | bytes 2621440 | tf_op jit(solution)/shard_map/all_to_all | solution.py:294
  27.7 14.7 %copy-start.1 = (bf16[8,640,128]{2,1,0:T(8,128)(2,1)}, bf16[8,640,128]{2,1,0:T(8,128)(2,1)S(1)}, u32[]{:S(2)}) copy-start(bf16[8,640,128]{2,1,0:T(8,128)(2,1)S(1)} %all-to-all-done.q_ref) | copy-start | bytes 3932164
  27.8 9.8 %copy-start.4 = (bf16[8,128,128]{2,1,0:T(8,128)(2,1)}, bf16[8,128,128]{2,1,0:T(8,128)(2,1)S(1)}, u32[]{:S(2)}) copy-start(bf16[8,128,128]{2,1,0:T(8,128)(2,1)S(1)} %slice.28.kv0_ref) | copy-start | bytes 786436
  27.8 9.8 %collective-permute-start = (bf16[8,128,128]{2,1,0:T(8,128)(2,1)S(1)}, bf16[8,128,128]{2,1,0:T(8,128)(2,1)S(1)}, u32[]{:S(2)}, u32[]{:S(2)}) collective-permute-start(bf16[8,128,128]{2,1,0:T(8,128)(2,1)S(1)} %slice.28.kv0_ref), channel_id=1, source_target_pairs={{0,1},{1,2},{2,3},{3,4},{4,5},{5,6},{6,7},{7,8},{8,9},{9,10},{10,1... | collective-permute-start | bytes 786440 | tf_op jit(solution)/shard_map/ppermute | solution.py:40
  33.5 8.9 %collective-permute-start.1 = (bf16[8,128,128]{2,1,0:T(8,128)(2,1)S(1)}, bf16[8,128,128]{2,1,0:T(8,128)(2,1)}, u32[]{:S(2)}, u32[]{:S(2)}) collective-permute-start(bf16[8,128,128]{2,1,0:T(8,128)(2,1)S(1)} %slice.28.kv0_ref), channel_id=1, source_target_pairs={{0,2},{1,3},{2,4},{3,5},{4,6},{5,7},{6,8},{7,9},{8,10},{9,11},{10,... | collective-permute-start | bytes 786440 | tf_op jit(solution)/shard_map/ppermute | solution.py:40
  37.6 0.7 copy-start.9
  42.5 19.9 %all-to-all-start.2 = ((bf16[8,512,128]{2,1,0:T(8,128)(2,1)}), bf16[8,512,128]{2,1,0:T(8,128)(2,1)S(1)}, u32[]{:S(2)}, u32[]{:S(2)}) async-start(bf16[8,512,128]{2,1,0:T(8,128)(2,1)} %copy_bitcast_fusion.2), calls=%async_computation.2 | async-start | bytes 2097152 | tf_op jit(solution)/shard_map/all_to_all | solution.py:294
  62.3 5.4 %copy-start.3 = (bf16[8,512,128]{2,1,0:T(8,128)(2,1)}, bf16[8,512,128]{2,1,0:T(8,128)(2,1)S(1)}, u32[]{:S(2)}) copy-start(bf16[8,512,128]{2,1,0:T(8,128)(2,1)S(1)} %all-to-all-done.2.grad_ref) | copy-start | bytes 3145732
  62.3 20.0 %all-to-all-start.1 = ((bf16[8,512,128]{2,1,0:T(8,128)(2,1)}), bf16[8,512,128]{2,1,0:T(8,128)(2,1)S(1)}, u32[]{:S(2)}, u32[]{:S(2)}) async-start(bf16[8,512,128]{2,1,0:T(8,128)(2,1)} %get-tuple-element.21), calls=%async_computation.1 | async-start | bytes 2097152 | tf_op jit(solution)/shard_map/all_to_all | solution.py:294
  82.4 13.5 %collective-permute-start.3 = (bf16[8,128,128]{2,1,0:T(8,128)(2,1)}, bf16[8,128,128]{2,1,0:T(8,128)(2,1)S(1)}, u32[]{:S(2)}, u32[]{:S(2)}) collective-permute-start(bf16[8,128,128]{2,1,0:T(8,128)(2,1)} %get-tuple-element.31), channel_id=1, source_target_pairs={{2,0},{3,1},{4,2},{5,3},{6,4},{7,5},{8,6},{9,7},{10,8},{11,9},{12,... | collective-permute-start | bytes 786440 | tf_op jit(solution)/shard_map/ppermute | solution.py:40
  84.6 19.3 %collective-permute-start.2 = (bf16[8,128,128]{2,1,0:T(8,128)(2,1)}, bf16[8,128,128]{2,1,0:T(8,128)(2,1)S(1)}, u32[]{:S(2)}, u32[]{:S(2)}) collective-permute-start(bf16[8,128,128]{2,1,0:T(8,128)(2,1)} %get-tuple-element.30), channel_id=1, source_target_pairs={{1,0},{2,1},{3,2},{4,3},{5,4},{6,5},{7,6},{8,7},{9,8},{10,9},{11,1... | collective-permute-start | bytes 786440 | tf_op jit(solution)/shard_map/ppermute | solution.py:40
  105.6 22.9 %all-to-all-start.3 = ((bf16[8,640,128]{2,1,0:T(8,128)(2,1)}), bf16[8,640,128]{2,1,0:T(8,128)(2,1)S(1)}, u32[]{:S(2)}, u32[]{:S(2)}) async-start(bf16[8,640,128]{2,1,0:T(8,128)(2,1)} %fusion), calls=%async_computation.3 | async-start | bytes 2621440 | tf_op jit(solution)/shard_map/all_to_all | solution.py:294
